TPU v7x, 32 devices: a whole 2x2x4 slice. The times are simulated.
32 devices in a mesh: dp: 8 (over z, core), tensor: 4 (over y, x).
Axes of the slice: x: 2, y: 2, z: 4, core: 2. Of those that a mesh axis runs over, the one named last changes fastest.
Arguments:
- tokens: bfloat16 [8192, 1024], P(('dp', 'tensor'))
- segments: int32 [8192], P('dp'), may hold values from 0 to 2, as said below
- cotangent: bfloat16 [8192, 1024], P(('dp', 'tensor')), may hold values from -6 to 6
- query_weight: bfloat16 [1024, 1024], P('dp', 'tensor'), may hold values from -0.1875 to 0.1875
- key_weight: bfloat16 [1024, 512], P('dp', 'tensor'), may hold values from -0.1875 to 0.1875
- value_weight: bfloat16 [1024, 512], P('dp', 'tensor'), may hold values from -0.1875 to 0.1875
- out_weight: bfloat16 [1024, 1024], P('tensor', 'dp'), may hold values from -1.5 to 1.5
- gate_weight: bfloat16 [1024, 4608], P('dp', 'tensor'), may hold values from -0.1875 to 0.1875
- up_weight: bfloat16 [1024, 4608], P('dp', 'tensor'), may hold values from -0.1875 to 0.1875
- down_weight: bfloat16 [4608, 1024], P('tensor', 'dp'), may hold values from -0.1875 to 0.1875
- attention_gain: float32 [1024], replicated, may hold values from 0.1 to 1.9
- feedfwd_gain: float32 [1024], replicated, may hold values from 0.1 to 1.9
- query_gain: float32 [64], replicated, may hold values from 0.1 to 1.9
- key_gain: float32 [64], replicated, may hold values from 0.1 to 1.9
Outputs:
- block_out: bfloat16 [8192, 1024], P(('dp', 'tensor'))
- grad_tokens: bfloat16 [8192, 1024], P(('dp', 'tensor'))
- grad_query: float32 [1024, 1024], P('dp', 'tensor')
- grad_key: float32 [1024, 512], P('dp', 'tensor')
- grad_value: float32 [1024, 512], P('dp', 'tensor')
- grad_output: float32 [1024, 1024], P('tensor', 'dp')
- grad_gate: float32 [1024, 4608], P('dp', 'tensor')
- grad_up: float32 [1024, 4608], P('dp', 'tensor')
- grad_down: float32 [4608, 1024], P('tensor', 'dp')
- grad_attention: float32 [1024], replicated
- grad_feedfwd: float32 [1024], replicated
- grad_querynorm: float32 [64], replicated
- grad_keynorm: float32 [64], replicated
Inputs may be any that keep to these rules, and one draw needn't show every extreme that they name: `segments`: each sequence of 1024 consecutive tokens holds exactly three documents, numbered 0, 1, 2 in order, each of 204 tokens or more.
All inputs are finite; a program needn't handle non-finite values.
Results may differ from a plain program's by a relative error of at most 0.023.
Values may be sent and summed in bfloat16 or wider, within the bound.
No kernel may reach another device: no remote copies, remote signals or barrier semaphores. Data moves between devices by JAX's collectives and lax.ppermute only.
A program may use at most 128 MiB of HBM per device.

v0:
```python
from functools import partial
import math

import jax
import jax.numpy as jnp
from jax import lax
from jax.experimental import pallas as pl
from jax.experimental.pallas import tpu as pltpu
from jax.sharding import PartitionSpec as P

LEN = 1024


EPSILON = 1e-05
THETA = 1000000.0
MASKED = -1e30
DOCUMENTS = 3
SHORTEST = 204
TILE = 256
LOG2E = math.log2(math.e)
VMEM_LIMIT = 56 * 2**20
HEAVY, LIGHT = 16 * 10**9, 10**9
BFLOAT, SINGLE = jnp.bfloat16, jnp.float32


def call_kernel(kernel, name, weight, shapes, scalars, arrays, scratch=(), earlier=(), **grid):
    whole = pl.BlockSpec(memory_space=pltpu.VMEM)
    specs = [pl.BlockSpec(memory_space=pltpu.SMEM)] * len(scalars) + [whole] * len(arrays)
    return pl.pallas_call(
        kernel,
        out_shape=[jax.ShapeDtypeStruct(*shape) for shape in shapes],
        in_specs=specs + [pl.BlockSpec(memory_space=pl.ANY)] * len(earlier),
        out_specs=[whole] * len(shapes),
        scratch_shapes=[pltpu.VMEM(*shape) for shape in scratch],
        compiler_params=pltpu.CompilerParams(vmem_limit_bytes=VMEM_LIMIT),
        cost_estimate=pl.CostEstimate(flops=weight, bytes_accessed=2**20, transcendentals=0),
        name=name,
    )(*scalars, *arrays, *earlier)


def dot(left, right):
    return jnp.dot(left, right, preferred_element_type=SINGLE)


def dot_last(left, right):
    return lax.dot_general(left, right, (((1,), (1,)), ((), ())), preferred_element_type=SINGLE)


def key_span(start):
    reach = LEN - (DOCUMENTS - 1) * SHORTEST - 1
    return max(0, (start - reach) // 128 * 128), start + TILE


def mask_bias(begin_ref, start, low, high):
    shape = (high - low, TILE)
    key_pos = low + lax.broadcasted_iota(jnp.int32, shape, 0)
    query_pos = start + lax.broadcasted_iota(jnp.int32, shape, 1)
    counts = (key_pos >= begin_ref[:, start : start + TILE]) & (key_pos <= query_pos)
    return jnp.where(counts, 0.0, MASKED)


def head_ratio(values):
    return lax.rsqrt(jnp.mean(values * values, axis=0, keepdims=True) + EPSILON)


def turn(values, cosine, sine):
    half_dim = values.shape[0] // 2
    first, second = values[:half_dim], values[half_dim:]
    return jnp.concatenate([first * cosine - second * sine, second * cosine + first * sine], axis=0)


def gain_columns(gain_ref, head_dim):
    turned = jnp.broadcast_to(gain_ref[...], (8, gain_ref.shape[1])).T
    return turned[:head_dim, :1], turned[head_dim : 2 * head_dim, :1]


def spread(place_ref, natural, out_ref):
    rows = LEN // place_ref.shape[0]
    for block in range(place_ref.shape[0]):
        start = pl.multiple_of(place_ref[block], rows)
        out_ref[pl.ds(start, rows), :] = natural[block * rows : (block + 1) * rows, :]


def collect(place_ref, value_ref, natural):
    rows = LEN // place_ref.shape[0]
    for block in range(place_ref.shape[0]):
        start = pl.multiple_of(place_ref[block], rows)
        natural[block * rows : (block + 1) * rows, :] = value_ref[pl.ds(start, rows), :]


def attend_kernel(
    sizes,
    place_ref,
    rows_a_ref,
    rows_b_ref,
    rows_c_ref,
    rows_d_ref,
    weight_ref,
    gain_ref,
    segment_ref,
    raw_ref,
    query_ref,
    key_ref,
    query_row_ref,
    key_row_ref,
    value_row_ref,
    total_ref,
    attended_ref,
    cosine_ref,
    sine_ref,
    begin_ref,
    context_ref,
    part_a_ref,
    part_b_ref,
    part_c_ref,
    part_d_ref,
    mixed,
    natural,
    extended,
    bias,
    context,
):
    query_heads, key_heads, head_dim = sizes
    group_size = query_heads // key_heads
    heads = query_heads + key_heads
    columns = natural.shape[1]
    quarter = rows_a_ref.shape[0]
    weight = weight_ref[:, :columns]
    for q, rows_ref in enumerate((rows_a_ref, rows_b_ref, rows_c_ref, rows_d_ref)):
        mixed[q * quarter : (q + 1) * quarter, :] = dot(rows_ref[...], weight)
    collect(place_ref, mixed, natural)
    for start in range(0, LEN, 128):
        raw_ref[:, start : start + 128] = natural[start : start + 128, :].T

    segment = segment_ref[...]
    first_count = jnp.sum((segment == 0).astype(SINGLE), axis=1, keepdims=True)
    second_count = jnp.sum((segment == 1).astype(SINGLE), axis=1, keepdims=True)
    begin = jnp.where(
        segment == 0, 0.0, jnp.where(segment == 1, first_count, first_count + second_count)
    )
    begin_ref[...] = begin.astype(jnp.int32)
    half_dim = head_dim // 2
    shape = (half_dim, LEN)
    steps = lax.broadcasted_iota(jnp.int32, shape, 0).astype(SINGLE)
    order = lax.broadcasted_iota(jnp.int32, shape, 1).astype(SINGLE)
    angles = (order - begin) * jnp.exp(steps * (-math.log(THETA) / half_dim))
    cosine, sine = jnp.cos(angles), jnp.sin(angles)
    cosine_ref[...] = cosine
    sine_ref[...] = sine

    gains = gain_columns(gain_ref, head_dim)
    for head in range(heads):
        values = raw_ref[head * head_dim : (head + 1) * head_dim, :]
        gain = gains[0] if head < query_heads else gains[1]
        turned = turn(values * head_ratio(values) * gain, cosine, sine)
        if head < query_heads:
            query_ref[head] = turned.astype(BFLOAT)
            query_row_ref[head] = turned.T.astype(BFLOAT)
        else:
            key_ref[head - query_heads] = turned.astype(BFLOAT)
            key_row_ref[head - query_heads] = turned.T.astype(BFLOAT)
    for head in range(key_heads):
        first = (heads + head) * head_dim
        extended[head, :head_dim, :] = raw_ref[first : first + head_dim, :].astype(BFLOAT)
        extended[head, head_dim:, :] = jnp.ones((extended.shape[1] - head_dim, LEN), BFLOAT)
        value_row_ref[head] = natural[:, first : first + head_dim].astype(BFLOAT)
    factor = LOG2E * head_dim ** (-0.5)
    for start in range(0, LEN, TILE):
        low, high = key_span(start)
        span, tile = slice(low, high), slice(start, start + TILE)
        bias[: high - low, :] = mask_bias(begin_ref, start, low, high)

        def one_head(head, carry):
            key_head = head // group_size
            scores = dot(key_row_ref[key_head, span, :], query_ref[head, :, tile])
            powers = jnp.exp2(scores * factor + bias[: high - low, :])
            summed = dot(extended[key_head, :, span], powers.astype(BFLOAT))
            total = summed[head_dim : head_dim + 1, :]
            total_ref[head, :, tile] = jnp.log2(total)
            attended_ref[head, :, tile] = summed[:head_dim, :] / total
            return carry

        lax.fori_loop(0, query_heads, one_head, 0)
    for head in range(query_heads):
        context[:, head * head_dim : (head + 1) * head_dim] = attended_ref[head].T.astype(BFLOAT)
    spread(place_ref, context, context_ref)
    out_weight = weight_ref[:, columns:]
    for q, part_ref in enumerate((part_a_ref, part_b_ref, part_c_ref, part_d_ref)):
        rows = context_ref[q * quarter : (q + 1) * quarter, :]
        part_ref[...] = dot_last(rows, out_weight).astype(BFLOAT)


def attend(sizes, place, quarters, weight, gains, segments):
    query_heads, key_heads, head_dim = sizes
    columns = (query_heads + 2 * key_heads) * head_dim
    quarter, width = quarters[0].shape
    shapes = [
        ((columns, LEN), SINGLE),
        ((query_heads, head_dim, LEN), BFLOAT),
        ((key_heads, head_dim, LEN), BFLOAT),
        ((query_heads, LEN, head_dim), BFLOAT),
        ((key_heads, LEN, head_dim), BFLOAT),
        ((key_heads, LEN, head_dim), BFLOAT),
        ((query_heads, 1, LEN), SINGLE),
        ((query_heads, head_dim, LEN), SINGLE),
        ((head_dim // 2, LEN), SINGLE),
        ((head_dim // 2, LEN), SINGLE),
        ((1, LEN), jnp.int32),
        ((LEN, query_heads * head_dim), BFLOAT),
    ] + [((quarter, width), BFLOAT)] * 4
    scratch = [
        ((LEN, columns), SINGLE),
        ((LEN, columns), SINGLE),
        ((key_heads, head_dim + 16, LEN), BFLOAT),
        ((LEN, TILE), SINGLE),
        ((LEN, query_heads * head_dim), BFLOAT),
    ]
    arrays = (*quarters, weight, gains, segments)
    outs = call_kernel(
        partial(attend_kernel, sizes), "attend", HEAVY, shapes, (place,), arrays, scratch
    )
    return outs[:11], outs[11], outs[12:]


def attend_back_kernel(
    sizes,
    place_ref,
    grad_a_ref,
    grad_b_ref,
    grad_c_ref,
    grad_d_ref,
    rows_a_ref,
    rows_b_ref,
    rows_c_ref,
    rows_d_ref,
    weight_ref,
    gain_ref,
    raw_ref,
    query_ref,
    key_ref,
    query_row_ref,
    key_row_ref,
    value_row_ref,
    total_ref,
    attended_ref,
    cosine_ref,
    sine_ref,
    begin_ref,
    out_ref,
    head_gain_ref,
    row_gain_ref,
    part_a_ref,
    part_b_ref,
    part_c_ref,
    part_d_ref,
    mixed,
    context,
    grad_row,
    grad_col,
    query_grad,
    key_grad,
    value_grad,
    joined,
    natural,
    bias,
):
    query_heads, key_heads, head_dim = sizes
    group_size = query_heads // key_heads
    heads = query_heads + key_heads
    columns = natural.shape[1]
    quarter = grad_a_ref.shape[0]
    out_weight = weight_ref[:, columns:]
    for q, rows_ref in enumerate((grad_a_ref, grad_b_ref, grad_c_ref, grad_d_ref)):
        mixed[q * quarter : (q + 1) * quarter, :] = dot(rows_ref[...], out_weight).astype(BFLOAT)
    collect(place_ref, mixed, context)
    for head in range(query_heads):
        part = context[:, head * head_dim : (head + 1) * head_dim]
        grad_row[head] = part
        grad_col[head] = part.astype(SINGLE).T
    key_grad[...] = jnp.zeros(key_grad.shape, SINGLE)
    value_grad[...] = jnp.zeros(value_grad.shape, SINGLE)
    scale = head_dim ** (-0.5)
    factor = LOG2E * scale
    for start in range(0, LEN, TILE):
        low, high = key_span(start)
        span, tile = slice(low, high), slice(start, start + TILE)
        bias[: high - low, :] = mask_bias(begin_ref, start, low, high)

        def one_head(head, carry):
            key_head = head // group_size
            scores = dot(key_row_ref[key_head, span, :], query_ref[head, :, tile])
            probs = jnp.exp2(scores * factor + bias[: high - low, :] - total_ref[head, :, tile])
            grads = grad_col[head, :, tile]
            inner = jnp.sum(grads * attended_ref[head, :, tile], axis=0, keepdims=True)
            probs_grad = dot(value_row_ref[key_head, span, :], grads.astype(BFLOAT))
            scores_grad = (probs * (probs_grad - inner)).astype(BFLOAT)
            value_grad[key_head, span, :] += dot(probs.astype(BFLOAT), grad_row[head, tile, :])
            key_grad[key_head, span, :] += dot(scores_grad, query_row_ref[head, tile, :])
            query_grad[head, :, tile] = dot(key_ref[key_head, :, span], scores_grad)
            return carry

        lax.fori_loop(0, query_heads, one_head, 0)
    cosine, sine = cosine_ref[...], sine_ref[...]
    gains = gain_columns(gain_ref, head_dim)
    for kind in range(2):
        head_gain_ref[kind] = jnp.zeros(head_gain_ref.shape[1:], SINGLE)
    for head in range(heads):
        kind = 0 if head < query_heads else 1
        grads = query_grad[head] if kind == 0 else key_grad[head - query_heads].T
        grads = turn(grads * scale, cosine, -sine)
        values = raw_ref[head * head_dim : (head + 1) * head_dim, :]
        ratio = head_ratio(values)
        normed = values * ratio
        weighted = grads * gains[kind]
        inner = jnp.mean(weighted * normed, axis=0, keepdims=True)
        joined[head * head_dim : (head + 1) * head_dim, :] = ratio * (weighted - normed * inner)
        products = grads * normed
        folded = products[:, :128]
        for first in range(128, LEN, 128):
            folded = folded + products[:, first : first + 128]
        head_gain_ref[kind] += folded
    for start in range(0, LEN, 128):
        natural[start : start + 128, : heads * head_dim] = joined[:, start : start + 128].T.astype(
            BFLOAT
        )
    for head in range(key_heads):
        first = (heads + head) * head_dim
        natural[:, first : first + head_dim] = value_grad[head].astype(BFLOAT)
    spread(place_ref, natural, out_ref)
    weight = weight_ref[:, :columns]
    row_gain = jnp.zeros(row_gain_ref.shape, SINGLE)
    rows_refs = (rows_a_ref, rows_b_ref, rows_c_ref, rows_d_ref)
    for q, part_ref in enumerate((part_a_ref, part_b_ref, part_c_ref, part_d_ref)):
        part = dot_last(out_ref[q * quarter : (q + 1) * quarter, :], weight)
        part_ref[...] = part.astype(BFLOAT)
        row_gain += jnp.sum(part * rows_refs[q][...].astype(SINGLE), axis=0, keepdims=True)
    row_gain_ref[...] = row_gain


def attend_back(sizes, place, grads, quarters, weight, gains, saved):
    query_heads, key_heads, head_dim = sizes
    heads = query_heads + key_heads
    columns = (heads + key_heads) * head_dim
    quarter, width = quarters[0].shape
    shapes = [
        ((LEN, columns), BFLOAT),
        ((2, head_dim, 128), SINGLE),
        ((1, width), SINGLE),
    ] + [((quarter, width), BFLOAT)] * 4
    scratch = [
        ((LEN, query_heads * head_dim), BFLOAT),
        ((LEN, query_heads * head_dim), BFLOAT),
        ((query_heads, LEN, head_dim), BFLOAT),
        ((query_heads, head_dim, LEN), SINGLE),
        ((query_heads, head_dim, LEN), SINGLE),
        ((key_heads, LEN, head_dim), SINGLE),
        ((key_heads, LEN, head_dim), SINGLE),
        ((heads * head_dim, LEN), SINGLE),
        ((LEN, columns), BFLOAT),
        ((LEN, TILE), SINGLE),
    ]
    arrays = (*grads, *quarters, weight, gains, *saved)
    outs = call_kernel(
        partial(attend_back_kernel, sizes), "attend_back", HEAVY, shapes, (place,), arrays, scratch
    )
    return outs[0], outs[1], outs[2], outs[3:]


def feedfwd_kernel(
    rows_a_ref,
    rows_b_ref,
    rows_c_ref,
    rows_d_ref,
    cot_a_ref,
    cot_b_ref,
    cot_c_ref,
    cot_d_ref,
    weight_ref,
    hidden_ref,
    grad_ref,
    part_a_ref,
    part_b_ref,
    part_c_ref,
    part_d_ref,
    gate_up,
    grad_hidden,
):
    hidden_cols = hidden_ref.shape[1]
    quarter = rows_a_ref.shape[0]
    step = 384 if hidden_cols % 384 == 0 else hidden_cols
    quarters = (
        (rows_a_ref, cot_a_ref, part_a_ref),
        (rows_b_ref, cot_b_ref, part_b_ref),
        (rows_c_ref, cot_c_ref, part_c_ref),
        (rows_d_ref, cot_d_ref, part_d_ref),
    )
    for q, (rows_ref, cot_ref, part_ref) in enumerate(quarters):
        tile, slot = slice(q * quarter, (q + 1) * quarter), q % 2
        gate_up[slot] = dot(rows_ref[...], weight_ref[:, : 2 * hidden_cols])
        grad_hidden[slot] = dot(cot_ref[...], weight_ref[:, 2 * hidden_cols :])
        for first in range(0, hidden_cols, step):
            cols = slice(first, first + step)
            up_cols = slice(hidden_cols + first, hidden_cols + first + step)
            gate_proj, upward = gate_up[slot, :, cols], gate_up[slot, :, up_cols]
            grads = grad_hidden[slot, :, cols]
            sigmoid = 1.0 / (1.0 + jnp.exp(-gate_proj))
            active = gate_proj * sigmoid
            hidden_ref[tile, cols] = (active * upward).astype(BFLOAT)
            slope = sigmoid * (1.0 + gate_proj * (1.0 - sigmoid))
            grad_ref[tile, cols] = (grads * upward * slope).astype(BFLOAT)
            grad_ref[tile, up_cols] = (grads * active).astype(BFLOAT)
        part_ref[...] = dot_last(grad_ref[tile, :], weight_ref[:, : 2 * hidden_cols]).astype(BFLOAT)


def feedfwd(quarters, cots, weight):
    quarter, width = quarters[0].shape
    hidden_cols = weight.shape[1] // 3
    shapes = [((LEN, hidden_cols), BFLOAT), ((LEN, 2 * hidden_cols), BFLOAT)]
    shapes += [((quarter, width), BFLOAT)] * 4
    scratch = [((2, quarter, 2 * hidden_cols), SINGLE), ((2, quarter, hidden_cols), SINGLE)]
    outs = call_kernel(
        feedfwd_kernel, "feedfwd", HEAVY, shapes, (), (*quarters, *cots, weight), scratch
    )
    return outs[0], outs[1], outs[2:]


def weights_kernel(
    first_tiles,
    first_a_ref,
    first_b_ref,
    first_c_ref,
    first_d_ref,
    second_a_ref,
    second_b_ref,
    second_c_ref,
    second_d_ref,
    first_grad_ref,
    second_grad_ref,
    out_ref,
    turned_ref,
):
    step = pl.program_id(0)
    quarter = first_a_ref.shape[0]

    def turn_over(*refs):
        for q, ref in enumerate(refs):
            turned_ref[:, q * quarter : (q + 1) * quarter] = ref[...].T

    @pl.when(step == 0)
    def _():
        turn_over(first_a_ref, first_b_ref, first_c_ref, first_d_ref)

    @pl.when(step < first_tiles)
    def _():
        out_ref[...] = dot(turned_ref[...], first_grad_ref[...]).astype(BFLOAT)

    @pl.when(step == first_tiles)
    def _():
        turn_over(second_a_ref, second_b_ref, second_c_ref, second_d_ref)

    @pl.when(step >= first_tiles)
    def _():
        out_ref[...] = dot(turned_ref[...], second_grad_ref[...]).astype(BFLOAT)


def weight_parts(firsts, first_grad, seconds, second_grad):
    first_cols, second_cols = first_grad.shape[1], second_grad.shape[1]
    quarter, width = firsts[0].shape
    tiles = [t for t in (1152, 256, 128) if first_cols % t == 0 and second_cols % t == 0]
    if not tiles:
        sums = []
        for lefts, right in ((firsts, first_grad), (seconds, second_grad)):
            left = jnp.concatenate(lefts, axis=0)
            total = jnp.einsum("nd,ne->de", left, right, preferred_element_type=SINGLE)
            sums.append(total.astype(BFLOAT))
        return jnp.concatenate(sums, axis=1)
    tile = tiles[0]
    first_tiles = first_cols // tile
    whole = pl.BlockSpec((quarter, width), lambda j: (0, 0))
    first_spec = pl.BlockSpec((LEN, tile), lambda j: (0, jnp.minimum(j, first_tiles - 1)))
    second_spec = pl.BlockSpec((LEN, tile), lambda j: (0, jnp.maximum(j - first_tiles, 0)))
    columns = first_cols + second_cols
    return pl.pallas_call(
        partial(weights_kernel, first_tiles),
        grid=(columns // tile,),
        out_shape=jax.ShapeDtypeStruct((width, columns), BFLOAT),
        in_specs=[whole] * 8 + [first_spec, second_spec],
        out_specs=pl.BlockSpec((width, tile), lambda j: (0, j)),
        scratch_shapes=[pltpu.VMEM((width, LEN), BFLOAT)],
        compiler_params=pltpu.CompilerParams(vmem_limit_bytes=VMEM_LIMIT),
        cost_estimate=pl.CostEstimate(flops=LIGHT, bytes_accessed=2**20, transcendentals=0),
        name="weight_parts",
    )(*firsts, *seconds, first_grad, second_grad)


def pair_sum_kernel(stay_a_ref, got_a_ref, stay_b_ref, got_b_ref, *refs):
    outs = refs[-4:]
    rows = stay_a_ref.shape[0] // 2
    pairs = ((stay_a_ref, got_a_ref), (stay_b_ref, got_b_ref))
    for half, (stay_ref, got_ref) in enumerate(pairs):
        total = stay_ref[...].astype(SINGLE) + got_ref[...].astype(SINGLE)
        outs[2 * half][...] = total[:rows].astype(outs[2 * half].dtype)
        outs[2 * half + 1][...] = total[rows:].astype(BFLOAT)


def pair_sum(stays, gots, last, earlier):
    rows, width = stays[0].shape
    shapes = [((rows // 2, width), SINGLE if last else BFLOAT), ((rows // 2, width), BFLOAT)] * 2
    arrays = (stays[0], gots[0], stays[1], gots[1])
    outs = call_kernel(
        pair_sum_kernel, "pair_sum", LIGHT, shapes, (), arrays, earlier=earlier
    )
    return outs[0::2], outs[1::2]


def down_kernel(hidden_ref, weight_ref, *refs):
    quarter = hidden_ref.shape[0] // 4
    for q, part_ref in enumerate(refs[-4:]):
        rows = hidden_ref[q * quarter : (q + 1) * quarter, :]
        part_ref[...] = dot_last(rows, weight_ref[...]).astype(BFLOAT)


def down_parts_of(hidden, weight, earlier):
    hidden_cols = hidden.shape[1]
    quarter, width = LEN // 4, weight.shape[0]
    if hidden_cols % 128:
        down = weight[:, 2 * hidden_cols :]
        return [
            dot_last(hidden[q * quarter : (q + 1) * quarter], down).astype(BFLOAT) for q in range(4)
        ]
    part = pl.BlockSpec((quarter, width), lambda i: (0, 0))
    return pl.pallas_call(
        down_kernel,
        grid=(1,),
        out_shape=[jax.ShapeDtypeStruct((quarter, width), BFLOAT)] * 4,
        in_specs=[
            pl.BlockSpec((LEN, hidden_cols), lambda i: (0, 0)),
            pl.BlockSpec((width, hidden_cols), lambda i: (0, 2)),
        ]
        + [pl.BlockSpec(memory_space=pl.ANY)] * len(earlier),
        out_specs=[part] * 4,
        compiler_params=pltpu.CompilerParams(vmem_limit_bytes=VMEM_LIMIT),
        cost_estimate=pl.CostEstimate(flops=LIGHT, bytes_accessed=2**20, transcendentals=0),
        name="down_parts",
    )(hidden, weight, *earlier)


def later(value, earlier):
    anywhere = pl.BlockSpec(memory_space=pl.ANY)
    return pl.pallas_call(
        lambda *refs: None,
        out_shape=jax.ShapeDtypeStruct(value.shape, value.dtype),
        in_specs=[anywhere, anywhere],
        out_specs=anywhere,
        input_output_aliases={0: 0},
        name="later",
    )(value, earlier)


def rms_scale(values, gain):
    return values * lax.rsqrt(jnp.mean(values * values, axis=-1, keepdims=True) + EPSILON) * gain


def swap(value, axis, bit):
    size = lax.axis_size(axis)
    return lax.ppermute(value, axis, [(i, i ^ bit) for i in range(size)])


def axis_bits(axis):
    return [1 << k for k in range(lax.axis_size(axis).bit_length() - 1)]


def block_order(bits):
    order = [0]
    for bit in bits:
        order = order + [r ^ bit for r in order]
    return order


def butterfly_sum(value):
    for axis in ("dp", "tensor"):
        for bit in axis_bits(axis):
            value = value + swap(value, axis, bit)
    return value


def rms_back(values, gain, grad):
    ratio = lax.rsqrt(jnp.mean(values * values, axis=-1, keepdims=True) + EPSILON)
    scaled = grad * gain
    inner = jnp.mean(scaled * values, axis=-1, keepdims=True)
    return ratio * scaled - values * (ratio * ratio * ratio * inner), grad * values * ratio


def on_device(
    tokens,
    segments,
    cotangent,
    query_weight,
    key_weight,
    value_weight,
    out_weight,
    gate_weight,
    up_weight,
    down_weight,
    attention_gain,
    feedfwd_gain,
    query_gain,
    key_gain,
):
    head_dim = query_gain.shape[0]
    local_rows, width = tokens.shape
    half_rows = local_rows // 2
    tensor_size, here = lax.axis_size("tensor"), lax.axis_index("tensor")
    tensor_bits = axis_bits("tensor")
    half_bits = (tensor_bits, tensor_bits[::-1])
    half_order = [block_order(bits) for bits in half_bits]
    place = jnp.stack(
        [
            jnp.array([order.index(r) for r in range(tensor_size)], jnp.int32)[here ^ j] * half_rows
            + c * (LEN // 2)
            for j in range(tensor_size)
            for c, order in enumerate(half_order)
        ]
    )

    def rows_gather(halves):
        for bits in zip(*half_bits):
            pairs = [(part, swap(part, "tensor", bit)) for part, bit in zip(halves, bits)]
            halves = [jnp.concatenate(pair, axis=0) for pair in pairs]
        return [*pairs[0], *pairs[1]]

    def rows_scatter(parts, earlier=()):
        stays, aways = parts[0::2], parts[1::2]
        for step, bits in enumerate(zip(*(bits[::-1] for bits in half_bits))):
            gots = [swap(part, "tensor", bit) for part, bit in zip(aways, bits)]
            if step < len(tensor_bits) - 1:
                last = step == len(tensor_bits) - 2
                stays, aways = pair_sum(stays, gots, last, earlier)
                earlier = ()
        return [stay.astype(SINGLE) + got.astype(SINGLE) for stay, got in zip(stays, gots)]

    def halves_of(value):
        return [value[:half_rows], value[half_rows:]]

    token_values = tokens.astype(SINGLE)
    normed = rms_scale(token_values, attention_gain).astype(BFLOAT)
    gathered = rows_gather(halves_of(normed))
    attention_full = lax.all_gather(
        jnp.concatenate([query_weight, key_weight, value_weight, out_weight.T], axis=1),
        "dp",
        axis=0,
        tiled=True,
    )
    feedfwd_full = lax.all_gather(
        jnp.concatenate([gate_weight, up_weight, down_weight.T], axis=1), "dp", axis=0, tiled=True
    )
    cots = rows_gather(halves_of(cotangent))

    hidden_cols = gate_weight.shape[1]
    query_cols, key_cols = query_weight.shape[1], key_weight.shape[1]
    qkv_cols = query_cols + 2 * key_cols
    sizes = (query_cols // head_dim, key_cols // head_dim, head_dim)
    gains = jnp.concatenate([query_gain, key_gain])[None, :]
    saved, context, attended_parts = attend(
        sizes, place, gathered, attention_full, gains, segments[None, :]
    )
    residuals, normed_two = [], []
    for token_part, sum_part in zip(halves_of(token_values), rows_scatter(attended_parts)):
        residuals.append(token_part + sum_part)
        normed_two.append(rms_scale(residuals[-1], feedfwd_gain).astype(BFLOAT))
    gathered_two = rows_gather(normed_two)

    hidden, gate_up_grad, two_parts = feedfwd(gathered_two, cots, feedfwd_full)
    feedfwd_part = weight_parts(gathered_two, gate_up_grad, cots, hidden)
    grad_feedfwd = lax.psum_scatter(feedfwd_part, "dp", scatter_dimension=0, tiled=True)
    two_sums = rows_scatter(two_parts, (feedfwd_part,))
    grad_residual, gain_two_part = [], 0.0
    for residual_part, sum_part, cot_part in zip(residuals, two_sums, halves_of(cotangent)):
        back, gain_part = rms_back(residual_part, feedfwd_gain, sum_part)
        grad_residual.append(cot_part.astype(SINGLE) + back)
        gain_two_part = gain_two_part + jnp.sum(gain_part, axis=0)
    gathered_grad = rows_gather([part.astype(BFLOAT) for part in grad_residual])

    qkv_grad, head_gains, row_gain, normed_parts = attend_back(
        sizes, place, gathered_grad, gathered, attention_full, gains, saved
    )
    attention_part = weight_parts(gathered, qkv_grad, gathered_grad, context)
    grad_attention = lax.psum_scatter(
        later(attention_part, grad_feedfwd), "dp", scatter_dimension=0, tiled=True
    )
    normed_sums = rows_scatter(normed_parts)
    grad_tokens = []
    for token_part, sum_part, grad_part in zip(
        halves_of(token_values), normed_sums, grad_residual
    ):
        back, _ = rms_back(token_part, attention_gain, sum_part)
        grad_tokens.append((grad_part + back).astype(BFLOAT))

    down_parts = down_parts_of(hidden, feedfwd_full, gathered_grad)
    down_sums = rows_scatter(down_parts)
    block_out = [(res + part).astype(BFLOAT) for res, part in zip(residuals, down_sums)]

    gain_sums = butterfly_sum(
        jnp.concatenate(
            [row_gain[0] / attention_gain, gain_two_part, *jnp.sum(head_gains, axis=2)]
        )
    )
    grad_attention, grad_feedfwd = grad_attention.astype(SINGLE), grad_feedfwd.astype(SINGLE)
    return (
        jnp.concatenate(block_out, axis=0),
        jnp.concatenate(grad_tokens, axis=0),
        grad_attention[:, :query_cols],
        grad_attention[:, query_cols : query_cols + key_cols],
        grad_attention[:, query_cols + key_cols : qkv_cols],
        grad_attention[:, qkv_cols:].T,
        grad_feedfwd[:, :hidden_cols],
        grad_feedfwd[:, hidden_cols : 2 * hidden_cols],
        grad_feedfwd[:, 2 * hidden_cols :].T,
        gain_sums[:width],
        gain_sums[width : 2 * width],
        gain_sums[2 * width : 2 * width + head_dim],
        gain_sums[2 * width + head_dim :],
    )


def solution(mesh):
    in_specs = (
        P(("dp", "tensor"), None),
        P("dp"),
        P(("dp", "tensor"), None),
        P("dp", "tensor"),
        P("dp", "tensor"),
        P("dp", "tensor"),
        P("tensor", "dp"),
        P("dp", "tensor"),
        P("dp", "tensor"),
        P("tensor", "dp"),
        P(),
        P(),
        P(),
        P(),
    )
    out_specs = (
        P(("dp", "tensor"), None),
        P(("dp", "tensor"), None),
        P("dp", "tensor"),
        P("dp", "tensor"),
        P("dp", "tensor"),
        P("tensor", "dp"),
        P("dp", "tensor"),
        P("dp", "tensor"),
        P("tensor", "dp"),
        P(),
        P(),
        P(),
        P(),
    )
    return jax.shard_map(
        on_device, mesh=mesh, in_specs=in_specs, out_specs=out_specs, check_vma=False
    )
```

profile of v0, /device:TPU:0, one launch (start us, length us, event | category | flops | bytes accessed | tf_op | source)
XLA Modules:
  0.0 293.7 jit_solution(11889258041275239058)
XLA Ops:
  8.2 1.6 pad_maximum_fusion.11
  9.8 1.2 copy.37
  11.0 2.1 pad_maximum_fusion
  13.7 3.0 %collective-permute-start = (bf16[128,1024]{1,0:T(8,128)(2,1)S(1)}, bf16[128,1024]{1,0:T(8,128)(2,1)S(1)}, u32[]{:S(2)}, u32[]{:S(2)}) collective-permute-start(bf16[128,1024]{1,0:T(8,128)(2,1)S(1)} %get-tuple-element.151), channel_id=1, source_target_pairs={{0,1},{1,0},{2,3},{3,2},{4,5},{5,4},{6,7},{7,6},{8,9},{9,8},{10,11... | collective-permute-start | bytes 786440 | tf_op jit(solution)/shard_map/ppermute | solution.py:566
  16.7 1.5 collective-permute-start.2
  18.2 4.8 %collective-permute-done = bf16[128,1024]{1,0:T(8,128)(2,1)S(1)} collective-permute-done((bf16[128,1024]{1,0:T(8,128)(2,1)S(1)}, bf16[128,1024]{1,0:T(8,128)(2,1)S(1)}, u32[]{:S(2)}, u32[]{:S(2)}) %collective-permute-start) | collective-permute-done | bytes 262176 | tf_op jit(solution)/shard_map/ppermute | solution.py:566
  23.1 1.8 collective-permute-start.1
  24.9 1.6 collective-permute-start.3
  30.9 5.3 %collective-permute-done.1.rows_b_ref.first_b_ref = bf16[256,1024]{1,0:T(8,128)(2,1)S(1)} collective-permute-done((bf16[256,1024]{1,0:T(8,128)(2,1)S(1)}, bf16[256,1024]{1,0:T(8,128)(2,1)S(1)}, u32[]{:S(2)}, u32[]{:S(2)}) %collective-permute-start.1) | collective-permute-done | bytes 524320 | tf_op jit(solution)/shard_map/ppermute | solution.py:566
  36.2 1.3 collective-permute-done.3.rows_d_ref.first_d_ref
  38.3 16.5 %attend.1 = (f32[512,1024]{1,0:T(8,128)}, bf16[4,64,1024]{2,1,0:T(8,128)(2,1)}, bf16[2,64,1024]{2,1,0:T(8,128)(2,1)}, bf16[4,1024,64]{2,1,0:T(8,128)(2,1)}, bf16...) custom-call(s32[8]{0:T(128)} %stack.2.place_ref, ...), custom_call_target="tpu_custom_call" | custom-call | flops 16000000000 | bytes 1048576 | tf_op jit(solution)/shard_map/attend/pallas_call | solution.py:29
  54.8 1.2 collective-permute-start.4
  56.1 1.5 collective-permute-start.5
  57.5 11.3 %collective-permute-done.4.got_a_ref = bf16[256,1024]{1,0:T(8,128)(2,1)S(1)} collective-permute-done((bf16[256,1024]{1,0:T(8,128)(2,1)}, bf16[256,1024]{1,0:T(8,128)(2,1)S(1)}, u32[]{:S(2)}, u32[]{:S(2)}) %collective-permute-start.4) | collective-permute-done | bytes 524320 | tf_op jit(solution)/shard_map/ppermute | solution.py:566
  68.9 1.2 collective-permute-done.5.got_b_ref
  70.9 2.8 pair_sum.4
  73.7 1.5 collective-permute-start.6
  75.7 1.5 collective-permute-start.14
  78.0 5.2 %collective-permute-done.6 = bf16[128,1024]{1,0:T(8,128)(2,1)S(1)} collective-permute-done((bf16[128,1024]{1,0:T(8,128)(2,1)}, bf16[128,1024]{1,0:T(8,128)(2,1)S(1)}, u32[]{:S(2)}, u32[]{:S(2)}) %collective-permute-start.6) | collective-permute-done | bytes 262176 | tf_op jit(solution)/shard_map/ppermute | solution.py:566
  83.1 1.5 collective-permute-done.9
  86.6 2.1 collective-permute-done.12
  91.0 3.8 %collective-permute-done.7 = bf16[128,1024]{1,0:T(8,128)(2,1)S(1)} collective-permute-done((bf16[128,1024]{1,0:T(8,128)(2,1)S(1)}, bf16[128,1024]{1,0:T(8,128)(2,1)S(1)}, u32[]{:S(2)}, u32[]{:S(2)}) %collective-permute-start.7) | collective-permute-done | bytes 262176 | tf_op jit(solution)/shard_map/ppermute | solution.py:566
  95.9 1.0 collective-permute-start.11
  96.9 10.2 %collective-permute-done.13.cot_b_ref.second_b_ref = bf16[256,1024]{1,0:T(8,128)(2,1)S(1)} collective-permute-done((bf16[256,1024]{1,0:T(8,128)(2,1)S(1)}, bf16[256,1024]{1,0:T(8,128)(2,1)S(1)}, u32[]{:S(2)}, u32[]{:S(2)}) %collective-permute-start.13) | collective-permute-done | bytes 524320 | tf_op jit(solution)/shard_map/ppermute | solution.py:566
  107.1 9.1 %collective-permute-done.8.rows_b_ref.first_b_ref = bf16[256,1024]{1,0:T(8,128)(2,1)S(1)} collective-permute-done((bf16[256,1024]{1,0:T(8,128)(2,1)S(1)}, bf16[256,1024]{1,0:T(8,128)(2,1)S(1)}, u32[]{:S(2)}, u32[]{:S(2)}) %collective-permute-start.8) | collective-permute-done | bytes 524320 | tf_op jit(solution)/shard_map/ppermute | solution.py:566
  117.0 19.5 %feedfwd.1 = (bf16[1024,1152]{1,0:T(8,128)(2,1)}, bf16[1024,2304]{1,0:T(8,128)(2,1)}, bf16[256,1024]{1,0:T(8,128)(2,1)}, bf16[256,1024]{1,0:T(8,128)(2,1)}, bf16...) custom-call(bf16[256,1024]{1,0:T(8,128)(2,1)} %copy-done.13, bf16[256,1024]{1,0:T(8,128)(2,1)} %copy-done.25, ...), custom_call_target="tpu_custom_call" | custom-call | flops 16000000000 | bytes 1048576 | tf_op jit(solution)/shard_map/feedfwd/pallas_call | solution.py:29
  136.5 15.1 %weight_parts.2.refs_0_ = bf16[1024,3456]{1,0:T(8,128)(2,1)} custom-call(bf16[256,1024]{1,0:T(8,128)(2,1)} %copy-done.13, bf16[256,1024]{1,0:T(8,128)(2,1)} %copy-done.25, bf16[256,1024]{1,0:T(8,128)(2,1)} %copy-done.14, bf16[256,1024]{1,0:T(8,128)(2,1)} %collective-permute-done.11.rows_d_ref.first_d_ref, bf16[256,1024]{1,0:T(8,128)(2,1)} %copy-done.11, ...), custom_call_target="tpu_custom_call" | custom-call | flops 1000000000 | bytes 1048576 | tf_op jit(solution)/shard_map/weight_parts/pallas_call | solution.py:483
  153.2 10.7 %collective-permute-done.16.got_a_ref = bf16[256,1024]{1,0:T(8,128)(2,1)S(1)} collective-permute-done((bf16[256,1024]{1,0:T(8,128)(2,1)}, bf16[256,1024]{1,0:T(8,128)(2,1)S(1)}, u32[]{:S(2)}, u32[]{:S(2)}) %collective-permute-start.16) | collective-permute-done | bytes 524320 | tf_op jit(solution)/shard_map/ppermute | solution.py:566
  165.4 2.7 pair_sum.5
  169.4 5.3 %collective-permute-done.18 = bf16[128,1024]{1,0:T(8,128)(2,1)S(1)} collective-permute-done((bf16[128,1024]{1,0:T(8,128)(2,1)}, bf16[128,1024]{1,0:T(8,128)(2,1)S(1)}, u32[]{:S(2)}, u32[]{:S(2)}) %collective-permute-start.18) | collective-permute-done | bytes 262176 | tf_op jit(solution)/shard_map/ppermute | solution.py:566
  175.1 1.6 multiply_reduce_fusion.1
  176.7 1.3 fusion.4
  178.0 1.7 collective-permute-start.19
  179.7 1.0 collective-permute-start.22
  180.6 4.0 %collective-permute-done.19 = bf16[128,1024]{1,0:T(8,128)(2,1)S(1)} collective-permute-done((bf16[128,1024]{1,0:T(8,128)(2,1)S(1)}, bf16[128,1024]{1,0:T(8,128)(2,1)S(1)}, u32[]{:S(2)}, u32[]{:S(2)}) %collective-permute-start.19) | collective-permute-done | bytes 262176 | tf_op jit(solution)/shard_map/ppermute | solution.py:566
  184.7 1.1 collective-permute-start.20
  185.8 3.0 %collective-permute-done.22 = bf16[128,1024]{1,0:T(8,128)(2,1)S(1)} collective-permute-done((bf16[128,1024]{1,0:T(8,128)(2,1)S(1)}, bf16[128,1024]{1,0:T(8,128)(2,1)S(1)}, u32[]{:S(2)}, u32[]{:S(2)}) %collective-permute-start.22) | collective-permute-done | bytes 262176 | tf_op jit(solution)/shard_map/ppermute | solution.py:566
  188.9 7.7 %collective-permute-done.20.refs_1_.grad_b_ref.second_b_ref = bf16[256,1024]{1,0:T(8,128)(2,1)S(1)} collective-permute-done((bf16[256,1024]{1,0:T(8,128)(2,1)S(1)}, bf16[256,1024]{1,0:T(8,128)(2,1)S(1)}, u32[]{:S(2)}, u32[]{:S(2)}) %collective-permute-start.20) | collective-permute-done | bytes 524320 | tf_op jit(solution)/shard_map/ppermute | solution.py:566
  196.6 1.4 collective-permute-done.23.refs_3_.grad_d_ref.second_d_ref
  198.9 18.9 %attend_back.1 = (bf16[1024,512]{1,0:T(8,128)(2,1)}, f32[2,64,128]{2,1,0:T(8,128)}, f32[1,1024]{1,0:T(1,128)}, bf16[256,1024]{1,0:T(8,128)(2,1)}, bf16[256,1024]...) custom-call(s32[8]{0:T(128)} %stack.2.place_ref, bf16[256,1024]{1,0:T(8,128)(2,1)} %copy-done.1, ...), custom_call_target="tpu_custom_call" | custom-call | flops 16000000000 | bytes 1048576 | tf_op jit(solution)/shard_map/attend_back/pallas_call | solution.py:29
  218.5 6.3 %down_parts.1 = (bf16[256,1024]{1,0:T(8,128)(2,1)}, bf16[256,1024]{1,0:T(8,128)(2,1)}, bf16[256,1024]{1,0:T(8,128)(2,1)}, bf16[256,1024]{1,0:T(8,128)(2,1)}) custom-call(bf16[1024,1152]{1,0:T(8,128)(2,1)} %get-tuple-element.70.second_grad_ref.hidden_ref, bf16[1024,3456]{1,0:T(8,128)(2,1)} %all-gather.5.cloned.1.call-done.weight_ref, ...), custom_call_target="tpu_custom_call" | custom-call | flops 1000000000 | bytes 1048576 | tf_op jit(solution)/shard_map/down_parts/pallas_call | solution.py:532
  224.7 1.0 collective-permute-start.24
  225.9 1.2 collective-permute-done.32
  227.1 1.5 collective-permute-start.33
  228.6 2.2 collective-permute-done.33
  230.8 1.4 collective-permute-start.34
  232.1 3.2 %collective-permute-done.34 = f32[2176]{0:T(1024)S(1)} collective-permute-done((f32[2176]{0:T(1024)S(1)}, f32[2176]{0:T(1024)S(1)}, u32[]{:S(2)}, u32[]{:S(2)}) %collective-permute-start.34) | collective-permute-done | bytes 8736 | tf_op jit(solution)/shard_map/ppermute | solution.py:566
  235.4 2.0 collective-permute-start.35
  237.4 1.1 collective-permute-start.28
  239.2 1.1 collective-permute-start.36
  240.3 6.9 %weight_parts.3.refs_0_ = bf16[1024,768]{1,0:T(8,128)(2,1)} custom-call(bf16[256,1024]{1,0:T(8,128)(2,1)} %copy-done.6, bf16[256,1024]{1,0:T(8,128)(2,1)} %copy-done.19, bf16[256,1024]{1,0:T(8,128)(2,1)} %copy-done.7, bf16[256,1024]{1,0:T(8,128)(2,1)} %copy-done.20, bf16[256,1024]{1,0:T(8,128)(2,1)} %copy-done.1, bf16[256,1024]{1,0:T(8,128)(2,1)} %copy-done.4, ...), custom_call_target="tpu_custom_call" | custom-call | flops 1000000000 | bytes 1048576 | tf_op jit(solution)/shard_map/weight_parts/pallas_call | solution.py:483
  247.2 2.3 collective-permute-done.36
  250.1 2.7 pair_sum.6
  253.8 1.1 collective-permute-start.27
  254.9 2.8 pair_sum.7
  257.7 1.7 collective-permute-start.30
  259.4 1.0 collective-permute-start.31
  260.3 1.2 collective-permute-done.26
  263.2 1.9 collective-permute-done.30
  267.7 1.1 copy.39
  268.8 1.1 fusion.6
  269.9 12.2 %reduce-scatter.5.cloned.1.call-done = bf16[128,768]{1,0:T(8,128)(2,1)} async-done(((bf16[1024,768]{1,0:T(8,128)(2,1)}), bf16[128,768]{1,0:T(8,128)(2,1)}) %reduce-scatter.5.cloned.1.call-update) | async-done | bytes 196624 | tf_op jit(solution)/shard_map/reduce_scatter | solution.py:688
  283.8 1.5 slice.76
  285.3 1.4 fusion.9
  (172 shorter events, 27.3 us)
Async XLA Ops:
  7.2 30.8 %all-gather.3.cloned.1.call-start = ((), (), s32[]{:S(2)}) async-start(), calls=%async_computation.2 | async-start | bytes 1769472 | tf_op jit(solution)/shard_map/all_gather | solution.py:648
  9.8 107.2 %all-gather.5.cloned.1.call-start = ((), (), s32[]{:S(2)}) async-start(), calls=%async_computation.3 | async-start | bytes 7962624 | tf_op jit(solution)/shard_map/all_gather | solution.py:654
  13.2 236.9 %reduce-scatter.3.cloned.1.call-start = ((), (), s32[]{:S(2)}) async-start(), calls=%async_computation.4 | async-start | bytes 7962624 | tf_op jit(solution)/shard_map/reduce_scatter | solution.py:675
  13.6 12.9 %copy-start.33 = (s32[4]{0:T(128)S(1)}, s32[4]{0:T(128)}, u32[]{:S(2)}) copy-start(s32[4]{0:T(128)} %constant.51.clone) | copy-start | bytes 52
  13.6 16.7 %copy-start.39 = (f32[64]{0:T(128)S(1)}, f32[64]{0:T(128)}, u32[]{:S(2)}) copy-start(f32[64]{0:T(128)} %param.35) | copy-start | bytes 772
  13.6 16.7 %copy-start.40 = (f32[64]{0:T(128)S(1)}, f32[64]{0:T(128)}, u32[]{:S(2)}) copy-start(f32[64]{0:T(128)} %param.34) | copy-start | bytes 772
  13.7 9.3 %collective-permute-start = (bf16[128,1024]{1,0:T(8,128)(2,1)S(1)}, bf16[128,1024]{1,0:T(8,128)(2,1)S(1)}, u32[]{:S(2)}, u32[]{:S(2)}) collective-permute-start(bf16[128,1024]{1,0:T(8,128)(2,1)S(1)} %get-tuple-element.151), channel_id=1, source_target_pairs={{0,1},{1,0},{2,3},{3,2},{4,5},{5,4},{6,7},{7,6},{8,9},{9,8},{10,11... | collective-permute-start | bytes 786440 | tf_op jit(solution)/shard_map/ppermute | solution.py:566
  16.7 8.2 %collective-permute-start.2 = (bf16[128,1024]{1,0:T(8,128)(2,1)S(1)}, bf16[128,1024]{1,0:T(8,128)(2,1)S(1)}, u32[]{:S(2)}, u32[]{:S(2)}) collective-permute-start(bf16[128,1024]{1,0:T(8,128)(2,1)S(1)} %get-tuple-element.150), channel_id=1, source_target_pairs={{0,2},{1,3},{2,0},{3,1},{4,6},{5,7},{6,4},{7,5},{8,10},{9,11},{10,... | collective-permute-start | bytes 786440 | tf_op jit(solution)/shard_map/ppermute | solution.py:566
  23.0 15.0 %copy-start.6 = (bf16[256,1024]{1,0:T(8,128)(2,1)}, bf16[256,1024]{1,0:T(8,128)(2,1)S(1)}, u32[]{:S(2)}) copy-start(bf16[256,1024]{1,0:T(8,128)(2,1)S(1)} %pad_maximum_fusion.1.rows_a_ref.first_a_ref) | copy-start | bytes 1572868
  23.1 13.2 %collective-permute-start.1 = (bf16[256,1024]{1,0:T(8,128)(2,1)S(1)}, bf16[256,1024]{1,0:T(8,128)(2,1)S(1)}, u32[]{:S(2)}, u32[]{:S(2)}) collective-permute-start(bf16[256,1024]{1,0:T(8,128)(2,1)S(1)} %pad_maximum_fusion.1.rows_a_ref.first_a_ref), channel_id=1, source_target_pairs={{0,2},{1,3},{2,0},{3,1},{4,6},{5,7},{6,4},{7,5},{8,10},{9,11},{10,... | collective-permute-start | bytes 1572872 | tf_op jit(solution)/shard_map/ppermute | solution.py:566
  24.9 13.1 %copy-start.7 = (bf16[256,1024]{1,0:T(8,128)(2,1)}, bf16[256,1024]{1,0:T(8,128)(2,1)S(1)}, u32[]{:S(2)}) copy-start(bf16[256,1024]{1,0:T(8,128)(2,1)S(1)} %pad_maximum_fusion.2.rows_c_ref.first_c_ref) | copy-start | bytes 1572868
  24.9 12.6 %collective-permute-start.3 = (bf16[256,1024]{1,0:T(8,128)(2,1)S(1)}, bf16[256,1024]{1,0:T(8,128)(2,1)S(1)}, u32[]{:S(2)}, u32[]{:S(2)}) collective-permute-start(bf16[256,1024]{1,0:T(8,128)(2,1)S(1)} %pad_maximum_fusion.2.rows_c_ref.first_c_ref), channel_id=1, source_target_pairs={{0,1},{1,0},{2,3},{3,2},{4,5},{5,4},{6,7},{7,6},{8,9},{9,8},{10,11... | collective-permute-start | bytes 1572872 | tf_op jit(solution)/shard_map/ppermute | solution.py:566
  54.8 14.0 %collective-permute-start.4 = (bf16[256,1024]{1,0:T(8,128)(2,1)}, bf16[256,1024]{1,0:T(8,128)(2,1)S(1)}, u32[]{:S(2)}, u32[]{:S(2)}) collective-permute-start(bf16[256,1024]{1,0:T(8,128)(2,1)} %get-tuple-element.63), channel_id=1, source_target_pairs={{0,2},{1,3},{2,0},{3,1},{4,6},{5,7},{6,4},{7,5},{8,10},{9,11},{10,... | collective-permute-start | bytes 1572872 | tf_op jit(solution)/shard_map/ppermute | solution.py:566
  56.1 14.0 %collective-permute-start.5 = (bf16[256,1024]{1,0:T(8,128)(2,1)}, bf16[256,1024]{1,0:T(8,128)(2,1)S(1)}, u32[]{:S(2)}, u32[]{:S(2)}) collective-permute-start(bf16[256,1024]{1,0:T(8,128)(2,1)} %get-tuple-element.65), channel_id=1, source_target_pairs={{0,1},{1,0},{2,3},{3,2},{4,5},{5,4},{6,7},{7,6},{8,9},{9,8},{10,11... | collective-permute-start | bytes 1572872 | tf_op jit(solution)/shard_map/ppermute | solution.py:566
  70.9 4.9 %copy-start.10 = (bf16[256,1024]{1,0:T(8,128)(2,1)S(1)}, bf16[256,1024]{1,0:T(8,128)(2,1)}, u32[]{:S(2)}) copy-start(bf16[256,1024]{1,0:T(8,128)(2,1)} %param.24) | copy-start | bytes 1572868
  73.7 10.9 %copy-start.28 = (f32[128,1024]{1,0:T(8,128)S(1)}, f32[128,1024]{1,0:T(8,128)}, u32[]{:S(2)}) copy-start(f32[128,1024]{1,0:T(8,128)} %get-tuple-element.66) | copy-start | bytes 1572868
  73.7 10.9 %copy-start.29 = (f32[128,1024]{1,0:T(8,128)S(1)}, f32[128,1024]{1,0:T(8,128)}, u32[]{:S(2)}) copy-start(f32[128,1024]{1,0:T(8,128)} %get-tuple-element.68) | copy-start | bytes 1572868
  73.7 9.5 %collective-permute-start.6 = (bf16[128,1024]{1,0:T(8,128)(2,1)}, bf16[128,1024]{1,0:T(8,128)(2,1)S(1)}, u32[]{:S(2)}, u32[]{:S(2)}) collective-permute-start(bf16[128,1024]{1,0:T(8,128)(2,1)} %get-tuple-element.67), channel_id=1, source_target_pairs={{0,1},{1,0},{2,3},{3,2},{4,5},{5,4},{6,7},{7,6},{8,9},{9,8},{10,11... | collective-permute-start | bytes 786440 | tf_op jit(solution)/shard_map/ppermute | solution.py:566
  75.2 9.5 %collective-permute-start.9 = (bf16[128,1024]{1,0:T(8,128)(2,1)}, bf16[128,1024]{1,0:T(8,128)(2,1)S(1)}, u32[]{:S(2)}, u32[]{:S(2)}) collective-permute-start(bf16[128,1024]{1,0:T(8,128)(2,1)} %get-tuple-element.69), channel_id=1, source_target_pairs={{0,2},{1,3},{2,0},{3,1},{4,6},{5,7},{6,4},{7,5},{8,10},{9,11},{10,... | collective-permute-start | bytes 786440 | tf_op jit(solution)/shard_map/ppermute | solution.py:566
  75.7 14.5 %collective-permute-start.14 = (bf16[128,1024]{1,0:T(8,128)(2,1)S(1)}, bf16[128,1024]{1,0:T(8,128)(2,1)S(1)}, u32[]{:S(2)}, u32[]{:S(2)}) collective-permute-start(bf16[128,1024]{1,0:T(8,128)(2,1)S(1)} %get-tuple-element.148), channel_id=1, source_target_pairs={{0,2},{1,3},{2,0},{3,1},{4,6},{5,7},{6,4},{7,5},{8,10},{9,11},{10,... | collective-permute-start | bytes 786440 | tf_op jit(solution)/shard_map/ppermute | solution.py:566
  77.3 11.5 %collective-permute-start.12 = (bf16[128,1024]{1,0:T(8,128)(2,1)S(1)}, bf16[128,1024]{1,0:T(8,128)(2,1)S(1)}, u32[]{:S(2)}, u32[]{:S(2)}) collective-permute-start(bf16[128,1024]{1,0:T(8,128)(2,1)S(1)} %get-tuple-element.149), channel_id=1, source_target_pairs={{0,1},{1,0},{2,3},{3,2},{4,5},{5,4},{6,7},{7,6},{8,9},{9,8},{10,11... | collective-permute-start | bytes 786440 | tf_op jit(solution)/shard_map/ppermute | solution.py:566
  85.5 9.3 %collective-permute-start.7 = (bf16[128,1024]{1,0:T(8,128)(2,1)S(1)}, bf16[128,1024]{1,0:T(8,128)(2,1)S(1)}, u32[]{:S(2)}, u32[]{:S(2)}) collective-permute-start(bf16[128,1024]{1,0:T(8,128)(2,1)S(1)} %get-tuple-element.161), channel_id=1, source_target_pairs={{0,1},{1,0},{2,3},{3,2},{4,5},{5,4},{6,7},{7,6},{8,9},{9,8},{10,11... | collective-permute-start | bytes 786440 | tf_op jit(solution)/shard_map/ppermute | solution.py:566
  86.1 9.8 %collective-permute-start.10 = (bf16[128,1024]{1,0:T(8,128)(2,1)S(1)}, bf16[128,1024]{1,0:T(8,128)(2,1)S(1)}, u32[]{:S(2)}, u32[]{:S(2)}) collective-permute-start(bf16[128,1024]{1,0:T(8,128)(2,1)S(1)} %get-tuple-element.160), channel_id=1, source_target_pairs={{0,2},{1,3},{2,0},{3,1},{4,6},{5,7},{6,4},{7,5},{8,10},{9,11},{10,... | collective-permute-start | bytes 786440 | tf_op jit(solution)/shard_map/ppermute | solution.py:566
  88.8 28.2 %copy-start.11 = (bf16[256,1024]{1,0:T(8,128)(2,1)}, bf16[256,1024]{1,0:T(8,128)(2,1)S(1)}, u32[]{:S(2)}) copy-start(bf16[256,1024]{1,0:T(8,128)(2,1)S(1)} %pad_maximum_fusion.5.cot_a_ref.second_a_ref) | copy-start | bytes 1572868
  88.8 18.3 %collective-permute-start.13 = (bf16[256,1024]{1,0:T(8,128)(2,1)S(1)}, bf16[256,1024]{1,0:T(8,128)(2,1)S(1)}, u32[]{:S(2)}, u32[]{:S(2)}) collective-permute-start(bf16[256,1024]{1,0:T(8,128)(2,1)S(1)} %pad_maximum_fusion.5.cot_a_ref.second_a_ref), channel_id=1, source_target_pairs={{0,2},{1,3},{2,0},{3,1},{4,6},{5,7},{6,4},{7,5},{8,10},{9,11},{10,... | collective-permute-start | bytes 1572872 | tf_op jit(solution)/shard_map/ppermute | solution.py:566
  90.3 16.8 %copy-start.12 = (bf16[256,1024]{1,0:T(8,128)(2,1)}, bf16[256,1024]{1,0:T(8,128)(2,1)S(1)}, u32[]{:S(2)}) copy-start(bf16[256,1024]{1,0:T(8,128)(2,1)S(1)} %pad_maximum_fusion.6.cot_c_ref.second_c_ref) | copy-start | bytes 1572868
  90.3 16.8 %collective-permute-start.15 = (bf16[256,1024]{1,0:T(8,128)(2,1)S(1)}, bf16[256,1024]{1,0:T(8,128)(2,1)S(1)}, u32[]{:S(2)}, u32[]{:S(2)}) collective-permute-start(bf16[256,1024]{1,0:T(8,128)(2,1)S(1)} %pad_maximum_fusion.6.cot_c_ref.second_c_ref), channel_id=1, source_target_pairs={{0,1},{1,0},{2,3},{3,2},{4,5},{5,4},{6,7},{7,6},{8,9},{9,8},{10,11... | collective-permute-start | bytes 1572872 | tf_op jit(solution)/shard_map/ppermute | solution.py:566
  94.8 12.3 %copy-start.13 = (bf16[256,1024]{1,0:T(8,128)(2,1)}, bf16[256,1024]{1,0:T(8,128)(2,1)S(1)}, u32[]{:S(2)}) copy-start(bf16[256,1024]{1,0:T(8,128)(2,1)S(1)} %pad_maximum_fusion.3.rows_a_ref.first_a_ref) | copy-start | bytes 1572868
  94.8 21.4 %collective-permute-start.8 = (bf16[256,1024]{1,0:T(8,128)(2,1)S(1)}, bf16[256,1024]{1,0:T(8,128)(2,1)S(1)}, u32[]{:S(2)}, u32[]{:S(2)}) collective-permute-start(bf16[256,1024]{1,0:T(8,128)(2,1)S(1)} %pad_maximum_fusion.3.rows_a_ref.first_a_ref), channel_id=1, source_target_pairs={{0,2},{1,3},{2,0},{3,1},{4,6},{5,7},{6,4},{7,5},{8,10},{9,11},{10,... | collective-permute-start | bytes 1572872 | tf_op jit(solution)/shard_map/ppermute | solution.py:566
  95.9 20.3 %copy-start.14 = (bf16[256,1024]{1,0:T(8,128)(2,1)}, bf16[256,1024]{1,0:T(8,128)(2,1)S(1)}, u32[]{:S(2)}) copy-start(bf16[256,1024]{1,0:T(8,128)(2,1)S(1)} %pad_maximum_fusion.4.rows_c_ref.first_c_ref) | copy-start | bytes 1572868
  95.9 21.1 %collective-permute-start.11 = (bf16[256,1024]{1,0:T(8,128)(2,1)S(1)}, bf16[256,1024]{1,0:T(8,128)(2,1)}, u32[]{:S(2)}, u32[]{:S(2)}) collective-permute-start(bf16[256,1024]{1,0:T(8,128)(2,1)S(1)} %pad_maximum_fusion.4.rows_c_ref.first_c_ref), channel_id=1, source_target_pairs={{0,1},{1,0},{2,3},{3,2},{4,5},{5,4},{6,7},{7,6},{8,9},{9,8},{10,11... | collective-permute-start | bytes 1572872 | tf_op jit(solution)/shard_map/ppermute | solution.py:566
  107.1 9.1 %copy-start.22 = (bf16[256,1024]{1,0:T(8,128)(2,1)}, bf16[256,1024]{1,0:T(8,128)(2,1)S(1)}, u32[]{:S(2)}) copy-start(bf16[256,1024]{1,0:T(8,128)(2,1)S(1)} %collective-permute-done.13.cot_b_ref.second_b_ref) | copy-start | bytes 1572868
  107.1 9.1 %copy-start.24 = (bf16[256,1024]{1,0:T(8,128)(2,1)}, bf16[256,1024]{1,0:T(8,128)(2,1)S(1)}, u32[]{:S(2)}) copy-start(bf16[256,1024]{1,0:T(8,128)(2,1)S(1)} %collective-permute-done.15.cot_d_ref.second_d_ref) | copy-start | bytes 1572868
  151.6 130.4 %reduce-scatter.5.cloned.1.call-start = ((), (), s32[]{:S(2)}) async-start(), calls=%async_computation.5 | async-start | bytes 1769472 | tf_op jit(solution)/shard_map/reduce_scatter | solution.py:688
  151.7 12.2 %collective-permute-start.16 = (bf16[256,1024]{1,0:T(8,128)(2,1)}, bf16[256,1024]{1,0:T(8,128)(2,1)S(1)}, u32[]{:S(2)}, u32[]{:S(2)}) collective-permute-start(bf16[256,1024]{1,0:T(8,128)(2,1)} %get-tuple-element.72), channel_id=1, source_target_pairs={{0,2},{1,3},{2,0},{3,1},{4,6},{5,7},{6,4},{7,5},{8,10},{9,11},{10,... | collective-permute-start | bytes 1572872 | tf_op jit(solution)/shard_map/ppermute | solution.py:566
  152.6 11.9 %collective-permute-start.17 = (bf16[256,1024]{1,0:T(8,128)(2,1)S(1)}, bf16[256,1024]{1,0:T(8,128)(2,1)S(1)}, u32[]{:S(2)}, u32[]{:S(2)}) collective-permute-start(bf16[256,1024]{1,0:T(8,128)(2,1)S(1)} %copy-done.36), channel_id=1, source_target_pairs={{0,1},{1,0},{2,3},{3,2},{4,5},{5,4},{6,7},{7,6},{8,9},{9,8},{10,11... | collective-permute-start | bytes 1572872 | tf_op jit(solution)/shard_map/ppermute | solution.py:566
  168.1 8.5 %copy-start.17 = (f32[128,1024]{1,0:T(8,128)S(1)}, f32[128,1024]{1,0:T(8,128)}, u32[]{:S(2)}) copy-start(f32[128,1024]{1,0:T(8,128)} %get-tuple-element.76) | copy-start | bytes 1572868
  168.1 8.5 %copy-start.18 = (f32[128,1024]{1,0:T(8,128)S(1)}, f32[128,1024]{1,0:T(8,128)}, u32[]{:S(2)}) copy-start(f32[128,1024]{1,0:T(8,128)} %get-tuple-element.78) | copy-start | bytes 1572868
  168.1 6.6 %collective-permute-start.18 = (bf16[128,1024]{1,0:T(8,128)(2,1)}, bf16[128,1024]{1,0:T(8,128)(2,1)S(1)}, u32[]{:S(2)}, u32[]{:S(2)}) collective-permute-start(bf16[128,1024]{1,0:T(8,128)(2,1)} %get-tuple-element.77), channel_id=1, source_target_pairs={{0,1},{1,0},{2,3},{3,2},{4,5},{5,4},{6,7},{7,6},{8,9},{9,8},{10,11... | collective-permute-start | bytes 786440 | tf_op jit(solution)/shard_map/ppermute | solution.py:566
  168.5 6.6 %collective-permute-start.21 = (bf16[128,1024]{1,0:T(8,128)(2,1)}, bf16[128,1024]{1,0:T(8,128)(2,1)S(1)}, u32[]{:S(2)}, u32[]{:S(2)}) collective-permute-start(bf16[128,1024]{1,0:T(8,128)(2,1)} %get-tuple-element.79), channel_id=1, source_target_pairs={{0,2},{1,3},{2,0},{3,1},{4,6},{5,7},{6,4},{7,5},{8,10},{9,11},{10,... | collective-permute-start | bytes 786440 | tf_op jit(solution)/shard_map/ppermute | solution.py:566
  178.0 6.7 %collective-permute-start.19 = (bf16[128,1024]{1,0:T(8,128)(2,1)S(1)}, bf16[128,1024]{1,0:T(8,128)(2,1)S(1)}, u32[]{:S(2)}, u32[]{:S(2)}) collective-permute-start(bf16[128,1024]{1,0:T(8,128)(2,1)S(1)} %get-tuple-element.146), channel_id=1, source_target_pairs={{0,1},{1,0},{2,3},{3,2},{4,5},{5,4},{6,7},{7,6},{8,9},{9,8},{10,11... | collective-permute-start | bytes 786440 | tf_op jit(solution)/shard_map/ppermute | solution.py:566
  179.7 9.1 %collective-permute-start.22 = (bf16[128,1024]{1,0:T(8,128)(2,1)S(1)}, bf16[128,1024]{1,0:T(8,128)(2,1)S(1)}, u32[]{:S(2)}, u32[]{:S(2)}) collective-permute-start(bf16[128,1024]{1,0:T(8,128)(2,1)S(1)} %get-tuple-element.132), channel_id=1, source_target_pairs={{0,2},{1,3},{2,0},{3,1},{4,6},{5,7},{6,4},{7,5},{8,10},{9,11},{10,... | collective-permute-start | bytes 786440 | tf_op jit(solution)/shard_map/ppermute | solution.py:566
  184.7 13.4 %copy-start.1 = (bf16[256,1024]{1,0:T(8,128)(2,1)}, bf16[256,1024]{1,0:T(8,128)(2,1)S(1)}, u32[]{:S(2)}) copy-start(bf16[256,1024]{1,0:T(8,128)(2,1)S(1)} %pad_maximum_fusion.7.refs_0_.grad_a_ref.second_a_ref) | copy-start | bytes 1572868
  184.7 11.9 %collective-permute-start.20 = (bf16[256,1024]{1,0:T(8,128)(2,1)S(1)}, bf16[256,1024]{1,0:T(8,128)(2,1)S(1)}, u32[]{:S(2)}, u32[]{:S(2)}) collective-permute-start(bf16[256,1024]{1,0:T(8,128)(2,1)S(1)} %pad_maximum_fusion.7.refs_0_.grad_a_ref.second_a_ref), channel_id=1, source_target_pairs={{0,2},{1,3},{2,0},{3,1},{4,6},{5,7},{6,4},{7,5},{8,10},{9,11},{10,... | collective-permute-start | bytes 1572872 | tf_op jit(solution)/shard_map/ppermute | solution.py:566
  188.8 9.3 %copy-start.2 = (bf16[256,1024]{1,0:T(8,128)(2,1)}, bf16[256,1024]{1,0:T(8,128)(2,1)S(1)}, u32[]{:S(2)}) copy-start(bf16[256,1024]{1,0:T(8,128)(2,1)S(1)} %pad_maximum_fusion.8.refs_2_.grad_c_ref.second_c_ref) | copy-start | bytes 1572868
  188.8 9.2 %collective-permute-start.23 = (bf16[256,1024]{1,0:T(8,128)(2,1)S(1)}, bf16[256,1024]{1,0:T(8,128)(2,1)S(1)}, u32[]{:S(2)}, u32[]{:S(2)}) collective-permute-start(bf16[256,1024]{1,0:T(8,128)(2,1)S(1)} %pad_maximum_fusion.8.refs_2_.grad_c_ref.second_c_ref), channel_id=1, source_target_pairs={{0,1},{1,0},{2,3},{3,2},{4,5},{5,4},{6,7},{7,6},{8,9},{9,8},{10,11... | collective-permute-start | bytes 1572872 | tf_op jit(solution)/shard_map/ppermute | solution.py:566
  218.5 7.2 %copy-start.31 = (f32[2,64,128]{2,1,0:T(8,128)S(1)}, f32[2,64,128]{2,1,0:T(8,128)}, u32[]{:S(2)}) copy-start(f32[2,64,128]{2,1,0:T(8,128)} %get-tuple-element.110) | copy-start | bytes 196612
  218.5 18.9 %copy-start.35 = (bf16[256,1024]{1,0:T(8,128)(2,1)S(1)}, bf16[256,1024]{1,0:T(8,128)(2,1)}, u32[]{:S(2)}) copy-start(bf16[256,1024]{1,0:T(8,128)(2,1)} %get-tuple-element.100) | copy-start | bytes 1572868
  218.5 20.0 %copy-start.34 = (bf16[256,1024]{1,0:T(8,128)(2,1)S(1)}, bf16[256,1024]{1,0:T(8,128)(2,1)}, u32[]{:S(2)}) copy-start(bf16[256,1024]{1,0:T(8,128)(2,1)} %get-tuple-element.102) | copy-start | bytes 1572868
  224.7 25.4 %collective-permute-start.24 = (bf16[256,1024]{1,0:T(8,128)(2,1)}, bf16[256,1024]{1,0:T(8,128)(2,1)}, u32[]{:S(2)}, u32[]{:S(2)}) collective-permute-start(bf16[256,1024]{1,0:T(8,128)(2,1)} %get-tuple-element.81), channel_id=1, source_target_pairs={{0,2},{1,3},{2,0},{3,1},{4,6},{5,7},{6,4},{7,5},{8,10},{9,11},{10,... | collective-permute-start | bytes 1572872 | tf_op jit(solution)/shard_map/ppermute | solution.py:566
  225.7 24.4 %collective-permute-start.25 = (bf16[256,1024]{1,0:T(8,128)(2,1)}, bf16[256,1024]{1,0:T(8,128)(2,1)}, u32[]{:S(2)}, u32[]{:S(2)}) collective-permute-start(bf16[256,1024]{1,0:T(8,128)(2,1)} %get-tuple-element.83), channel_id=1, source_target_pairs={{0,1},{1,0},{2,3},{3,2},{4,5},{5,4},{6,7},{7,6},{8,9},{9,8},{10,11... | collective-permute-start | bytes 1572872 | tf_op jit(solution)/shard_map/ppermute | solution.py:566
  225.9 1.2 collective-permute-start.32
  227.1 3.7 %collective-permute-start.33 = (f32[2176]{0:T(1024)S(1)}, f32[2176]{0:T(1024)S(1)}, u32[]{:S(2)}, u32[]{:S(2)}) collective-permute-start(f32[2176]{0:T(1024)S(1)} %add.190), channel_id=1, source_target_pairs={{0,8},{4,12},{8,0},{12,4},{16,24},{20,28},{24,16},{28,20},{1,9},{5... | collective-permute-start | bytes 26120 | tf_op jit(solution)/shard_map/ppermute | solution.py:566
  230.8 4.6 %collective-permute-start.34 = (f32[2176]{0:T(1024)S(1)}, f32[2176]{0:T(1024)S(1)}, u32[]{:S(2)}, u32[]{:S(2)}) collective-permute-start(f32[2176]{0:T(1024)S(1)} %add.191), channel_id=1, source_target_pairs={{0,16},{4,20},{8,24},{12,28},{16,0},{20,4},{24,8},{28,12},{1,17},{... | collective-permute-start | bytes 26120 | tf_op jit(solution)/shard_map/ppermute | solution.py:566
  235.4 3.8 %collective-permute-start.35 = (f32[2176]{0:T(1024)S(1)}, f32[2176]{0:T(1024)S(1)}, u32[]{:S(2)}, u32[]{:S(2)}) collective-permute-start(f32[2176]{0:T(1024)S(1)} %add.192), channel_id=1, source_target_pairs={{0,1},{1,0},{2,3},{3,2},{4,5},{5,4},{6,7},{7,6},{8,9},{9,8},{10,11... | collective-permute-start | bytes 26120 | tf_op jit(solution)/shard_map/ppermute | solution.py:566
  237.4 17.5 %collective-permute-start.28 = (bf16[256,1024]{1,0:T(8,128)(2,1)S(1)}, bf16[256,1024]{1,0:T(8,128)(2,1)}, u32[]{:S(2)}, u32[]{:S(2)}) collective-permute-start(bf16[256,1024]{1,0:T(8,128)(2,1)S(1)} %copy-done.35), channel_id=1, source_target_pairs={{0,2},{1,3},{2,0},{3,1},{4,6},{5,7},{6,4},{7,5},{8,10},{9,11},{10,... | collective-permute-start | bytes 1572872 | tf_op jit(solution)/shard_map/ppermute | solution.py:566
  238.5 16.4 %collective-permute-start.29 = (bf16[256,1024]{1,0:T(8,128)(2,1)S(1)}, bf16[256,1024]{1,0:T(8,128)(2,1)}, u32[]{:S(2)}, u32[]{:S(2)}) collective-permute-start(bf16[256,1024]{1,0:T(8,128)(2,1)S(1)} %copy-done.34), channel_id=1, source_target_pairs={{0,1},{1,0},{2,3},{3,2},{4,5},{5,4},{6,7},{7,6},{8,9},{9,8},{10,11... | collective-permute-start | bytes 1572872 | tf_op jit(solution)/shard_map/ppermute | solution.py:566
  239.2 10.3 %collective-permute-start.36 = (f32[2176]{0:T(1024)S(1)}, f32[2176]{0:T(1024)S(1)}, u32[]{:S(2)}, u32[]{:S(2)}) collective-permute-start(f32[2176]{0:T(1024)S(1)} %add.193), channel_id=1, source_target_pairs={{0,2},{1,3},{2,0},{3,1},{4,6},{5,7},{6,4},{7,5},{8,10},{9,11},{10,... | collective-permute-start | bytes 26120 | tf_op jit(solution)/shard_map/ppermute | solution.py:566
  252.9 8.7 %collective-permute-start.26 = (bf16[128,1024]{1,0:T(8,128)(2,1)}, bf16[128,1024]{1,0:T(8,128)(2,1)S(1)}, u32[]{:S(2)}, u32[]{:S(2)}) collective-permute-start(bf16[128,1024]{1,0:T(8,128)(2,1)} %get-tuple-element.85), channel_id=1, source_target_pairs={{0,1},{1,0},{2,3},{3,2},{4,5},{5,4},{6,7},{7,6},{8,9},{9,8},{10,11... | collective-permute-start | bytes 786440 | tf_op jit(solution)/shard_map/ppermute | solution.py:566
  253.8 8.5 %collective-permute-start.27 = (bf16[128,1024]{1,0:T(8,128)(2,1)}, bf16[128,1024]{1,0:T(8,128)(2,1)S(1)}, u32[]{:S(2)}, u32[]{:S(2)}) collective-permute-start(bf16[128,1024]{1,0:T(8,128)(2,1)} %get-tuple-element.87), channel_id=1, source_target_pairs={{0,2},{1,3},{2,0},{3,1},{4,6},{5,7},{6,4},{7,5},{8,10},{9,11},{10,... | collective-permute-start | bytes 786440 | tf_op jit(solution)/shard_map/ppermute | solution.py:566
  254.9 6.7 %copy-start.23 = (f32[128,1024]{1,0:T(8,128)S(1)}, f32[128,1024]{1,0:T(8,128)}, u32[]{:S(2)}) copy-start(f32[128,1024]{1,0:T(8,128)} %get-tuple-element.84) | copy-start | bytes 1572868
  254.9 7.4 %copy-start.21 = (f32[128,1024]{1,0:T(8,128)S(1)}, f32[128,1024]{1,0:T(8,128)}, u32[]{:S(2)}) copy-start(f32[128,1024]{1,0:T(8,128)} %get-tuple-element.86) | copy-start | bytes 1572868
  257.7 7.4 %collective-permute-start.30 = (bf16[128,1024]{1,0:T(8,128)(2,1)}, bf16[128,1024]{1,0:T(8,128)(2,1)S(1)}, u32[]{:S(2)}, u32[]{:S(2)}) collective-permute-start(bf16[128,1024]{1,0:T(8,128)(2,1)} %get-tuple-element.104), channel_id=1, source_target_pairs={{0,1},{1,0},{2,3},{3,2},{4,5},{5,4},{6,7},{7,6},{8,9},{9,8},{10,11... | collective-permute-start | bytes 786440 | tf_op jit(solution)/shard_map/ppermute | solution.py:566
  259.4 6.6 %collective-permute-start.31 = (bf16[128,1024]{1,0:T(8,128)(2,1)}, bf16[128,1024]{1,0:T(8,128)(2,1)S(1)}, u32[]{:S(2)}, u32[]{:S(2)}) collective-permute-start(bf16[128,1024]{1,0:T(8,128)(2,1)} %get-tuple-element.106), channel_id=1, source_target_pairs={{0,2},{1,3},{2,0},{3,1},{4,6},{5,7},{6,4},{7,5},{8,10},{9,11},{10,... | collective-permute-start | bytes 786440 | tf_op jit(solution)/shard_map/ppermute | solution.py:566
  (18 other events, 36.2 us)
Sparse Core Ops, SparseCore 0:
  10.2 27.7 all-gather.2
  39.7 70.8 all-gather.4
  151.7 74.6 reduce-scatter.2
  250.2 31.7 reduce-scatter.4
where the time goes:
time: 299 us; the launch traced here: 294 us
  waiting for transfers between devices  117 us (39%)
  Pallas kernels  94.3 us (32%)
  starting transfers between devices  37.7 us (13%)
  between operations  17.3 us (6%)
  local copies, waits for them, and re-layouts  14.7 us (5%)
  other arithmetic  12.7 us (4%)
    ppermute x37, waiting for transfers between devices, swap(): return lax.ppermute(value, axis, [(i, i ^ bit) for i in range(size)])  104 us
    pallas_call x7, Pallas kernels, call_kernel(): pl.pallas_call(kernel, out_shape=[jax.ShapeDtypeStruct(*shape) for shape...  66 us
    ppermute x37, starting transfers between devices, swap(): return lax.ppermute(value, axis, [(i, i ^ bit) for i in range(size)])  37.5 us
    pallas_call x2, Pallas kernels, weight_parts(): pl.pallas_call(partial(weights_kernel, first_tiles), grid=(columns // til...  22 us
    reduce_scatter x1, waiting for transfers between devices, on_device(): lax.psum_scatter(later(attention_part, grad_feedfwd), 'dp', scatter_dimen...  12.2 us
    unnamed x86, local copies, waits for them, and re-layouts  8.11 us
    pallas_call x1, Pallas kernels, down_parts_of(): pl.pallas_call(down_kernel, grid=(1,), out_shape=[jax.ShapeDtypeStruct((q...  6.26 us
  transfers between devices with their start and end apart: 41, of which 32 were waited for; matrix products, arithmetic and copies ran while one was open for 5% of the time, Pallas kernels for 20%

commit v1 on v0

--- a/solution.py
+++ b/solution.py
@@ -18,12 +18,12 @@
 SHORTEST = 204
 TILE = 256
 LOG2E = math.log2(math.e)
-VMEM_LIMIT = 56 * 2**20
+MIB = 2**20
 HEAVY, LIGHT = 16 * 10**9, 10**9
 BFLOAT, SINGLE = jnp.bfloat16, jnp.float32
 
 
-def call_kernel(kernel, name, weight, shapes, scalars, arrays, scratch=(), earlier=(), **grid):
+def call_kernel(kernel, name, weight, limit, shapes, scalars, arrays, scratch=(), earlier=()):
     whole = pl.BlockSpec(memory_space=pltpu.VMEM)
     specs = [pl.BlockSpec(memory_space=pltpu.SMEM)] * len(scalars) + [whole] * len(arrays)
     return pl.pallas_call(
@@ -32,7 +32,7 @@
         in_specs=specs + [pl.BlockSpec(memory_space=pl.ANY)] * len(earlier),
         out_specs=[whole] * len(shapes),
         scratch_shapes=[pltpu.VMEM(*shape) for shape in scratch],
-        compiler_params=pltpu.CompilerParams(vmem_limit_bytes=VMEM_LIMIT),
+        compiler_params=pltpu.CompilerParams(vmem_limit_bytes=limit * MIB),
         cost_estimate=pl.CostEstimate(flops=weight, bytes_accessed=2**20, transcendentals=0),
         name=name,
     )(*scalars, *arrays, *earlier)
@@ -217,7 +217,7 @@
     ]
     arrays = (*quarters, weight, gains, segments)
     outs = call_kernel(
-        partial(attend_kernel, sizes), "attend", HEAVY, shapes, (place,), arrays, scratch
+        partial(attend_kernel, sizes), "attend", HEAVY, 56, shapes, (place,), arrays, scratch
     )
     return outs[:11], outs[11], outs[12:]
 
@@ -246,6 +246,7 @@
     cosine_ref,
     sine_ref,
     begin_ref,
+    earlier_ref,
     out_ref,
     head_gain_ref,
     row_gain_ref,
@@ -337,7 +338,7 @@
     row_gain_ref[...] = row_gain
 
 
-def attend_back(sizes, place, grads, quarters, weight, gains, saved):
+def attend_back(sizes, place, grads, quarters, weight, gains, saved, earlier):
     query_heads, key_heads, head_dim = sizes
     heads = query_heads + key_heads
     columns = (heads + key_heads) * head_dim
@@ -360,8 +361,9 @@
         ((LEN, TILE), SINGLE),
     ]
     arrays = (*grads, *quarters, weight, gains, *saved)
+    kernel = partial(attend_back_kernel, sizes)
     outs = call_kernel(
-        partial(attend_back_kernel, sizes), "attend_back", HEAVY, shapes, (place,), arrays, scratch
+        kernel, "attend_back", HEAVY, 56, shapes, (place,), arrays, scratch, (earlier,)
     )
     return outs[0], outs[1], outs[2], outs[3:]
 
@@ -377,50 +379,95 @@
     cot_d_ref,
     weight_ref,
     hidden_ref,
-    grad_ref,
+    out_ref,
     part_a_ref,
     part_b_ref,
     part_c_ref,
     part_d_ref,
-    gate_up,
-    grad_hidden,
+    rows_turned,
+    cot_turned,
+    gate_up_grad,
+    total,
 ):
-    hidden_cols = hidden_ref.shape[1]
+    step = pl.program_id(0)
     quarter = rows_a_ref.shape[0]
-    step = 384 if hidden_cols % 384 == 0 else hidden_cols
-    quarters = (
-        (rows_a_ref, cot_a_ref, part_a_ref),
-        (rows_b_ref, cot_b_ref, part_b_ref),
-        (rows_c_ref, cot_c_ref, part_c_ref),
-        (rows_d_ref, cot_d_ref, part_d_ref),
-    )
-    for q, (rows_ref, cot_ref, part_ref) in enumerate(quarters):
-        tile, slot = slice(q * quarter, (q + 1) * quarter), q % 2
-        gate_up[slot] = dot(rows_ref[...], weight_ref[:, : 2 * hidden_cols])
-        grad_hidden[slot] = dot(cot_ref[...], weight_ref[:, 2 * hidden_cols :])
-        for first in range(0, hidden_cols, step):
-            cols = slice(first, first + step)
-            up_cols = slice(hidden_cols + first, hidden_cols + first + step)
-            gate_proj, upward = gate_up[slot, :, cols], gate_up[slot, :, up_cols]
-            grads = grad_hidden[slot, :, cols]
-            sigmoid = 1.0 / (1.0 + jnp.exp(-gate_proj))
-            active = gate_proj * sigmoid
-            hidden_ref[tile, cols] = (active * upward).astype(BFLOAT)
-            slope = sigmoid * (1.0 + gate_proj * (1.0 - sigmoid))
-            grad_ref[tile, cols] = (grads * upward * slope).astype(BFLOAT)
-            grad_ref[tile, up_cols] = (grads * active).astype(BFLOAT)
-        part_ref[...] = dot_last(grad_ref[tile, :], weight_ref[:, : 2 * hidden_cols]).astype(BFLOAT)
+    cols = hidden_ref.shape[1]
+    rows_refs = (rows_a_ref, rows_b_ref, rows_c_ref, rows_d_ref)
+    cot_refs = (cot_a_ref, cot_b_ref, cot_c_ref, cot_d_ref)
+    part_refs = (part_a_ref, part_b_ref, part_c_ref, part_d_ref)
+
+    @pl.when(step == 0)
+    def _():
+        for q in range(4):
+            rows_turned[:, q * quarter : (q + 1) * quarter] = rows_refs[q][...].T
+            cot_turned[:, q * quarter : (q + 1) * quarter] = cot_refs[q][...].T
+        total[...] = jnp.zeros(total.shape, SINGLE)
+
+    for q in range(4):
+        tile = slice(q * quarter, (q + 1) * quarter)
+        gate_up = dot(rows_refs[q][...], weight_ref[:, : 2 * cols])
+        gate_proj, upward = gate_up[:, :cols], gate_up[:, cols:]
+        grad_hidden = dot(cot_refs[q][...], weight_ref[:, 2 * cols :])
+        sigmoid = 0.5 * jnp.tanh(0.5 * gate_proj) + 0.5
+        active = gate_proj * sigmoid
+        hidden_ref[tile, :] = (active * upward).astype(BFLOAT)
+        slope = sigmoid + active * (1.0 - sigmoid)
+        gate_up_grad[tile, :cols] = (grad_hidden * upward * slope).astype(BFLOAT)
+        gate_up_grad[tile, cols:] = (grad_hidden * active).astype(BFLOAT)
+        total[tile, :] += dot_last(gate_up_grad[tile, :], weight_ref[:, : 2 * cols])
+    out_ref[:, : 2 * cols] = dot(rows_turned[...], gate_up_grad[...]).astype(BFLOAT)
+    out_ref[:, 2 * cols :] = dot(cot_turned[...], hidden_ref[...]).astype(BFLOAT)
+
+    @pl.when(step == pl.num_programs(0) - 1)
+    def _():
+        for q in range(4):
+            part_refs[q][...] = total[q * quarter : (q + 1) * quarter, :].astype(BFLOAT)
+
+
+def tile_of(hidden_cols):
+    return 384 if hidden_cols % 384 == 0 else hidden_cols
+
+
+def interleave(gate, up, down):
+    tile = tile_of(gate.shape[1])
+    pieces = []
+    for first in range(0, gate.shape[1], tile):
+        pieces += [value[:, first : first + tile] for value in (gate, up, down)]
+    return jnp.concatenate(pieces, axis=1)
+
+
+def part_of(value, kind):
+    tile = tile_of(value.shape[1] // 3)
+    starts = range(kind * tile, value.shape[1], 3 * tile)
+    return jnp.concatenate([value[:, first : first + tile] for first in starts], axis=1)
 
 
 def feedfwd(quarters, cots, weight):
     quarter, width = quarters[0].shape
     hidden_cols = weight.shape[1] // 3
-    shapes = [((LEN, hidden_cols), BFLOAT), ((LEN, 2 * hidden_cols), BFLOAT)]
-    shapes += [((quarter, width), BFLOAT)] * 4
-    scratch = [((2, quarter, 2 * hidden_cols), SINGLE), ((2, quarter, hidden_cols), SINGLE)]
-    outs = call_kernel(
-        feedfwd_kernel, "feedfwd", HEAVY, shapes, (), (*quarters, *cots, weight), scratch
-    )
+    cols = tile_of(hidden_cols)
+    whole = pl.BlockSpec((quarter, width), lambda j: (0, 0))
+    block = pl.BlockSpec((width, 3 * cols), lambda j: (0, j))
+    outs = pl.pallas_call(
+        feedfwd_kernel,
+        grid=(hidden_cols // cols,),
+        out_shape=[
+            jax.ShapeDtypeStruct((LEN, hidden_cols), BFLOAT),
+            jax.ShapeDtypeStruct((width, 3 * hidden_cols), BFLOAT),
+        ]
+        + [jax.ShapeDtypeStruct((quarter, width), BFLOAT)] * 4,
+        in_specs=[whole] * 8 + [block],
+        out_specs=[pl.BlockSpec((LEN, cols), lambda j: (0, j)), block] + [whole] * 4,
+        scratch_shapes=[
+            pltpu.VMEM((width, LEN), BFLOAT),
+            pltpu.VMEM((width, LEN), BFLOAT),
+            pltpu.VMEM((LEN, 2 * cols), BFLOAT),
+            pltpu.VMEM((LEN, width), SINGLE),
+        ],
+        compiler_params=pltpu.CompilerParams(vmem_limit_bytes=56 * MIB),
+        cost_estimate=pl.CostEstimate(flops=HEAVY, bytes_accessed=2**20, transcendentals=0),
+        name="feedfwd",
+    )(*quarters, *cots, weight)
     return outs[0], outs[1], outs[2:]
 
 
@@ -436,6 +483,7 @@
     second_d_ref,
     first_grad_ref,
     second_grad_ref,
+    earlier_ref,
     out_ref,
     turned_ref,
 ):
@@ -463,10 +511,10 @@
         out_ref[...] = dot(turned_ref[...], second_grad_ref[...]).astype(BFLOAT)
 
 
-def weight_parts(firsts, first_grad, seconds, second_grad):
+def weight_parts(firsts, first_grad, seconds, second_grad, earlier):
     first_cols, second_cols = first_grad.shape[1], second_grad.shape[1]
     quarter, width = firsts[0].shape
-    tiles = [t for t in (1152, 256, 128) if first_cols % t == 0 and second_cols % t == 0]
+    tiles = [t for t in (256, 128) if first_cols % t == 0 and second_cols % t == 0]
     if not tiles:
         sums = []
         for lefts, right in ((firsts, first_grad), (seconds, second_grad)):
@@ -484,13 +532,13 @@
         partial(weights_kernel, first_tiles),
         grid=(columns // tile,),
         out_shape=jax.ShapeDtypeStruct((width, columns), BFLOAT),
-        in_specs=[whole] * 8 + [first_spec, second_spec],
+        in_specs=[whole] * 8 + [first_spec, second_spec, pl.BlockSpec(memory_space=pl.ANY)],
         out_specs=pl.BlockSpec((width, tile), lambda j: (0, j)),
         scratch_shapes=[pltpu.VMEM((width, LEN), BFLOAT)],
-        compiler_params=pltpu.CompilerParams(vmem_limit_bytes=VMEM_LIMIT),
+        compiler_params=pltpu.CompilerParams(vmem_limit_bytes=56 * MIB),
         cost_estimate=pl.CostEstimate(flops=LIGHT, bytes_accessed=2**20, transcendentals=0),
         name="weight_parts",
-    )(*firsts, *seconds, first_grad, second_grad)
+    )(*firsts, *seconds, first_grad, second_grad, earlier)
 
 
 def pair_sum_kernel(stay_a_ref, got_a_ref, stay_b_ref, got_b_ref, *refs):
@@ -507,54 +555,98 @@
     rows, width = stays[0].shape
     shapes = [((rows // 2, width), SINGLE if last else BFLOAT), ((rows // 2, width), BFLOAT)] * 2
     arrays = (stays[0], gots[0], stays[1], gots[1])
-    outs = call_kernel(
-        pair_sum_kernel, "pair_sum", LIGHT, shapes, (), arrays, earlier=earlier
-    )
+    outs = call_kernel(pair_sum_kernel, "pair_sum", LIGHT, 8, shapes, (), arrays, earlier=earlier)
     return outs[0::2], outs[1::2]
 
 
 def down_kernel(hidden_ref, weight_ref, *refs):
-    quarter = hidden_ref.shape[0] // 4
-    for q, part_ref in enumerate(refs[-4:]):
-        rows = hidden_ref[q * quarter : (q + 1) * quarter, :]
-        part_ref[...] = dot_last(rows, weight_ref[...]).astype(BFLOAT)
+    outs, total = refs[-5:-1], refs[-1]
+    step = pl.program_id(0)
+    product = dot_last(hidden_ref[...], weight_ref[...])
+
+    @pl.when(step == 0)
+    def _():
+        total[...] = product
+
+    @pl.when(step > 0)
+    def _():
+        total[...] += product
+
+    @pl.when(step == pl.num_programs(0) - 1)
+    def _():
+        quarter = total.shape[0] // 4
+        for q, part_ref in enumerate(outs):
+            part_ref[...] = total[q * quarter : (q + 1) * quarter, :].astype(BFLOAT)
 
 
 def down_parts_of(hidden, weight, earlier):
     hidden_cols = hidden.shape[1]
     quarter, width = LEN // 4, weight.shape[0]
-    if hidden_cols % 128:
-        down = weight[:, 2 * hidden_cols :]
+    cols = tile_of(hidden_cols)
+    if cols % 128:
+        down = part_of(weight, 2)
         return [
             dot_last(hidden[q * quarter : (q + 1) * quarter], down).astype(BFLOAT) for q in range(4)
         ]
     part = pl.BlockSpec((quarter, width), lambda i: (0, 0))
     return pl.pallas_call(
         down_kernel,
-        grid=(1,),
+        grid=(hidden_cols // cols,),
         out_shape=[jax.ShapeDtypeStruct((quarter, width), BFLOAT)] * 4,
         in_specs=[
-            pl.BlockSpec((LEN, hidden_cols), lambda i: (0, 0)),
-            pl.BlockSpec((width, hidden_cols), lambda i: (0, 2)),
+            pl.BlockSpec((LEN, cols), lambda i: (0, i)),
+            pl.BlockSpec((width, cols), lambda i: (0, 3 * i + 2)),
         ]
         + [pl.BlockSpec(memory_space=pl.ANY)] * len(earlier),
         out_specs=[part] * 4,
-        compiler_params=pltpu.CompilerParams(vmem_limit_bytes=VMEM_LIMIT),
+        scratch_shapes=[pltpu.VMEM((LEN, width), SINGLE)],
+        compiler_params=pltpu.CompilerParams(vmem_limit_bytes=56 * MIB),
         cost_estimate=pl.CostEstimate(flops=LIGHT, bytes_accessed=2**20, transcendentals=0),
         name="down_parts",
     )(hidden, weight, *earlier)
 
 
-def later(value, earlier):
+def split_kernel(value_ref, query_ref, key_ref, value_out_ref, out_ref):
+    first = 0
+    for ref in (query_ref, key_ref, value_out_ref):
+        ref[...] = value_ref[:, first : first + ref.shape[1]].astype(SINGLE)
+        first += ref.shape[1]
+    out_ref[...] = value_ref[:, first:].astype(SINGLE).T
+
+
+def split_weights(value, shapes):
+    kinds = [(shape, SINGLE) for shape in shapes]
+    return call_kernel(split_kernel, "split_weights", LIGHT, 56, kinds, (), (value,))
+
+
+def pack_kernel(query_ref, key_ref, value_ref, out_ref, packed_ref):
+    first = 0
+    for ref in (query_ref, key_ref, value_ref):
+        packed_ref[:, first : first + ref.shape[1]] = ref[...]
+        first += ref.shape[1]
+    packed_ref[:, first:] = out_ref[...].astype(SINGLE).T.astype(BFLOAT)
+
+
+def pack_weights(*values):
+    columns = sum(value.shape[1] for value in values[:3]) + values[3].shape[0]
+    kinds = [((values[0].shape[0], columns), BFLOAT)]
+    return call_kernel(pack_kernel, "pack_weights", LIGHT, 56, kinds, (), values)[0]
+
+
+def later(value, *earlier):
     anywhere = pl.BlockSpec(memory_space=pl.ANY)
     return pl.pallas_call(
         lambda *refs: None,
         out_shape=jax.ShapeDtypeStruct(value.shape, value.dtype),
-        in_specs=[anywhere, anywhere],
+        in_specs=[anywhere] * (1 + len(earlier)),
         out_specs=anywhere,
         input_output_aliases={0: 0},
         name="later",
-    )(value, earlier)
+    )(value, *earlier)
+
+
+def wait_aways(parts, *earlier):
+    return [later(part, *earlier) if q % 2 else part for q, part in enumerate(parts)]
 
 
 def rms_scale(values, gain):
@@ -637,7 +729,7 @@
                 last = step == len(tensor_bits) - 2
                 stays, aways = pair_sum(stays, gots, last, earlier)
                 earlier = ()
-        return [stay.astype(SINGLE) + got.astype(SINGLE) for stay, got in zip(stays, gots)]
+        return [stay.astype(SINGLE) + got.astype(SINGLE) for stay, got in zip(stays, gots)], stays
 
     def halves_of(value):
         return [value[:half_rows], value[half_rows:]]
@@ -646,49 +738,51 @@
     normed = rms_scale(token_values, attention_gain).astype(BFLOAT)
     gathered = rows_gather(halves_of(normed))
     attention_full = lax.all_gather(
-        jnp.concatenate([query_weight, key_weight, value_weight, out_weight.T], axis=1),
+        pack_weights(query_weight, key_weight, value_weight, out_weight),
         "dp",
         axis=0,
         tiled=True,
     )
     feedfwd_full = lax.all_gather(
-        jnp.concatenate([gate_weight, up_weight, down_weight.T], axis=1), "dp", axis=0, tiled=True
+        interleave(gate_weight, up_weight, down_weight.T), "dp", axis=0, tiled=True
     )
     cots = rows_gather(halves_of(cotangent))
 
-    hidden_cols = gate_weight.shape[1]
     query_cols, key_cols = query_weight.shape[1], key_weight.shape[1]
-    qkv_cols = query_cols + 2 * key_cols
     sizes = (query_cols // head_dim, key_cols // head_dim, head_dim)
     gains = jnp.concatenate([query_gain, key_gain])[None, :]
     saved, context, attended_parts = attend(
         sizes, place, gathered, attention_full, gains, segments[None, :]
     )
+    attended_parts = wait_aways(attended_parts, cots[1], cots[3])
     residuals, normed_two = [], []
-    for token_part, sum_part in zip(halves_of(token_values), rows_scatter(attended_parts)):
+    for token_part, sum_part in zip(halves_of(token_values), rows_scatter(attended_parts)[0]):
         residuals.append(token_part + sum_part)
         normed_two.append(rms_scale(residuals[-1], feedfwd_gain).astype(BFLOAT))
     gathered_two = rows_gather(normed_two)
 
-    hidden, gate_up_grad, two_parts = feedfwd(gathered_two, cots, feedfwd_full)
-    feedfwd_part = weight_parts(gathered_two, gate_up_grad, cots, hidden)
+    hidden, feedfwd_part, two_parts = feedfwd(gathered_two, cots, feedfwd_full)
     grad_feedfwd = lax.psum_scatter(feedfwd_part, "dp", scatter_dimension=0, tiled=True)
-    two_sums = rows_scatter(two_parts, (feedfwd_part,))
+    two_sums, _ = rows_scatter(two_parts)
     grad_residual, gain_two_part = [], 0.0
     for residual_part, sum_part, cot_part in zip(residuals, two_sums, halves_of(cotangent)):
         back, gain_part = rms_back(residual_part, feedfwd_gain, sum_part)
         grad_residual.append(cot_part.astype(SINGLE) + back)
         gain_two_part = gain_two_part + jnp.sum(gain_part, axis=0)
-    gathered_grad = rows_gather([part.astype(BFLOAT) for part in grad_residual])
+    grad_low = [part.astype(BFLOAT) for part in grad_residual]
+    down_parts = down_parts_of(hidden, feedfwd_full, grad_low)
+    gathered_grad = rows_gather(grad_low)
 
     qkv_grad, head_gains, row_gain, normed_parts = attend_back(
-        sizes, place, gathered_grad, gathered, attention_full, gains, saved
-    )
-    attention_part = weight_parts(gathered, qkv_grad, gathered_grad, context)
-    grad_attention = lax.psum_scatter(
-        later(attention_part, grad_feedfwd), "dp", scatter_dimension=0, tiled=True
-    )
-    normed_sums = rows_scatter(normed_parts)
+        sizes, place, gathered_grad, gathered, attention_full, gains, saved, down_parts[0]
+    )
+    down_sums, down_stays = rows_scatter(
+        wait_aways(down_parts, gathered_grad[1], gathered_grad[3])
+    )
+    attention_part = weight_parts(gathered, qkv_grad, gathered_grad, context, down_stays[0])
+    attention_part = later(attention_part, grad_feedfwd)
+    grad_attention = lax.psum_scatter(attention_part, "dp", scatter_dimension=0, tiled=True)
+    normed_sums, normed_stays = rows_scatter(normed_parts, (attention_part,))
     grad_tokens = []
     for token_part, sum_part, grad_part in zip(
         halves_of(token_values), normed_sums, grad_residual
@@ -696,26 +790,21 @@
         back, _ = rms_back(token_part, attention_gain, sum_part)
         grad_tokens.append((grad_part + back).astype(BFLOAT))
 
-    down_parts = down_parts_of(hidden, feedfwd_full, gathered_grad)
-    down_sums = rows_scatter(down_parts)
     block_out = [(res + part).astype(BFLOAT) for res, part in zip(residuals, down_sums)]
 
-    gain_sums = butterfly_sum(
-        jnp.concatenate(
-            [row_gain[0] / attention_gain, gain_two_part, *jnp.sum(head_gains, axis=2)]
-        )
-    )
-    grad_attention, grad_feedfwd = grad_attention.astype(SINGLE), grad_feedfwd.astype(SINGLE)
+    gain_parts = jnp.concatenate(
+        [row_gain[0] / attention_gain, gain_two_part, *jnp.sum(head_gains, axis=2)]
+    )
+    gain_sums = butterfly_sum(gain_parts + 0.0 * normed_stays[0][0, 0].astype(SINGLE))
+    grad_feedfwd = grad_feedfwd.astype(SINGLE)
+    shapes = [value.shape for value in (query_weight, key_weight, value_weight, out_weight)]
     return (
         jnp.concatenate(block_out, axis=0),
         jnp.concatenate(grad_tokens, axis=0),
-        grad_attention[:, :query_cols],
-        grad_attention[:, query_cols : query_cols + key_cols],
-        grad_attention[:, query_cols + key_cols : qkv_cols],
-        grad_attention[:, qkv_cols:].T,
-        grad_feedfwd[:, :hidden_cols],
-        grad_feedfwd[:, hidden_cols : 2 * hidden_cols],
-        grad_feedfwd[:, 2 * hidden_cols :].T,
+        *split_weights(grad_attention, shapes),
+        part_of(grad_feedfwd, 0),
+        part_of(grad_feedfwd, 1),
+        part_of(grad_feedfwd, 2).T,
         gain_sums[:width],
         gain_sums[width : 2 * width],
         gain_sums[2 * width : 2 * width + head_dim],

time: 299 us -> 266 us (0.89); the launches traced: 294 us -> 265 us
  waiting for transfers between devices: 117 us -> 91 us
  Pallas kernels: 94.3 us -> 84.1 us
  starting transfers between devices: 37.7 us -> 42.7 us
    pallas_call x1 -> x2, Pallas kernels: 6.26 us -> 36.8 us  [the longest x1 29 us: feedfwd(): pl.pallas_call(feedfwd_kernel, grid=(hidden_cols // cols,), out_shape=[ja...]
    pallas_call x7 -> x8, Pallas kernels: 66 us -> 40.2 us  [call_kernel(): pl.pallas_call(kernel, out_shape=[jax.ShapeDtypeStruct(*shape) for shape...]
    ppermute x37, waiting for transfers between devices: 104 us -> 80.4 us  [swap(): return lax.ppermute(value, axis, [(i, i ^ bit) for i in range(size)])]
    pallas_call x2 -> x1, Pallas kernels: 22 us -> 7.03 us  [weight_parts(): pl.pallas_call(partial(weights_kernel, first_tiles), grid=(columns // til...]
    reduce_scatter x1, waiting for transfers between devices: 12.2 us -> 4.08 us  [on_device(): lax.psum_scatter(attention_part, 'dp', scatter_dimension=0, tiled=True)]
    all_gather x2, waiting for transfers between devices: 0.49 us -> 6.4 us  [the longest x1 6.4 us: on_device(): lax.all_gather(interleave(gate_weight, up_weight, down_weight.T), 'dp', a...]
    ppermute x37, starting transfers between devices: 37.5 us -> 42.3 us  [swap(): return lax.ppermute(value, axis, [(i, i ^ bit) for i in range(size)])]
    unnamed x86 -> x104, local copies, waits for them, and re-layouts: 8.11 us -> 11.6 us
  transfers between devices with their start and end apart: 41 -> 41, of which waited for: 32 -> 22; matrix products, arithmetic and copies ran while one was open for 5% -> 8% of each run, Pallas kernels for 20% -> 19%
where the time goes in v1:
time: 266 us; the launch traced here: 265 us
  waiting for transfers between devices  91 us (34%)
  Pallas kernels  84.1 us (32%)
  starting transfers between devices  42.7 us (16%)
  between operations  17.7 us (7%)
  other arithmetic  14.9 us (6%)
  local copies, waits for them, and re-layouts  14.8 us (6%)
    ppermute x37, waiting for transfers between devices, swap(): return lax.ppermute(value, axis, [(i, i ^ bit) for i in range(size)])  80.4 us
    ppermute x37, starting transfers between devices, swap(): return lax.ppermute(value, axis, [(i, i ^ bit) for i in range(size)])  42.3 us
    pallas_call x8, Pallas kernels, call_kernel(): pl.pallas_call(kernel, out_shape=[jax.ShapeDtypeStruct(*shape) for shape...  40.2 us
    pallas_call x1, Pallas kernels, feedfwd(): pl.pallas_call(feedfwd_kernel, grid=(hidden_cols // cols,), out_shape=[ja...  29 us
    unnamed x104, local copies, waits for them, and re-layouts  11.6 us
    pallas_call x1, Pallas kernels, down_parts_of(): pl.pallas_call(down_kernel, grid=(hidden_cols // cols,), out_shape=[jax.S...  7.77 us
    pallas_call x1, Pallas kernels, weight_parts(): pl.pallas_call(partial(weights_kernel, first_tiles), grid=(columns // til...  7.03 us
    all_gather x1, waiting for transfers between devices, on_device(): lax.all_gather(interleave(gate_weight, up_weight, down_weight.T), 'dp', a...  6.4 us
  transfers between devices with their start and end apart: 41, of which 22 were waited for; matrix products, arithmetic and copies ran while one was open for 8% of the time, Pallas kernels for 19%

profile of v1, /device:TPU:0, one launch (start us, length us, event | category | flops | bytes accessed | tf_op | source)
XLA Modules:
  0.0 265.1 jit_solution(18351227442402526625)
XLA Ops:
  7.3 1.8 pack_weights.1
  9.6 1.0 copy-done.33
  11.1 3.0 %collective-permute-start = (bf16[128,1024]{1,0:T(8,128)(2,1)S(1)}, bf16[128,1024]{1,0:T(8,128)(2,1)S(1)}, u32[]{:S(2)}, u32[]{:S(2)}) collective-permute-start(bf16[128,1024]{1,0:T(8,128)(2,1)S(1)} %get-tuple-element.166), channel_id=1, source_target_pairs={{0,1},{1,0},{2,3},{3,2},{4,5},{5,4},{6,7},{7,6},{8,9},{9,8},{10,11... | collective-permute-start | bytes 786440 | tf_op jit(solution)/shard_map/ppermute | solution.py:658
  14.1 1.5 collective-permute-start.2
  15.6 4.8 %collective-permute-done = bf16[128,1024]{1,0:T(8,128)(2,1)S(1)} collective-permute-done((bf16[128,1024]{1,0:T(8,128)(2,1)S(1)}, bf16[128,1024]{1,0:T(8,128)(2,1)S(1)}, u32[]{:S(2)}, u32[]{:S(2)}) %collective-permute-start) | collective-permute-done | bytes 262176 | tf_op jit(solution)/shard_map/ppermute | solution.py:658
  20.5 1.8 collective-permute-start.1
  22.4 1.6 collective-permute-start.3
  24.6 1.1 collective-permute-start.6
  30.1 10.5 %collective-permute-done.4 = bf16[128,1024]{1,0:T(8,128)(2,1)S(1)} collective-permute-done((bf16[128,1024]{1,0:T(8,128)(2,1)S(1)}, bf16[128,1024]{1,0:T(8,128)(2,1)S(1)}, u32[]{:S(2)}, u32[]{:S(2)}) %collective-permute-start.4) | collective-permute-done | bytes 262176 | tf_op jit(solution)/shard_map/ppermute | solution.py:658
  41.4 1.1 collective-permute-start.5
  43.3 0.9 collective-permute-start.7
  44.3 16.8 %attend.1 = (f32[512,1024]{1,0:T(8,128)}, bf16[4,64,1024]{2,1,0:T(8,128)(2,1)}, bf16[2,64,1024]{2,1,0:T(8,128)(2,1)}, bf16[4,1024,64]{2,1,0:T(8,128)(2,1)}, bf16...) custom-call(s32[8]{0:T(128)} %stack.2.place_ref, ...), custom_call_target="tpu_custom_call" | custom-call | flops 16000000000 | bytes 1048576 | tf_op jit(solution)/shard_map/attend/pallas_call | solution.py:29
  62.0 0.9 collective-permute-start.9
  62.9 1.0 collective-permute-start.8
  63.9 9.4 %collective-permute-done.9.got_b_ref = bf16[256,1024]{1,0:T(8,128)(2,1)S(1)} collective-permute-done((bf16[256,1024]{1,0:T(8,128)(2,1)}, bf16[256,1024]{1,0:T(8,128)(2,1)S(1)}, u32[]{:S(2)}, u32[]{:S(2)}) %collective-permute-start.9) | collective-permute-done | bytes 524320 | tf_op jit(solution)/shard_map/ppermute | solution.py:658
  73.3 1.0 collective-permute-done.8.got_a_ref
  75.3 2.0 collective-permute-start.13
  77.4 4.4 %collective-permute-done.10 = bf16[128,1024]{1,0:T(8,128)(2,1)S(1)} collective-permute-done((bf16[128,1024]{1,0:T(8,128)(2,1)S(1)}, bf16[128,1024]{1,0:T(8,128)(2,1)S(1)}, u32[]{:S(2)}, u32[]{:S(2)}) %collective-permute-start.10) | collective-permute-done | bytes 262176 | tf_op jit(solution)/shard_map/ppermute | solution.py:658
  83.1 1.6 collective-permute-start.11
  84.7 1.0 collective-permute-start.14
  85.7 5.9 %collective-permute-done.11 = bf16[128,1024]{1,0:T(8,128)(2,1)S(1)} collective-permute-done((bf16[128,1024]{1,0:T(8,128)(2,1)S(1)}, bf16[128,1024]{1,0:T(8,128)(2,1)S(1)}, u32[]{:S(2)}, u32[]{:S(2)}) %collective-permute-start.11) | collective-permute-done | bytes 262176 | tf_op jit(solution)/shard_map/ppermute | solution.py:658
  91.6 3.1 %collective-permute-start.12 = (bf16[256,1024]{1,0:T(8,128)(2,1)S(1)}, bf16[256,1024]{1,0:T(8,128)(2,1)S(1)}, u32[]{:S(2)}, u32[]{:S(2)}) collective-permute-start(bf16[256,1024]{1,0:T(8,128)(2,1)S(1)} %pad_maximum_fusion.6.rows_a_ref), channel_id=1, source_target_pairs={{0,2},{1,3},{2,0},{3,1},{4,6},{5,7},{6,4},{7,5},{8,10},{9,11},{10,... | collective-permute-start | bytes 1572872 | tf_op jit(solution)/shard_map/ppermute | solution.py:658
  95.0 6.9 %collective-permute-done.12.rows_b_ref = bf16[256,1024]{1,0:T(8,128)(2,1)S(1)} collective-permute-done((bf16[256,1024]{1,0:T(8,128)(2,1)S(1)}, bf16[256,1024]{1,0:T(8,128)(2,1)S(1)}, u32[]{:S(2)}, u32[]{:S(2)}) %collective-permute-start.12) | collective-permute-done | bytes 524320 | tf_op jit(solution)/shard_map/ppermute | solution.py:658
  101.9 2.2 collective-permute-done.15.rows_d_ref
  104.1 6.4 %all-gather.5.cloned.1.call-done.weight_ref = bf16[1024,3456]{1,0:T(8,128)(2,1)} async-done(((bf16[128,3456]{1,0:T(8,128)(2,1)}), bf16[1024,3456]{1,0:T(8,128)(2,1)}) %all-gather.5.cloned.1.call-update) | async-done | bytes 7077904 | tf_op jit(solution)/shard_map/all_gather | solution.py:746
  110.5 29.0 %feedfwd.1 = (bf16[1024,1152]{1,0:T(8,128)(2,1)}, bf16[1024,3456]{1,0:T(8,128)(2,1)}, bf16[256,1024]{1,0:T(8,128)(2,1)}, bf16[256,1024]{1,0:T(8,128)(2,1)}, bf16...) custom-call(bf16[256,1024]{1,0:T(8,128)(2,1)} %copy-done.35, bf16[256,1024]{1,0:T(8,128)(2,1)} %copy-done.44, ...), custom_call_target="tpu_custom_call" | custom-call | flops 16000000000 | bytes 1048576 | tf_op jit(solution)/shard_map/feedfwd/pallas_call | solution.py:451
  139.9 1.5 collective-permute-start.16
  141.4 1.5 collective-permute-start.17
  142.9 11.3 %collective-permute-done.16.got_a_ref = bf16[256,1024]{1,0:T(8,128)(2,1)S(1)} collective-permute-done((bf16[256,1024]{1,0:T(8,128)(2,1)}, bf16[256,1024]{1,0:T(8,128)(2,1)S(1)}, u32[]{:S(2)}, u32[]{:S(2)}) %collective-permute-start.16) | collective-permute-done | bytes 524320 | tf_op jit(solution)/shard_map/ppermute | solution.py:658
  154.3 1.0 collective-permute-done.17.got_b_ref
  155.5 1.5 collective-permute-start.18
  157.0 0.9 collective-permute-start.19
  157.9 5.0 %collective-permute-done.18 = bf16[128,1024]{1,0:T(8,128)(2,1)S(1)} collective-permute-done((bf16[128,1024]{1,0:T(8,128)(2,1)S(1)}, bf16[128,1024]{1,0:T(8,128)(2,1)S(1)}, u32[]{:S(2)}, u32[]{:S(2)}) %collective-permute-start.18) | collective-permute-done | bytes 262176 | tf_op jit(solution)/shard_map/ppermute | solution.py:658
  163.0 1.2 collective-permute-done.19
  164.6 1.3 fusion.4
  166.5 1.2 collective-permute-start.22
  167.8 4.6 %collective-permute-done.20 = bf16[128,1024]{1,0:T(8,128)(2,1)S(1)} collective-permute-done((bf16[128,1024]{1,0:T(8,128)(2,1)S(1)}, bf16[128,1024]{1,0:T(8,128)(2,1)S(1)}, u32[]{:S(2)}, u32[]{:S(2)}) %collective-permute-start.20) | collective-permute-done | bytes 262176 | tf_op jit(solution)/shard_map/ppermute | solution.py:658
  172.4 1.6 collective-permute-start.21
  174.0 1.7 collective-permute-start.23
  175.8 7.8 %down_parts.1 = (bf16[256,1024]{1,0:T(8,128)(2,1)}, bf16[256,1024]{1,0:T(8,128)(2,1)}, bf16[256,1024]{1,0:T(8,128)(2,1)}, bf16[256,1024]{1,0:T(8,128)(2,1)}) custom-call(bf16[1024,1152]{1,0:T(8,128)(2,1)} %get-tuple-element.74.hidden_ref, bf16[1024,3456]{1,0:T(8,128)(2,1)} %all-gather.5.cloned.1.call-done.weight_ref, bf16[128,1024]{1,0:T(8,128)(2,1)} %copy-done.23, ...), custom_call_target="tpu_custom_call" | custom-call | flops 1000000000 | bytes 1048576 | tf_op jit(solution)/shard_map/down_parts/pallas_call | solution.py:592
  184.1 1.1 collective-permute-done.23.refs_2_.grad_d_ref.second_d_ref
  186.4 1.4 collective-permute-start.25
  187.8 18.5 %attend_back.1 = (bf16[1024,512]{1,0:T(8,128)(2,1)}, f32[2,64,128]{2,1,0:T(8,128)}, f32[1,1024]{1,0:T(1,128)}, bf16[256,1024]{1,0:T(8,128)(2,1)}, bf16[256,1024]...) custom-call(s32[8]{0:T(128)} %stack.2.place_ref, bf16[256,1024]{1,0:T(8,128)(2,1)} %copy-done.31, ...), custom_call_target="tpu_custom_call" | custom-call | flops 16000000000 | bytes 1048576 | tf_op jit(solution)/shard_map/attend_back/pallas_call | solution.py:29
  207.8 1.5 collective-permute-start.29
  209.2 0.9 reduce_sum.127
  211.0 1.0 copy-done.6
  214.4 1.2 collective-permute-start.27
  215.6 7.0 %weight_parts.1.refs_0_ = bf16[1024,768]{1,0:T(8,128)(2,1)} custom-call(bf16[256,1024]{1,0:T(8,128)(2,1)} %copy-done.29, bf16[256,1024]{1,0:T(8,128)(2,1)} %collective-permute-done.1.rows_b_ref.first_b_ref, bf16[256,1024]{1,0:T(8,128)(2,1)} %copy-done.30, bf16[256,1024]{1,0:T(8,128)(2,1)} %collective-permute-done.3.rows_d_ref.first_d_ref, ...), custom_call_target="tpu_custom_call" | custom-call | flops 1000000000 | bytes 1048576 | tf_op jit(solution)/shard_map/weight_parts/pallas_call | solution.py:531
  222.6 1.9 collective-permute-done.26
  225.4 1.4 copy-done
  226.8 1.0 copy-done.7
  227.9 1.1 copy-done.8
  230.5 1.2 add_convert_fusion.2
  232.9 1.0 collective-permute-start.31
  233.8 1.8 collective-permute-done.33
  236.6 3.7 %collective-permute-done.34 = f32[2176]{0:T(1024)S(1)} collective-permute-done((f32[2176]{0:T(1024)S(1)}, f32[2176]{0:T(1024)S(1)}, u32[]{:S(2)}, u32[]{:S(2)}) %collective-permute-start.34) | collective-permute-done | bytes 8736 | tf_op jit(solution)/shard_map/ppermute | solution.py:658
  240.6 1.1 pad_maximum_fusion
  241.7 2.3 collective-permute-done.35
  244.0 1.2 collective-permute-start.36
  246.0 2.2 copy.41
  249.4 1.3 multiply_reduce_fusion.5
  250.7 1.3 add_convert_fusion.1
  252.8 4.1 %reduce-scatter.5.cloned.1.call-done.value_ref = bf16[128,768]{1,0:T(8,128)(2,1)} async-done(((bf16[1024,768]{1,0:T(8,128)(2,1)}), bf16[128,768]{1,0:T(8,128)(2,1)}) %reduce-scatter.5.cloned.1.call-update) | async-done | bytes 196624 | tf_op jit(solution)/shard_map/reduce_scatter | solution.py:784
  256.9 1.7 split_weights.1
  (192 shorter events, 23.7 us)
Async XLA Ops:
  7.2 37.0 %all-gather.3.cloned.1.call-start = ((), (), s32[]{:S(2)}) async-start(), calls=%async_computation.2 | async-start | bytes 1769472 | tf_op jit(solution)/shard_map/all_gather | solution.py:740
  9.0 101.5 %all-gather.5.cloned.1.call-start = ((), (), s32[]{:S(2)}) async-start(), calls=%async_computation.3 | async-start | bytes 7962624 | tf_op jit(solution)/shard_map/all_gather | solution.py:746
  10.6 214.8 %reduce-scatter.3.cloned.1.call-start = ((), (), s32[]{:S(2)}) async-start(), calls=%async_computation.4 | async-start | bytes 7962624 | tf_op jit(solution)/shard_map/reduce_scatter | solution.py:765
  10.8 13.1 %copy-start.26 = (bf16[256,1024]{1,0:T(8,128)(2,1)S(1)}, bf16[256,1024]{1,0:T(8,128)(2,1)}, u32[]{:S(2)}) copy-start(bf16[256,1024]{1,0:T(8,128)(2,1)} %param.24) | copy-start | bytes 1572868
  11.0 14.6 %copy-start.42 = (s32[4]{0:T(128)S(1)}, s32[4]{0:T(128)}, u32[]{:S(2)}) copy-start(s32[4]{0:T(128)} %constant.53.clone) | copy-start | bytes 52
  11.0 18.4 %copy-start.45 = (f32[64]{0:T(128)S(1)}, f32[64]{0:T(128)}, u32[]{:S(2)}) copy-start(f32[64]{0:T(128)} %param.35) | copy-start | bytes 772
  11.1 18.4 %copy-start.46 = (f32[64]{0:T(128)S(1)}, f32[64]{0:T(128)}, u32[]{:S(2)}) copy-start(f32[64]{0:T(128)} %param.34) | copy-start | bytes 772
  11.1 9.3 %collective-permute-start = (bf16[128,1024]{1,0:T(8,128)(2,1)S(1)}, bf16[128,1024]{1,0:T(8,128)(2,1)S(1)}, u32[]{:S(2)}, u32[]{:S(2)}) collective-permute-start(bf16[128,1024]{1,0:T(8,128)(2,1)S(1)} %get-tuple-element.166), channel_id=1, source_target_pairs={{0,1},{1,0},{2,3},{3,2},{4,5},{5,4},{6,7},{7,6},{8,9},{9,8},{10,11... | collective-permute-start | bytes 786440 | tf_op jit(solution)/shard_map/ppermute | solution.py:658
  14.1 8.2 %collective-permute-start.2 = (bf16[128,1024]{1,0:T(8,128)(2,1)S(1)}, bf16[128,1024]{1,0:T(8,128)(2,1)S(1)}, u32[]{:S(2)}, u32[]{:S(2)}) collective-permute-start(bf16[128,1024]{1,0:T(8,128)(2,1)S(1)} %get-tuple-element.165), channel_id=1, source_target_pairs={{0,2},{1,3},{2,0},{3,1},{4,6},{5,7},{6,4},{7,5},{8,10},{9,11},{10,... | collective-permute-start | bytes 786440 | tf_op jit(solution)/shard_map/ppermute | solution.py:658
  20.5 22.8 %copy-start.29 = (bf16[256,1024]{1,0:T(8,128)(2,1)}, bf16[256,1024]{1,0:T(8,128)(2,1)S(1)}, u32[]{:S(2)}) copy-start(bf16[256,1024]{1,0:T(8,128)(2,1)S(1)} %pad_maximum_fusion.2.rows_a_ref.first_a_ref) | copy-start | bytes 1572868
  20.5 23.8 %collective-permute-start.1 = (bf16[256,1024]{1,0:T(8,128)(2,1)S(1)}, bf16[256,1024]{1,0:T(8,128)(2,1)}, u32[]{:S(2)}, u32[]{:S(2)}) collective-permute-start(bf16[256,1024]{1,0:T(8,128)(2,1)S(1)} %pad_maximum_fusion.2.rows_a_ref.first_a_ref), channel_id=1, source_target_pairs={{0,2},{1,3},{2,0},{3,1},{4,6},{5,7},{6,4},{7,5},{8,10},{9,11},{10,... | collective-permute-start | bytes 1572872 | tf_op jit(solution)/shard_map/ppermute | solution.py:658
  22.4 21.9 %copy-start.30 = (bf16[256,1024]{1,0:T(8,128)(2,1)}, bf16[256,1024]{1,0:T(8,128)(2,1)S(1)}, u32[]{:S(2)}) copy-start(bf16[256,1024]{1,0:T(8,128)(2,1)S(1)} %pad_maximum_fusion.3.rows_c_ref.first_c_ref) | copy-start | bytes 1572868
  22.4 21.9 %collective-permute-start.3 = (bf16[256,1024]{1,0:T(8,128)(2,1)S(1)}, bf16[256,1024]{1,0:T(8,128)(2,1)}, u32[]{:S(2)}, u32[]{:S(2)}) collective-permute-start(bf16[256,1024]{1,0:T(8,128)(2,1)S(1)} %pad_maximum_fusion.3.rows_c_ref.first_c_ref), channel_id=1, source_target_pairs={{0,1},{1,0},{2,3},{3,2},{4,5},{5,4},{6,7},{7,6},{8,9},{9,8},{10,11... | collective-permute-start | bytes 1572872 | tf_op jit(solution)/shard_map/ppermute | solution.py:658
  24.0 16.6 %collective-permute-start.4 = (bf16[128,1024]{1,0:T(8,128)(2,1)S(1)}, bf16[128,1024]{1,0:T(8,128)(2,1)S(1)}, u32[]{:S(2)}, u32[]{:S(2)}) collective-permute-start(bf16[128,1024]{1,0:T(8,128)(2,1)S(1)} %get-tuple-element.164), channel_id=1, source_target_pairs={{0,1},{1,0},{2,3},{3,2},{4,5},{5,4},{6,7},{7,6},{8,9},{9,8},{10,11... | collective-permute-start | bytes 786440 | tf_op jit(solution)/shard_map/ppermute | solution.py:658
  24.6 17.9 %collective-permute-start.6 = (bf16[128,1024]{1,0:T(8,128)(2,1)S(1)}, bf16[128,1024]{1,0:T(8,128)(2,1)S(1)}, u32[]{:S(2)}, u32[]{:S(2)}) collective-permute-start(bf16[128,1024]{1,0:T(8,128)(2,1)S(1)} %get-tuple-element.163), channel_id=1, source_target_pairs={{0,2},{1,3},{2,0},{3,1},{4,6},{5,7},{6,4},{7,5},{8,10},{9,11},{10,... | collective-permute-start | bytes 786440 | tf_op jit(solution)/shard_map/ppermute | solution.py:658
  41.4 19.6 %collective-permute-start.5 = (bf16[256,1024]{1,0:T(8,128)(2,1)}, bf16[256,1024]{1,0:T(8,128)(2,1)S(1)}, u32[]{:S(2)}, u32[]{:S(2)}) collective-permute-start(bf16[256,1024]{1,0:T(8,128)(2,1)} %pad_maximum_fusion.4.cot_a_ref), channel_id=1, source_target_pairs={{0,2},{1,3},{2,0},{3,1},{4,6},{5,7},{6,4},{7,5},{8,10},{9,11},{10,... | collective-permute-start | bytes 1572872 | tf_op jit(solution)/shard_map/ppermute | solution.py:658
  43.3 17.7 %collective-permute-start.7 = (bf16[256,1024]{1,0:T(8,128)(2,1)}, bf16[256,1024]{1,0:T(8,128)(2,1)S(1)}, u32[]{:S(2)}, u32[]{:S(2)}) collective-permute-start(bf16[256,1024]{1,0:T(8,128)(2,1)} %pad_maximum_fusion.5.cot_c_ref), channel_id=1, source_target_pairs={{0,1},{1,0},{2,3},{3,2},{4,5},{5,4},{6,7},{7,6},{8,9},{9,8},{10,11... | collective-permute-start | bytes 1572872 | tf_op jit(solution)/shard_map/ppermute | solution.py:658
  62.0 12.3 %copy-start.9 = (bf16[256,1024]{1,0:T(8,128)(2,1)S(1)}, bf16[256,1024]{1,0:T(8,128)(2,1)}, u32[]{:S(2)}) copy-start(bf16[256,1024]{1,0:T(8,128)(2,1)} %get-tuple-element.66.stay_a_ref) | copy-start | bytes 1572868
  62.0 12.3 %copy-start.10 = (bf16[256,1024]{1,0:T(8,128)(2,1)S(1)}, bf16[256,1024]{1,0:T(8,128)(2,1)}, u32[]{:S(2)}) copy-start(bf16[256,1024]{1,0:T(8,128)(2,1)} %get-tuple-element.68.stay_b_ref) | copy-start | bytes 1572868
  62.0 11.2 %collective-permute-start.9 = (bf16[256,1024]{1,0:T(8,128)(2,1)}, bf16[256,1024]{1,0:T(8,128)(2,1)S(1)}, u32[]{:S(2)}, u32[]{:S(2)}) collective-permute-start(bf16[256,1024]{1,0:T(8,128)(2,1)} %later.6), channel_id=1, source_target_pairs={{0,1},{1,0},{2,3},{3,2},{4,5},{5,4},{6,7},{7,6},{8,9},{9,8},{10,11... | collective-permute-start | bytes 1572872 | tf_op jit(solution)/shard_map/ppermute | solution.py:658
  62.9 11.4 %collective-permute-start.8 = (bf16[256,1024]{1,0:T(8,128)(2,1)}, bf16[256,1024]{1,0:T(8,128)(2,1)S(1)}, u32[]{:S(2)}, u32[]{:S(2)}) collective-permute-start(bf16[256,1024]{1,0:T(8,128)(2,1)} %later.5), channel_id=1, source_target_pairs={{0,2},{1,3},{2,0},{3,1},{4,6},{5,7},{6,4},{7,5},{8,10},{9,11},{10,... | collective-permute-start | bytes 1572872 | tf_op jit(solution)/shard_map/ppermute | solution.py:658
  74.5 7.3 %collective-permute-start.10 = (bf16[128,1024]{1,0:T(8,128)(2,1)S(1)}, bf16[128,1024]{1,0:T(8,128)(2,1)S(1)}, u32[]{:S(2)}, u32[]{:S(2)}) collective-permute-start(bf16[128,1024]{1,0:T(8,128)(2,1)S(1)} %get-tuple-element.71), channel_id=1, source_target_pairs={{0,1},{1,0},{2,3},{3,2},{4,5},{5,4},{6,7},{7,6},{8,9},{9,8},{10,11... | collective-permute-start | bytes 786440 | tf_op jit(solution)/shard_map/ppermute | solution.py:658
  75.3 7.3 %collective-permute-start.13 = (bf16[128,1024]{1,0:T(8,128)(2,1)S(1)}, bf16[128,1024]{1,0:T(8,128)(2,1)S(1)}, u32[]{:S(2)}, u32[]{:S(2)}) collective-permute-start(bf16[128,1024]{1,0:T(8,128)(2,1)S(1)} %get-tuple-element.73), channel_id=1, source_target_pairs={{0,2},{1,3},{2,0},{3,1},{4,6},{5,7},{6,4},{7,5},{8,10},{9,11},{10,... | collective-permute-start | bytes 786440 | tf_op jit(solution)/shard_map/ppermute | solution.py:658
  82.9 81.7 %copy-start.15 = (f32[128,1024]{1,0:T(8,128)}, f32[128,1024]{1,0:T(8,128)S(1)}, u32[]{:S(2)}) copy-start(f32[128,1024]{1,0:T(8,128)S(1)} %get-tuple-element.151) | copy-start | bytes 1572868
  82.9 81.7 %copy-start.16 = (f32[128,1024]{1,0:T(8,128)}, f32[128,1024]{1,0:T(8,128)S(1)}, u32[]{:S(2)}) copy-start(f32[128,1024]{1,0:T(8,128)S(1)} %get-tuple-element.147) | copy-start | bytes 1572868
  83.1 8.5 %collective-permute-start.11 = (bf16[128,1024]{1,0:T(8,128)(2,1)S(1)}, bf16[128,1024]{1,0:T(8,128)(2,1)S(1)}, u32[]{:S(2)}, u32[]{:S(2)}) collective-permute-start(bf16[128,1024]{1,0:T(8,128)(2,1)S(1)} %get-tuple-element.174), channel_id=1, source_target_pairs={{0,1},{1,0},{2,3},{3,2},{4,5},{5,4},{6,7},{7,6},{8,9},{9,8},{10,11... | collective-permute-start | bytes 786440 | tf_op jit(solution)/shard_map/ppermute | solution.py:658
  84.7 10.0 %collective-permute-start.14 = (bf16[128,1024]{1,0:T(8,128)(2,1)S(1)}, bf16[128,1024]{1,0:T(8,128)(2,1)S(1)}, u32[]{:S(2)}, u32[]{:S(2)}) collective-permute-start(bf16[128,1024]{1,0:T(8,128)(2,1)S(1)} %get-tuple-element.173), channel_id=1, source_target_pairs={{0,2},{1,3},{2,0},{3,1},{4,6},{5,7},{6,4},{7,5},{8,10},{9,11},{10,... | collective-permute-start | bytes 786440 | tf_op jit(solution)/shard_map/ppermute | solution.py:658
  91.6 18.9 %copy-start.35 = (bf16[256,1024]{1,0:T(8,128)(2,1)}, bf16[256,1024]{1,0:T(8,128)(2,1)S(1)}, u32[]{:S(2)}) copy-start(bf16[256,1024]{1,0:T(8,128)(2,1)S(1)} %pad_maximum_fusion.6.rows_a_ref) | copy-start | bytes 1572868
  91.6 10.3 %collective-permute-start.12 = (bf16[256,1024]{1,0:T(8,128)(2,1)S(1)}, bf16[256,1024]{1,0:T(8,128)(2,1)S(1)}, u32[]{:S(2)}, u32[]{:S(2)}) collective-permute-start(bf16[256,1024]{1,0:T(8,128)(2,1)S(1)} %pad_maximum_fusion.6.rows_a_ref), channel_id=1, source_target_pairs={{0,2},{1,3},{2,0},{3,1},{4,6},{5,7},{6,4},{7,5},{8,10},{9,11},{10,... | collective-permute-start | bytes 1572872 | tf_op jit(solution)/shard_map/ppermute | solution.py:658
  94.8 15.8 %copy-start.36 = (bf16[256,1024]{1,0:T(8,128)(2,1)}, bf16[256,1024]{1,0:T(8,128)(2,1)S(1)}, u32[]{:S(2)}) copy-start(bf16[256,1024]{1,0:T(8,128)(2,1)S(1)} %pad_maximum_fusion.7.rows_c_ref) | copy-start | bytes 1572868
  94.8 9.4 %collective-permute-start.15 = (bf16[256,1024]{1,0:T(8,128)(2,1)S(1)}, bf16[256,1024]{1,0:T(8,128)(2,1)}, u32[]{:S(2)}, u32[]{:S(2)}) collective-permute-start(bf16[256,1024]{1,0:T(8,128)(2,1)S(1)} %pad_maximum_fusion.7.rows_c_ref), channel_id=1, source_target_pairs={{0,1},{1,0},{2,3},{3,2},{4,5},{5,4},{6,7},{7,6},{8,9},{9,8},{10,11... | collective-permute-start | bytes 1572872 | tf_op jit(solution)/shard_map/ppermute | solution.py:658
  139.6 15.7 %copy-start.11 = (bf16[256,1024]{1,0:T(8,128)(2,1)S(1)}, bf16[256,1024]{1,0:T(8,128)(2,1)}, u32[]{:S(2)}) copy-start(bf16[256,1024]{1,0:T(8,128)(2,1)} %get-tuple-element.75.stay_a_ref) | copy-start | bytes 1572868
  139.6 15.6 %copy-start.12 = (bf16[256,1024]{1,0:T(8,128)(2,1)S(1)}, bf16[256,1024]{1,0:T(8,128)(2,1)}, u32[]{:S(2)}) copy-start(bf16[256,1024]{1,0:T(8,128)(2,1)} %get-tuple-element.77.stay_b_ref) | copy-start | bytes 1572868
  139.6 117.3 %reduce-scatter.5.cloned.1.call-start = ((), (), s32[]{:S(2)}) async-start(), calls=%async_computation.5 | async-start | bytes 1769472 | tf_op jit(solution)/shard_map/reduce_scatter | solution.py:784
  139.9 14.3 %collective-permute-start.16 = (bf16[256,1024]{1,0:T(8,128)(2,1)}, bf16[256,1024]{1,0:T(8,128)(2,1)S(1)}, u32[]{:S(2)}, u32[]{:S(2)}) collective-permute-start(bf16[256,1024]{1,0:T(8,128)(2,1)} %get-tuple-element.76), channel_id=1, source_target_pairs={{0,2},{1,3},{2,0},{3,1},{4,6},{5,7},{6,4},{7,5},{8,10},{9,11},{10,... | collective-permute-start | bytes 1572872 | tf_op jit(solution)/shard_map/ppermute | solution.py:658
  141.4 13.8 %collective-permute-start.17 = (bf16[256,1024]{1,0:T(8,128)(2,1)S(1)}, bf16[256,1024]{1,0:T(8,128)(2,1)S(1)}, u32[]{:S(2)}, u32[]{:S(2)}) collective-permute-start(bf16[256,1024]{1,0:T(8,128)(2,1)S(1)} %copy-done.43), channel_id=1, source_target_pairs={{0,1},{1,0},{2,3},{3,2},{4,5},{5,4},{6,7},{7,6},{8,9},{9,8},{10,11... | collective-permute-start | bytes 1572872 | tf_op jit(solution)/shard_map/ppermute | solution.py:658
  155.5 7.5 %collective-permute-start.18 = (bf16[128,1024]{1,0:T(8,128)(2,1)S(1)}, bf16[128,1024]{1,0:T(8,128)(2,1)S(1)}, u32[]{:S(2)}, u32[]{:S(2)}) collective-permute-start(bf16[128,1024]{1,0:T(8,128)(2,1)S(1)} %get-tuple-element.80), channel_id=1, source_target_pairs={{0,1},{1,0},{2,3},{3,2},{4,5},{5,4},{6,7},{7,6},{8,9},{9,8},{10,11... | collective-permute-start | bytes 786440 | tf_op jit(solution)/shard_map/ppermute | solution.py:658
  157.0 7.1 %collective-permute-start.19 = (bf16[128,1024]{1,0:T(8,128)(2,1)S(1)}, bf16[128,1024]{1,0:T(8,128)(2,1)S(1)}, u32[]{:S(2)}, u32[]{:S(2)}) collective-permute-start(bf16[128,1024]{1,0:T(8,128)(2,1)S(1)} %get-tuple-element.82), channel_id=1, source_target_pairs={{0,2},{1,3},{2,0},{3,1},{4,6},{5,7},{6,4},{7,5},{8,10},{9,11},{10,... | collective-permute-start | bytes 786440 | tf_op jit(solution)/shard_map/ppermute | solution.py:658
  165.9 9.8 %copy-start.22 = (bf16[128,1024]{1,0:T(8,128)(2,1)}, bf16[128,1024]{1,0:T(8,128)(2,1)S(1)}, u32[]{:S(2)}) copy-start(bf16[128,1024]{1,0:T(8,128)(2,1)S(1)} %get-tuple-element.140.refs_1_) | copy-start | bytes 786436
  165.9 9.8 %copy-start.23 = (bf16[128,1024]{1,0:T(8,128)(2,1)}, bf16[128,1024]{1,0:T(8,128)(2,1)S(1)}, u32[]{:S(2)}) copy-start(bf16[128,1024]{1,0:T(8,128)(2,1)S(1)} %get-tuple-element.161.refs_0_) | copy-start | bytes 786436
  165.9 6.4 %collective-permute-start.20 = (bf16[128,1024]{1,0:T(8,128)(2,1)S(1)}, bf16[128,1024]{1,0:T(8,128)(2,1)S(1)}, u32[]{:S(2)}, u32[]{:S(2)}) collective-permute-start(bf16[128,1024]{1,0:T(8,128)(2,1)S(1)} %get-tuple-element.161.refs_0_), channel_id=1, source_target_pairs={{0,1},{1,0},{2,3},{3,2},{4,5},{5,4},{6,7},{7,6},{8,9},{9,8},{10,11... | collective-permute-start | bytes 786440 | tf_op jit(solution)/shard_map/ppermute | solution.py:658
  166.5 7.4 %collective-permute-start.22 = (bf16[128,1024]{1,0:T(8,128)(2,1)S(1)}, bf16[128,1024]{1,0:T(8,128)(2,1)S(1)}, u32[]{:S(2)}, u32[]{:S(2)}) collective-permute-start(bf16[128,1024]{1,0:T(8,128)(2,1)S(1)} %get-tuple-element.140.refs_1_), channel_id=1, source_target_pairs={{0,2},{1,3},{2,0},{3,1},{4,6},{5,7},{6,4},{7,5},{8,10},{9,11},{10,... | collective-permute-start | bytes 786440 | tf_op jit(solution)/shard_map/ppermute | solution.py:658
  172.4 11.2 %copy-start.31 = (bf16[256,1024]{1,0:T(8,128)(2,1)}, bf16[256,1024]{1,0:T(8,128)(2,1)S(1)}, u32[]{:S(2)}) copy-start(bf16[256,1024]{1,0:T(8,128)(2,1)S(1)} %pad_maximum_fusion.8.grad_a_ref.second_a_ref) | copy-start | bytes 1572868
  172.4 11.7 %collective-permute-start.21 = (bf16[256,1024]{1,0:T(8,128)(2,1)S(1)}, bf16[256,1024]{1,0:T(8,128)(2,1)S(1)}, u32[]{:S(2)}, u32[]{:S(2)}) collective-permute-start(bf16[256,1024]{1,0:T(8,128)(2,1)S(1)} %pad_maximum_fusion.8.grad_a_ref.second_a_ref), channel_id=1, source_target_pairs={{0,2},{1,3},{2,0},{3,1},{4,6},{5,7},{6,4},{7,5},{8,10},{9,11},{10,... | collective-permute-start | bytes 1572872 | tf_op jit(solution)/shard_map/ppermute | solution.py:658
  174.0 9.5 %copy-start.32 = (bf16[256,1024]{1,0:T(8,128)(2,1)}, bf16[256,1024]{1,0:T(8,128)(2,1)S(1)}, u32[]{:S(2)}) copy-start(bf16[256,1024]{1,0:T(8,128)(2,1)S(1)} %pad_maximum_fusion.9.grad_c_ref.second_c_ref) | copy-start | bytes 1572868
  174.0 11.2 %collective-permute-start.23 = (bf16[256,1024]{1,0:T(8,128)(2,1)S(1)}, bf16[256,1024]{1,0:T(8,128)(2,1)S(1)}, u32[]{:S(2)}, u32[]{:S(2)}) collective-permute-start(bf16[256,1024]{1,0:T(8,128)(2,1)S(1)} %pad_maximum_fusion.9.grad_c_ref.second_c_ref), channel_id=1, source_target_pairs={{0,1},{1,0},{2,3},{3,2},{4,5},{5,4},{6,7},{7,6},{8,9},{9,8},{10,11... | collective-permute-start | bytes 1572872 | tf_op jit(solution)/shard_map/ppermute | solution.py:658
  186.0 24.1 %collective-permute-start.24 = (bf16[256,1024]{1,0:T(8,128)(2,1)}, bf16[256,1024]{1,0:T(8,128)(2,1)S(1)}, u32[]{:S(2)}, u32[]{:S(2)}) collective-permute-start(bf16[256,1024]{1,0:T(8,128)(2,1)} %later.7), channel_id=1, source_target_pairs={{0,2},{1,3},{2,0},{3,1},{4,6},{5,7},{6,4},{7,5},{8,10},{9,11},{10,... | collective-permute-start | bytes 1572872 | tf_op jit(solution)/shard_map/ppermute | solution.py:658
  186.4 23.8 %collective-permute-start.25 = (bf16[256,1024]{1,0:T(8,128)(2,1)}, bf16[256,1024]{1,0:T(8,128)(2,1)S(1)}, u32[]{:S(2)}, u32[]{:S(2)}) collective-permute-start(bf16[256,1024]{1,0:T(8,128)(2,1)} %later.8), channel_id=1, source_target_pairs={{0,1},{1,0},{2,3},{3,2},{4,5},{5,4},{6,7},{7,6},{8,9},{9,8},{10,11... | collective-permute-start | bytes 1572872 | tf_op jit(solution)/shard_map/ppermute | solution.py:658
  187.8 23.2 %copy-start.3 = (bf16[256,1024]{1,0:T(8,128)(2,1)S(1)}, bf16[256,1024]{1,0:T(8,128)(2,1)}, u32[]{:S(2)}) copy-start(bf16[256,1024]{1,0:T(8,128)(2,1)} %get-tuple-element.83.stay_a_ref.earlier_ref) | copy-start | bytes 1572868
  187.8 23.2 %copy-start.4 = (bf16[256,1024]{1,0:T(8,128)(2,1)S(1)}, bf16[256,1024]{1,0:T(8,128)(2,1)}, u32[]{:S(2)}) copy-start(bf16[256,1024]{1,0:T(8,128)(2,1)} %get-tuple-element.85.stay_b_ref) | copy-start | bytes 1572868
  207.0 18.4 %collective-permute-start.28 = (bf16[256,1024]{1,0:T(8,128)(2,1)}, bf16[256,1024]{1,0:T(8,128)(2,1)S(1)}, u32[]{:S(2)}, u32[]{:S(2)}) collective-permute-start(bf16[256,1024]{1,0:T(8,128)(2,1)} %get-tuple-element.103), channel_id=1, source_target_pairs={{0,2},{1,3},{2,0},{3,1},{4,6},{5,7},{6,4},{7,5},{8,10},{9,11},{10,... | collective-permute-start | bytes 1572872 | tf_op jit(solution)/shard_map/ppermute | solution.py:658
  207.8 17.6 %collective-permute-start.29 = (bf16[256,1024]{1,0:T(8,128)(2,1)}, bf16[256,1024]{1,0:T(8,128)(2,1)S(1)}, u32[]{:S(2)}, u32[]{:S(2)}) collective-permute-start(bf16[256,1024]{1,0:T(8,128)(2,1)} %get-tuple-element.105), channel_id=1, source_target_pairs={{0,1},{1,0},{2,3},{3,2},{4,5},{5,4},{6,7},{7,6},{8,9},{9,8},{10,11... | collective-permute-start | bytes 1572872 | tf_op jit(solution)/shard_map/ppermute | solution.py:658
  213.7 10.9 %collective-permute-start.26 = (bf16[128,1024]{1,0:T(8,128)(2,1)}, bf16[128,1024]{1,0:T(8,128)(2,1)S(1)}, u32[]{:S(2)}, u32[]{:S(2)}) collective-permute-start(bf16[128,1024]{1,0:T(8,128)(2,1)} %get-tuple-element.88), channel_id=1, source_target_pairs={{0,1},{1,0},{2,3},{3,2},{4,5},{5,4},{6,7},{7,6},{8,9},{9,8},{10,11... | collective-permute-start | bytes 786440 | tf_op jit(solution)/shard_map/ppermute | solution.py:658
  214.4 16.1 %collective-permute-start.27 = (bf16[128,1024]{1,0:T(8,128)(2,1)S(1)}, bf16[128,1024]{1,0:T(8,128)(2,1)}, u32[]{:S(2)}, u32[]{:S(2)}) collective-permute-start(bf16[128,1024]{1,0:T(8,128)(2,1)S(1)} %get-tuple-element.90), channel_id=1, source_target_pairs={{0,2},{1,3},{2,0},{3,1},{4,6},{5,7},{6,4},{7,5},{8,10},{9,11},{10,... | collective-permute-start | bytes 786440 | tf_op jit(solution)/shard_map/ppermute | solution.py:658
  215.6 9.0 %copy-start.2 = (f32[128,1024]{1,0:T(8,128)S(1)}, f32[128,1024]{1,0:T(8,128)}, u32[]{:S(2)}) copy-start(f32[128,1024]{1,0:T(8,128)} %copy-done.1) | copy-start | bytes 1572868
  215.6 9.0 %copy-start.17 = (f32[128,1024]{1,0:T(8,128)S(1)}, f32[128,1024]{1,0:T(8,128)}, u32[]{:S(2)}) copy-start(f32[128,1024]{1,0:T(8,128)} %copy-done.16) | copy-start | bytes 1572868
  230.4 1.3 collective-permute-start.32
  231.7 4.0 %collective-permute-start.33 = (f32[2176]{0:T(1024)S(1)}, f32[2176]{0:T(1024)S(1)}, u32[]{:S(2)}, u32[]{:S(2)}) collective-permute-start(f32[2176]{0:T(1024)S(1)} %fusion.12), channel_id=1, source_target_pairs={{0,8},{4,12},{8,0},{12,4},{16,24},{20,28},{24,16},{28,20},{1,9},{5... | collective-permute-start | bytes 26120 | tf_op jit(solution)/shard_map/ppermute | solution.py:658
  232.6 16.8 %collective-permute-start.30 = (bf16[128,1024]{1,0:T(8,128)(2,1)S(1)}, bf16[128,1024]{1,0:T(8,128)(2,1)S(1)}, u32[]{:S(2)}, u32[]{:S(2)}) collective-permute-start(bf16[128,1024]{1,0:T(8,128)(2,1)S(1)} %get-tuple-element.110), channel_id=1, source_target_pairs={{0,1},{1,0},{2,3},{3,2},{4,5},{5,4},{6,7},{7,6},{8,9},{9,8},{10,11... | collective-permute-start | bytes 786440 | tf_op jit(solution)/shard_map/ppermute | solution.py:658
  232.9 16.6 %collective-permute-start.31 = (bf16[128,1024]{1,0:T(8,128)(2,1)S(1)}, bf16[128,1024]{1,0:T(8,128)(2,1)}, u32[]{:S(2)}, u32[]{:S(2)}) collective-permute-start(bf16[128,1024]{1,0:T(8,128)(2,1)S(1)} %get-tuple-element.112), channel_id=1, source_target_pairs={{0,2},{1,3},{2,0},{3,1},{4,6},{5,7},{6,4},{7,5},{8,10},{9,11},{10,... | collective-permute-start | bytes 786440 | tf_op jit(solution)/shard_map/ppermute | solution.py:658
  235.7 4.6 %collective-permute-start.34 = (f32[2176]{0:T(1024)S(1)}, f32[2176]{0:T(1024)S(1)}, u32[]{:S(2)}, u32[]{:S(2)}) collective-permute-start(f32[2176]{0:T(1024)S(1)} %add.199), channel_id=1, source_target_pairs={{0,16},{4,20},{8,24},{12,28},{16,0},{20,4},{24,8},{28,12},{1,17},{... | collective-permute-start | bytes 26120 | tf_op jit(solution)/shard_map/ppermute | solution.py:658
  240.3 3.7 %collective-permute-start.35 = (f32[2176]{0:T(1024)S(1)}, f32[2176]{0:T(1024)S(1)}, u32[]{:S(2)}, u32[]{:S(2)}) collective-permute-start(f32[2176]{0:T(1024)S(1)} %add.200), channel_id=1, source_target_pairs={{0,1},{1,0},{2,3},{3,2},{4,5},{5,4},{6,7},{7,6},{8,9},{9,8},{10,11... | collective-permute-start | bytes 26120 | tf_op jit(solution)/shard_map/ppermute | solution.py:658
  240.6 8.8 %copy-start.14 = (f32[256,1024]{1,0:T(8,128)S(1)}, f32[256,1024]{1,0:T(8,128)}, u32[]{:S(2)}) copy-start(f32[256,1024]{1,0:T(8,128)} %copy-done.13) | copy-start | bytes 3145732
  244.0 4.2 %collective-permute-start.36 = (f32[2176]{0:T(1024)S(1)}, f32[2176]{0:T(1024)S(1)}, u32[]{:S(2)}, u32[]{:S(2)}) collective-permute-start(f32[2176]{0:T(1024)S(1)} %add.201), channel_id=1, source_target_pairs={{0,2},{1,3},{2,0},{3,1},{4,6},{5,7},{6,4},{7,5},{8,10},{9,11},{10,... | collective-permute-start | bytes 26120 | tf_op jit(solution)/shard_map/ppermute | solution.py:658
  (24 other events, 59.4 us)
Sparse Core Ops, SparseCore 0:
  10.3 27.7 all-gather.2
  39.7 70.7 all-gather.4
  139.8 75.7 reduce-scatter.2
  225.5 31.3 reduce-scatter.4

commit v2 on v1

--- a/solution.py
+++ b/solution.py
@@ -246,8 +246,9 @@
     cosine_ref,
     sine_ref,
     begin_ref,
+    context_ref,
     earlier_ref,
-    out_ref,
+    weight_grad_ref,
     head_gain_ref,
     row_gain_ref,
     part_a_ref,
@@ -263,6 +264,8 @@
     value_grad,
     joined,
     natural,
+    out_ref,
+    turned,
     bias,
 ):
     query_heads, key_heads, head_dim = sizes
@@ -273,6 +276,8 @@
     out_weight = weight_ref[:, columns:]
     for q, rows_ref in enumerate((grad_a_ref, grad_b_ref, grad_c_ref, grad_d_ref)):
         mixed[q * quarter : (q + 1) * quarter, :] = dot(rows_ref[...], out_weight).astype(BFLOAT)
+        turned[:, q * quarter : (q + 1) * quarter] = rows_ref[...].T
+    weight_grad_ref[:, columns:] = dot(turned[...], context_ref[...]).astype(BFLOAT)
     collect(place_ref, mixed, context)
     for head in range(query_heads):
         part = context[:, head * head_dim : (head + 1) * head_dim]
@@ -336,15 +341,18 @@
         part_ref[...] = part.astype(BFLOAT)
         row_gain += jnp.sum(part * rows_refs[q][...].astype(SINGLE), axis=0, keepdims=True)
     row_gain_ref[...] = row_gain
-
-
-def attend_back(sizes, place, grads, quarters, weight, gains, saved, earlier):
+    for q, rows_ref in enumerate(rows_refs):
+        turned[:, q * quarter : (q + 1) * quarter] = rows_ref[...].T
+    weight_grad_ref[:, :columns] = dot(turned[...], out_ref[...]).astype(BFLOAT)
+
+
+def attend_back(sizes, place, grads, quarters, weight, gains, saved, context, earlier):
     query_heads, key_heads, head_dim = sizes
     heads = query_heads + key_heads
     columns = (heads + key_heads) * head_dim
     quarter, width = quarters[0].shape
     shapes = [
-        ((LEN, columns), BFLOAT),
+        (weight.shape, BFLOAT),
         ((2, head_dim, 128), SINGLE),
         ((1, width), SINGLE),
     ] + [((quarter, width), BFLOAT)] * 4
@@ -358,9 +366,11 @@
         ((key_heads, LEN, head_dim), SINGLE),
         ((heads * head_dim, LEN), SINGLE),
         ((LEN, columns), BFLOAT),
+        ((LEN, columns), BFLOAT),
+        ((width, LEN), BFLOAT),
         ((LEN, TILE), SINGLE),
     ]
-    arrays = (*grads, *quarters, weight, gains, *saved)
+    arrays = (*grads, *quarters, weight, gains, *saved, context)
     kernel = partial(attend_back_kernel, sizes)
     outs = call_kernel(
         kernel, "attend_back", HEAVY, 56, shapes, (place,), arrays, scratch, (earlier,)
@@ -471,76 +481,6 @@
     return outs[0], outs[1], outs[2:]
 
 
-def weights_kernel(
-    first_tiles,
-    first_a_ref,
-    first_b_ref,
-    first_c_ref,
-    first_d_ref,
-    second_a_ref,
-    second_b_ref,
-    second_c_ref,
-    second_d_ref,
-    first_grad_ref,
-    second_grad_ref,
-    earlier_ref,
-    out_ref,
-    turned_ref,
-):
-    step = pl.program_id(0)
-    quarter = first_a_ref.shape[0]
-
-    def turn_over(*refs):
-        for q, ref in enumerate(refs):
-            turned_ref[:, q * quarter : (q + 1) * quarter] = ref[...].T
-
-    @pl.when(step == 0)
-    def _():
-        turn_over(first_a_ref, first_b_ref, first_c_ref, first_d_ref)
-
-    @pl.when(step < first_tiles)
-    def _():
-        out_ref[...] = dot(turned_ref[...], first_grad_ref[...]).astype(BFLOAT)
-
-    @pl.when(step == first_tiles)
-    def _():
-        turn_over(second_a_ref, second_b_ref, second_c_ref, second_d_ref)
-
-    @pl.when(step >= first_tiles)
-    def _():
-        out_ref[...] = dot(turned_ref[...], second_grad_ref[...]).astype(BFLOAT)
-
-
-def weight_parts(firsts, first_grad, seconds, second_grad, earlier):
-    first_cols, second_cols = first_grad.shape[1], second_grad.shape[1]
-    quarter, width = firsts[0].shape
-    tiles = [t for t in (256, 128) if first_cols % t == 0 and second_cols % t == 0]
-    if not tiles:
-        sums = []
-        for lefts, right in ((firsts, first_grad), (seconds, second_grad)):
-            left = jnp.concatenate(lefts, axis=0)
-            total = jnp.einsum("nd,ne->de", left, right, preferred_element_type=SINGLE)
-            sums.append(total.astype(BFLOAT))
-        return jnp.concatenate(sums, axis=1)
-    tile = tiles[0]
-    first_tiles = first_cols // tile
-    whole = pl.BlockSpec((quarter, width), lambda j: (0, 0))
-    first_spec = pl.BlockSpec((LEN, tile), lambda j: (0, jnp.minimum(j, first_tiles - 1)))
-    second_spec = pl.BlockSpec((LEN, tile), lambda j: (0, jnp.maximum(j - first_tiles, 0)))
-    columns = first_cols + second_cols
-    return pl.pallas_call(
-        partial(weights_kernel, first_tiles),
-        grid=(columns // tile,),
-        out_shape=jax.ShapeDtypeStruct((width, columns), BFLOAT),
-        in_specs=[whole] * 8 + [first_spec, second_spec, pl.BlockSpec(memory_space=pl.ANY)],
-        out_specs=pl.BlockSpec((width, tile), lambda j: (0, j)),
-        scratch_shapes=[pltpu.VMEM((width, LEN), BFLOAT)],
-        compiler_params=pltpu.CompilerParams(vmem_limit_bytes=56 * MIB),
-        cost_estimate=pl.CostEstimate(flops=LIGHT, bytes_accessed=2**20, transcendentals=0),
-        name="weight_parts",
-    )(*firsts, *seconds, first_grad, second_grad, earlier)
-
-
 def pair_sum_kernel(stay_a_ref, got_a_ref, stay_b_ref, got_b_ref, *refs):
     outs = refs[-4:]
     rows = stay_a_ref.shape[0] // 2
@@ -604,6 +544,25 @@
         cost_estimate=pl.CostEstimate(flops=LIGHT, bytes_accessed=2**20, transcendentals=0),
         name="down_parts",
     )(hidden, weight, *earlier)
+
+
+def finish_kernel(tokens_ref, gain_ref, *refs):
+    block_ref, tokens_out_ref = refs[-2:]
+    rows = tokens_ref.shape[0] // 2
+    for half in range(2):
+        part = slice(half * rows, (half + 1) * rows)
+        residual, grad, down, down_got, norm, norm_got = refs[6 * half : 6 * half + 6]
+        summed = down[...] + down_got[...].astype(SINGLE)
+        block_ref[part, :] = (residual[...] + summed).astype(BFLOAT)
+        back = norm[...] + norm_got[...].astype(SINGLE)
+        back, _ = rms_back(tokens_ref[part, :].astype(SINGLE), gain_ref[...], back)
+        tokens_out_ref[part, :] = (grad[...] + back).astype(BFLOAT)
+
+
+def finish(tokens, gain, halves):
+    arrays = (tokens, gain[None, :], *(array for half in halves for array in half))
+    kinds = [(tokens.shape, BFLOAT)] * 2
+    return call_kernel(finish_kernel, "finish", HEAVY, 56, kinds, (), arrays)
 
 
 def split_kernel(value_ref, query_ref, key_ref, value_out_ref, out_ref):
@@ -728,8 +687,9 @@
             if step < len(tensor_bits) - 1:
                 last = step == len(tensor_bits) - 2
                 stays, aways = pair_sum(stays, gots, last, earlier)
+                first = stays[0] if step == 0 else first
                 earlier = ()
-        return [stay.astype(SINGLE) + got.astype(SINGLE) for stay, got in zip(stays, gots)], stays
+        return stays, gots, first
 
     def halves_of(value):
         return [value[:half_rows], value[half_rows:]]
@@ -756,14 +716,16 @@
     )
     attended_parts = wait_aways(attended_parts, cots[1], cots[3])
     residuals, normed_two = [], []
-    for token_part, sum_part in zip(halves_of(token_values), rows_scatter(attended_parts)[0]):
-        residuals.append(token_part + sum_part)
+    stays, gots, _ = rows_scatter(attended_parts)
+    for token_part, stay, got in zip(halves_of(token_values), stays, gots):
+        residuals.append(token_part + (stay + got.astype(SINGLE)))
         normed_two.append(rms_scale(residuals[-1], feedfwd_gain).astype(BFLOAT))
     gathered_two = rows_gather(normed_two)
 
     hidden, feedfwd_part, two_parts = feedfwd(gathered_two, cots, feedfwd_full)
     grad_feedfwd = lax.psum_scatter(feedfwd_part, "dp", scatter_dimension=0, tiled=True)
-    two_sums, _ = rows_scatter(two_parts)
+    stays, gots, _ = rows_scatter(two_parts)
+    two_sums = [stay + got.astype(SINGLE) for stay, got in zip(stays, gots)]
     grad_residual, gain_two_part = [], 0.0
     for residual_part, sum_part, cot_part in zip(residuals, two_sums, halves_of(cotangent)):
         back, gain_part = rms_back(residual_part, feedfwd_gain, sum_part)
@@ -773,34 +735,25 @@
     down_parts = down_parts_of(hidden, feedfwd_full, grad_low)
     gathered_grad = rows_gather(grad_low)
 
-    qkv_grad, head_gains, row_gain, normed_parts = attend_back(
-        sizes, place, gathered_grad, gathered, attention_full, gains, saved, down_parts[0]
-    )
-    down_sums, down_stays = rows_scatter(
-        wait_aways(down_parts, gathered_grad[1], gathered_grad[3])
-    )
-    attention_part = weight_parts(gathered, qkv_grad, gathered_grad, context, down_stays[0])
-    attention_part = later(attention_part, grad_feedfwd)
+    attention_part, head_gains, row_gain, normed_parts = attend_back(
+        sizes, place, gathered_grad, gathered, attention_full, gains, saved, context, down_parts[0]
+    )
+    down_stays, down_gots, down_first = rows_scatter(
+        wait_aways(down_parts, gathered_grad[1], gathered_grad[3]), (head_gains,)
+    )
+    attention_part = later(attention_part, grad_feedfwd, down_first)
     grad_attention = lax.psum_scatter(attention_part, "dp", scatter_dimension=0, tiled=True)
-    normed_sums, normed_stays = rows_scatter(normed_parts, (attention_part,))
-    grad_tokens = []
-    for token_part, sum_part, grad_part in zip(
-        halves_of(token_values), normed_sums, grad_residual
-    ):
-        back, _ = rms_back(token_part, attention_gain, sum_part)
-        grad_tokens.append((grad_part + back).astype(BFLOAT))
-
-    block_out = [(res + part).astype(BFLOAT) for res, part in zip(residuals, down_sums)]
+    normed_stays, normed_gots, normed_first = rows_scatter(normed_parts, (attention_part,))
 
     gain_parts = jnp.concatenate(
         [row_gain[0] / attention_gain, gain_two_part, *jnp.sum(head_gains, axis=2)]
     )
-    gain_sums = butterfly_sum(gain_parts + 0.0 * normed_stays[0][0, 0].astype(SINGLE))
+    gain_sums = butterfly_sum(gain_parts + 0.0 * normed_first[0, 0].astype(SINGLE))
     grad_feedfwd = grad_feedfwd.astype(SINGLE)
+    halves = [*zip(residuals, grad_residual, down_stays, down_gots, normed_stays, normed_gots)]
     shapes = [value.shape for value in (query_weight, key_weight, value_weight, out_weight)]
     return (
-        jnp.concatenate(block_out, axis=0),
-        jnp.concatenate(grad_tokens, axis=0),
+        *finish(tokens, attention_gain, halves),
         *split_weights(grad_attention, shapes),
         part_of(grad_feedfwd, 0),
         part_of(grad_feedfwd, 1),

time: 266 us -> 259 us (0.974)
  other arithmetic: 14.9 us -> 7.94 us
    pallas_call x1 -> x0, Pallas kernels: 7.03 us -> none  [weight_parts(): pl.pallas_call(partial(weights_kernel, first_tiles), grid=(columns // til...]
    pallas_call x8 -> x9, Pallas kernels: 40.2 us -> 45.4 us  [call_kernel(): pl.pallas_call(kernel, out_shape=[jax.ShapeDtypeStruct(*shape) for shape...]
    ppermute x37, waiting for transfers between devices: 80.4 us -> 83.7 us  [swap(): return lax.ppermute(value, axis, [(i, i ^ bit) for i in range(size)])]
    convert_element_type x3 -> x0, other arithmetic: 3.25 us -> none  [the longest x2 2 us: on_device(): (res + part).astype(BFLOAT)]
    reduce_scatter x1, waiting for transfers between devices: 4.08 us -> 0.88 us  [on_device(): lax.psum_scatter(attention_part, 'dp', scatter_dimension=0, tiled=True)]
    unnamed x104 -> x96, local copies, waits for them, and re-layouts: 11.6 us -> 11 us
  transfers between devices with their start and end apart: 41 -> 41, of which waited for: 22 -> 25; matrix products, arithmetic and copies ran while one was open for 8% -> 5% of each run, Pallas kernels for 19% -> 19%
where the time goes in v2:
time: 259 us
  waiting for transfers between devices  91.2 us (35%)
  Pallas kernels  82.5 us (32%)
  starting transfers between devices  43.9 us (17%)
  between operations  17.6 us (7%)
  local copies, waits for them, and re-layouts  15.5 us (6%)
  other arithmetic  7.94 us (3%)
    ppermute x37, waiting for transfers between devices, swap(): return lax.ppermute(value, axis, [(i, i ^ bit) for i in range(size)])  83.7 us
    pallas_call x9, Pallas kernels, call_kernel(): pl.pallas_call(kernel, out_shape=[jax.ShapeDtypeStruct(*shape) for shape...  45.4 us
    ppermute x37, starting transfers between devices, swap(): return lax.ppermute(value, axis, [(i, i ^ bit) for i in range(size)])  43.7 us
    pallas_call x1, Pallas kernels, feedfwd(): pl.pallas_call(feedfwd_kernel, grid=(hidden_cols // cols,), out_shape=[ja...  29.1 us
    unnamed x96, local copies, waits for them, and re-layouts  11 us
    pallas_call x1, Pallas kernels, down_parts_of(): pl.pallas_call(down_kernel, grid=(hidden_cols // cols,), out_shape=[jax.S...  7.99 us
    all_gather x1, waiting for transfers between devices, on_device(): lax.all_gather(interleave(gate_weight, up_weight, down_weight.T), 'dp', a...  6.4 us
  transfers between devices with their start and end apart: 41, of which 25 were waited for; matrix products, arithmetic and copies ran while one was open for 5% of the time, Pallas kernels for 19%

profile of v2, /device:TPU:0, one launch (start us, length us, event | category | flops | bytes accessed | tf_op | source)
XLA Modules:
  0.0 258.6 jit_solution(15848061388029506188)
XLA Ops:
  7.3 1.8 pack_weights.1
  9.6 1.0 copy-done.26
  11.1 3.0 %collective-permute-start = (bf16[128,1024]{1,0:T(8,128)(2,1)S(1)}, bf16[128,1024]{1,0:T(8,128)(2,1)S(1)}, u32[]{:S(2)}, u32[]{:S(2)}) collective-permute-start(bf16[128,1024]{1,0:T(8,128)(2,1)S(1)} %get-tuple-element.164), channel_id=1, source_target_pairs={{0,1},{1,0},{2,3},{3,2},{4,5},{5,4},{6,7},{7,6},{8,9},{9,8},{10,11... | collective-permute-start | bytes 786440 | tf_op jit(solution)/shard_map/ppermute | solution.py:617
  14.1 1.5 collective-permute-start.2
  15.6 4.8 %collective-permute-done = bf16[128,1024]{1,0:T(8,128)(2,1)S(1)} collective-permute-done((bf16[128,1024]{1,0:T(8,128)(2,1)S(1)}, bf16[128,1024]{1,0:T(8,128)(2,1)S(1)}, u32[]{:S(2)}, u32[]{:S(2)}) %collective-permute-start) | collective-permute-done | bytes 262176 | tf_op jit(solution)/shard_map/ppermute | solution.py:617
  20.5 1.8 collective-permute-start.1
  22.4 1.6 collective-permute-start.3
  24.6 1.1 collective-permute-start.6
  30.0 10.5 %collective-permute-done.4 = bf16[128,1024]{1,0:T(8,128)(2,1)S(1)} collective-permute-done((bf16[128,1024]{1,0:T(8,128)(2,1)S(1)}, bf16[128,1024]{1,0:T(8,128)(2,1)S(1)}, u32[]{:S(2)}, u32[]{:S(2)}) %collective-permute-start.4) | collective-permute-done | bytes 262176 | tf_op jit(solution)/shard_map/ppermute | solution.py:617
  41.4 1.1 collective-permute-start.5
  43.3 0.9 collective-permute-start.7
  44.3 16.7 %attend.1 = (f32[512,1024]{1,0:T(8,128)}, bf16[4,64,1024]{2,1,0:T(8,128)(2,1)}, bf16[2,64,1024]{2,1,0:T(8,128)(2,1)}, bf16[4,1024,64]{2,1,0:T(8,128)(2,1)}, bf16...) custom-call(s32[8]{0:T(128)} %stack.2.place_ref, ...), custom_call_target="tpu_custom_call" | custom-call | flops 16000000000 | bytes 1048576 | tf_op jit(solution)/shard_map/attend/pallas_call | solution.py:29
  62.0 0.9 collective-permute-start.9
  62.9 1.0 collective-permute-start.8
  63.8 9.4 %collective-permute-done.9.got_b_ref = bf16[256,1024]{1,0:T(8,128)(2,1)S(1)} collective-permute-done((bf16[256,1024]{1,0:T(8,128)(2,1)}, bf16[256,1024]{1,0:T(8,128)(2,1)S(1)}, u32[]{:S(2)}, u32[]{:S(2)}) %collective-permute-start.9) | collective-permute-done | bytes 524320 | tf_op jit(solution)/shard_map/ppermute | solution.py:617
  73.2 1.0 collective-permute-done.8.got_a_ref
  75.3 2.0 collective-permute-start.13
  77.4 4.4 %collective-permute-done.10 = bf16[128,1024]{1,0:T(8,128)(2,1)S(1)} collective-permute-done((bf16[128,1024]{1,0:T(8,128)(2,1)S(1)}, bf16[128,1024]{1,0:T(8,128)(2,1)S(1)}, u32[]{:S(2)}, u32[]{:S(2)}) %collective-permute-start.10) | collective-permute-done | bytes 262176 | tf_op jit(solution)/shard_map/ppermute | solution.py:617
  83.1 1.6 collective-permute-start.11
  84.7 1.0 collective-permute-start.14
  85.7 5.9 %collective-permute-done.11 = bf16[128,1024]{1,0:T(8,128)(2,1)S(1)} collective-permute-done((bf16[128,1024]{1,0:T(8,128)(2,1)S(1)}, bf16[128,1024]{1,0:T(8,128)(2,1)S(1)}, u32[]{:S(2)}, u32[]{:S(2)}) %collective-permute-start.11) | collective-permute-done | bytes 262176 | tf_op jit(solution)/shard_map/ppermute | solution.py:617
  91.6 3.1 %collective-permute-start.12 = (bf16[256,1024]{1,0:T(8,128)(2,1)S(1)}, bf16[256,1024]{1,0:T(8,128)(2,1)S(1)}, u32[]{:S(2)}, u32[]{:S(2)}) collective-permute-start(bf16[256,1024]{1,0:T(8,128)(2,1)S(1)} %pad_maximum_fusion.6.rows_a_ref), channel_id=1, source_target_pairs={{0,2},{1,3},{2,0},{3,1},{4,6},{5,7},{6,4},{7,5},{8,10},{9,11},{10,... | collective-permute-start | bytes 1572872 | tf_op jit(solution)/shard_map/ppermute | solution.py:617
  95.0 6.9 %collective-permute-done.12.rows_b_ref = bf16[256,1024]{1,0:T(8,128)(2,1)S(1)} collective-permute-done((bf16[256,1024]{1,0:T(8,128)(2,1)S(1)}, bf16[256,1024]{1,0:T(8,128)(2,1)S(1)}, u32[]{:S(2)}, u32[]{:S(2)}) %collective-permute-start.12) | collective-permute-done | bytes 524320 | tf_op jit(solution)/shard_map/ppermute | solution.py:617
  101.9 2.2 collective-permute-done.15.rows_d_ref
  104.1 6.4 %all-gather.5.cloned.1.call-done.weight_ref = bf16[1024,3456]{1,0:T(8,128)(2,1)} async-done(((bf16[128,3456]{1,0:T(8,128)(2,1)}), bf16[1024,3456]{1,0:T(8,128)(2,1)}) %all-gather.5.cloned.1.call-update) | async-done | bytes 7077904 | tf_op jit(solution)/shard_map/all_gather | solution.py:706
  110.5 29.1 %feedfwd.1 = (bf16[1024,1152]{1,0:T(8,128)(2,1)}, bf16[1024,3456]{1,0:T(8,128)(2,1)}, bf16[256,1024]{1,0:T(8,128)(2,1)}, bf16[256,1024]{1,0:T(8,128)(2,1)}, bf16...) custom-call(bf16[256,1024]{1,0:T(8,128)(2,1)} %copy-done.31, bf16[256,1024]{1,0:T(8,128)(2,1)} %copy-done.40, ...), custom_call_target="tpu_custom_call" | custom-call | flops 16000000000 | bytes 1048576 | tf_op jit(solution)/shard_map/feedfwd/pallas_call | solution.py:461
  139.8 1.5 collective-permute-start.16
  141.3 1.5 collective-permute-start.17
  142.8 11.3 %collective-permute-done.16.got_a_ref = bf16[256,1024]{1,0:T(8,128)(2,1)S(1)} collective-permute-done((bf16[256,1024]{1,0:T(8,128)(2,1)}, bf16[256,1024]{1,0:T(8,128)(2,1)S(1)}, u32[]{:S(2)}, u32[]{:S(2)}) %collective-permute-start.16) | collective-permute-done | bytes 524320 | tf_op jit(solution)/shard_map/ppermute | solution.py:617
  154.1 1.0 collective-permute-done.17.got_b_ref
  155.3 1.5 collective-permute-start.18
  156.9 1.1 collective-permute-start.19
  158.0 4.8 %collective-permute-done.18 = bf16[128,1024]{1,0:T(8,128)(2,1)S(1)} collective-permute-done((bf16[128,1024]{1,0:T(8,128)(2,1)S(1)}, bf16[128,1024]{1,0:T(8,128)(2,1)S(1)}, u32[]{:S(2)}, u32[]{:S(2)}) %collective-permute-start.18) | collective-permute-done | bytes 262176 | tf_op jit(solution)/shard_map/ppermute | solution.py:617
  162.8 1.2 collective-permute-done.19
  164.5 1.3 fusion.2
  166.4 1.5 collective-permute-start.22
  167.8 4.3 %collective-permute-done.20 = bf16[128,1024]{1,0:T(8,128)(2,1)S(1)} collective-permute-done((bf16[128,1024]{1,0:T(8,128)(2,1)S(1)}, bf16[128,1024]{1,0:T(8,128)(2,1)S(1)}, u32[]{:S(2)}, u32[]{:S(2)}) %collective-permute-start.20) | collective-permute-done | bytes 262176 | tf_op jit(solution)/shard_map/ppermute | solution.py:617
  172.2 1.8 collective-permute-start.21
  174.1 1.3 collective-permute-start.23
  175.4 8.0 %down_parts.1 = (bf16[256,1024]{1,0:T(8,128)(2,1)}, bf16[256,1024]{1,0:T(8,128)(2,1)}, bf16[256,1024]{1,0:T(8,128)(2,1)}, bf16[256,1024]{1,0:T(8,128)(2,1)}) custom-call(bf16[1024,1152]{1,0:T(8,128)(2,1)} %get-tuple-element.82.hidden_ref, bf16[1024,3456]{1,0:T(8,128)(2,1)} %all-gather.5.cloned.1.call-done.weight_ref, bf16[128,1024]{1,0:T(8,128)(2,1)} %copy-done.20, ...), custom_call_target="tpu_custom_call" | custom-call | flops 1000000000 | bytes 1048576 | tf_op jit(solution)/shard_map/down_parts/pallas_call | solution.py:532
  184.0 1.3 collective-permute-done.23.refs_2_.grad_d_ref
  186.5 1.4 collective-permute-start.25
  187.9 20.2 %attend_back.1 = (bf16[1024,768]{1,0:T(8,128)(2,1)}, f32[2,64,128]{2,1,0:T(8,128)}, f32[1,1024]{1,0:T(1,128)}, bf16[256,1024]{1,0:T(8,128)(2,1)}, bf16[256,1024]...) custom-call(s32[8]{0:T(128)} %stack.2.place_ref, bf16[256,1024]{1,0:T(8,128)(2,1)} %copy-done.29, ...), custom_call_target="tpu_custom_call" | custom-call | flops 16000000000 | bytes 1048576 | tf_op jit(solution)/shard_map/attend_back/pallas_call | solution.py:29
  208.9 1.5 collective-permute-start.28
  211.1 0.9 reduce_sum.87
  215.7 3.6 %collective-permute-done.27.got_a_ref = bf16[256,1024]{1,0:T(8,128)(2,1)S(1)} collective-permute-done((bf16[256,1024]{1,0:T(8,128)(2,1)}, bf16[256,1024]{1,0:T(8,128)(2,1)S(1)}, u32[]{:S(2)}, u32[]{:S(2)}) %collective-permute-start.27) | collective-permute-done | bytes 524320 | tf_op jit(solution)/shard_map/ppermute | solution.py:617
  219.9 1.4 copy-done
  221.3 1.1 copy-done.9
  222.4 1.0 copy-done.10
  225.0 1.2 collective-permute-done.32
  226.5 1.2 collective-permute-start.30
  227.7 1.7 collective-permute-start.29
  229.4 0.9 collective-permute-start.31
  230.3 1.4 collective-permute-start.34
  231.7 1.4 fusion.4
  233.1 2.3 collective-permute-done.34
  235.5 1.1 pad_maximum_fusion
  236.6 3.9 %collective-permute-done.35 = f32[2176]{0:T(1024)S(1)} collective-permute-done((f32[2176]{0:T(1024)S(1)}, f32[2176]{0:T(1024)S(1)}, u32[]{:S(2)}, u32[]{:S(2)}) %collective-permute-start.35) | collective-permute-done | bytes 8736 | tf_op jit(solution)/shard_map/ppermute | solution.py:617
  240.5 1.1 collective-permute-start.36
  241.6 1.1 copy.41
  242.7 1.5 collective-permute-done.36
  245.4 4.1 %finish.1 = (bf16[256,1024]{1,0:T(8,128)(2,1)}, bf16[256,1024]{1,0:T(8,128)(2,1)}) custom-call(bf16[256,1024]{1,0:T(8,128)(2,1)} %tokens_ref.1, f32[1,1024]{1,0:T(1,128)} %bitcast.20, f32[128,1024]{1,0:T(8,128)} %copy-done.17, f32[128,1024]{1,0:T(8,128)} %get-tuple-element.160.refs_1_, f32[128,1024]{1,0:T(8,128)} %copy-done.1, ...), custom_call_target="tpu_custom_call" | custom-call | flops 16000000000 | bytes 1048576 | tf_op jit(solution)/shard_map/finish/pallas_call | solution.py:29
  249.5 0.9 reduce-scatter.5.cloned.1.call-done.value_ref
  250.4 1.7 split_weights.1
  (176 shorter events, 20.1 us)
Async XLA Ops:
  7.2 37.1 %all-gather.3.cloned.1.call-start = ((), (), s32[]{:S(2)}) async-start(), calls=%async_computation.2 | async-start | bytes 1769472 | tf_op jit(solution)/shard_map/all_gather | solution.py:700
  9.0 101.5 %all-gather.5.cloned.1.call-start = ((), (), s32[]{:S(2)}) async-start(), calls=%async_computation.3 | async-start | bytes 7962624 | tf_op jit(solution)/shard_map/all_gather | solution.py:706
  10.6 205.1 %reduce-scatter.3.cloned.1.call-start = ((), (), s32[]{:S(2)}) async-start(), calls=%async_computation.4 | async-start | bytes 7962624 | tf_op jit(solution)/shard_map/reduce_scatter | solution.py:726
  10.8 13.1 %copy-start.21 = (bf16[256,1024]{1,0:T(8,128)(2,1)S(1)}, bf16[256,1024]{1,0:T(8,128)(2,1)}, u32[]{:S(2)}) copy-start(bf16[256,1024]{1,0:T(8,128)(2,1)} %param.24) | copy-start | bytes 1572868
  11.0 14.6 %copy-start.38 = (s32[4]{0:T(128)S(1)}, s32[4]{0:T(128)}, u32[]{:S(2)}) copy-start(s32[4]{0:T(128)} %constant.49.clone) | copy-start | bytes 52
  11.0 18.4 %copy-start.41 = (f32[64]{0:T(128)S(1)}, f32[64]{0:T(128)}, u32[]{:S(2)}) copy-start(f32[64]{0:T(128)} %param.35) | copy-start | bytes 772
  11.1 18.4 %copy-start.42 = (f32[64]{0:T(128)S(1)}, f32[64]{0:T(128)}, u32[]{:S(2)}) copy-start(f32[64]{0:T(128)} %param.34) | copy-start | bytes 772
  11.1 9.3 %collective-permute-start = (bf16[128,1024]{1,0:T(8,128)(2,1)S(1)}, bf16[128,1024]{1,0:T(8,128)(2,1)S(1)}, u32[]{:S(2)}, u32[]{:S(2)}) collective-permute-start(bf16[128,1024]{1,0:T(8,128)(2,1)S(1)} %get-tuple-element.164), channel_id=1, source_target_pairs={{0,1},{1,0},{2,3},{3,2},{4,5},{5,4},{6,7},{7,6},{8,9},{9,8},{10,11... | collective-permute-start | bytes 786440 | tf_op jit(solution)/shard_map/ppermute | solution.py:617
  14.1 8.2 %collective-permute-start.2 = (bf16[128,1024]{1,0:T(8,128)(2,1)S(1)}, bf16[128,1024]{1,0:T(8,128)(2,1)S(1)}, u32[]{:S(2)}, u32[]{:S(2)}) collective-permute-start(bf16[128,1024]{1,0:T(8,128)(2,1)S(1)} %get-tuple-element.163), channel_id=1, source_target_pairs={{0,2},{1,3},{2,0},{3,1},{4,6},{5,7},{6,4},{7,5},{8,10},{9,11},{10,... | collective-permute-start | bytes 786440 | tf_op jit(solution)/shard_map/ppermute | solution.py:617
  20.5 22.9 %copy-start.27 = (bf16[256,1024]{1,0:T(8,128)(2,1)}, bf16[256,1024]{1,0:T(8,128)(2,1)S(1)}, u32[]{:S(2)}) copy-start(bf16[256,1024]{1,0:T(8,128)(2,1)S(1)} %pad_maximum_fusion.2.rows_a_ref) | copy-start | bytes 1572868
  20.5 23.8 %collective-permute-start.1 = (bf16[256,1024]{1,0:T(8,128)(2,1)S(1)}, bf16[256,1024]{1,0:T(8,128)(2,1)}, u32[]{:S(2)}, u32[]{:S(2)}) collective-permute-start(bf16[256,1024]{1,0:T(8,128)(2,1)S(1)} %pad_maximum_fusion.2.rows_a_ref), channel_id=1, source_target_pairs={{0,2},{1,3},{2,0},{3,1},{4,6},{5,7},{6,4},{7,5},{8,10},{9,11},{10,... | collective-permute-start | bytes 1572872 | tf_op jit(solution)/shard_map/ppermute | solution.py:617
  22.3 21.9 %copy-start.28 = (bf16[256,1024]{1,0:T(8,128)(2,1)}, bf16[256,1024]{1,0:T(8,128)(2,1)S(1)}, u32[]{:S(2)}) copy-start(bf16[256,1024]{1,0:T(8,128)(2,1)S(1)} %pad_maximum_fusion.3.rows_c_ref) | copy-start | bytes 1572868
  22.4 21.9 %collective-permute-start.3 = (bf16[256,1024]{1,0:T(8,128)(2,1)S(1)}, bf16[256,1024]{1,0:T(8,128)(2,1)}, u32[]{:S(2)}, u32[]{:S(2)}) collective-permute-start(bf16[256,1024]{1,0:T(8,128)(2,1)S(1)} %pad_maximum_fusion.3.rows_c_ref), channel_id=1, source_target_pairs={{0,1},{1,0},{2,3},{3,2},{4,5},{5,4},{6,7},{7,6},{8,9},{9,8},{10,11... | collective-permute-start | bytes 1572872 | tf_op jit(solution)/shard_map/ppermute | solution.py:617
  24.0 16.6 %collective-permute-start.4 = (bf16[128,1024]{1,0:T(8,128)(2,1)S(1)}, bf16[128,1024]{1,0:T(8,128)(2,1)S(1)}, u32[]{:S(2)}, u32[]{:S(2)}) collective-permute-start(bf16[128,1024]{1,0:T(8,128)(2,1)S(1)} %get-tuple-element.162), channel_id=1, source_target_pairs={{0,1},{1,0},{2,3},{3,2},{4,5},{5,4},{6,7},{7,6},{8,9},{9,8},{10,11... | collective-permute-start | bytes 786440 | tf_op jit(solution)/shard_map/ppermute | solution.py:617
  24.6 17.9 %collective-permute-start.6 = (bf16[128,1024]{1,0:T(8,128)(2,1)S(1)}, bf16[128,1024]{1,0:T(8,128)(2,1)S(1)}, u32[]{:S(2)}, u32[]{:S(2)}) collective-permute-start(bf16[128,1024]{1,0:T(8,128)(2,1)S(1)} %get-tuple-element.161), channel_id=1, source_target_pairs={{0,2},{1,3},{2,0},{3,1},{4,6},{5,7},{6,4},{7,5},{8,10},{9,11},{10,... | collective-permute-start | bytes 786440 | tf_op jit(solution)/shard_map/ppermute | solution.py:617
  41.4 19.6 %collective-permute-start.5 = (bf16[256,1024]{1,0:T(8,128)(2,1)}, bf16[256,1024]{1,0:T(8,128)(2,1)S(1)}, u32[]{:S(2)}, u32[]{:S(2)}) collective-permute-start(bf16[256,1024]{1,0:T(8,128)(2,1)} %pad_maximum_fusion.4.cot_a_ref), channel_id=1, source_target_pairs={{0,2},{1,3},{2,0},{3,1},{4,6},{5,7},{6,4},{7,5},{8,10},{9,11},{10,... | collective-permute-start | bytes 1572872 | tf_op jit(solution)/shard_map/ppermute | solution.py:617
  43.3 17.7 %collective-permute-start.7 = (bf16[256,1024]{1,0:T(8,128)(2,1)}, bf16[256,1024]{1,0:T(8,128)(2,1)S(1)}, u32[]{:S(2)}, u32[]{:S(2)}) collective-permute-start(bf16[256,1024]{1,0:T(8,128)(2,1)} %pad_maximum_fusion.5.cot_c_ref), channel_id=1, source_target_pairs={{0,1},{1,0},{2,3},{3,2},{4,5},{5,4},{6,7},{7,6},{8,9},{9,8},{10,11... | collective-permute-start | bytes 1572872 | tf_op jit(solution)/shard_map/ppermute | solution.py:617
  62.0 12.2 %copy-start.12 = (bf16[256,1024]{1,0:T(8,128)(2,1)S(1)}, bf16[256,1024]{1,0:T(8,128)(2,1)}, u32[]{:S(2)}) copy-start(bf16[256,1024]{1,0:T(8,128)(2,1)} %get-tuple-element.68.stay_a_ref) | copy-start | bytes 1572868
  62.0 12.2 %copy-start.13 = (bf16[256,1024]{1,0:T(8,128)(2,1)S(1)}, bf16[256,1024]{1,0:T(8,128)(2,1)}, u32[]{:S(2)}) copy-start(bf16[256,1024]{1,0:T(8,128)(2,1)} %get-tuple-element.70.stay_b_ref) | copy-start | bytes 1572868
  62.0 11.2 %collective-permute-start.9 = (bf16[256,1024]{1,0:T(8,128)(2,1)}, bf16[256,1024]{1,0:T(8,128)(2,1)S(1)}, u32[]{:S(2)}, u32[]{:S(2)}) collective-permute-start(bf16[256,1024]{1,0:T(8,128)(2,1)} %later.6), channel_id=1, source_target_pairs={{0,1},{1,0},{2,3},{3,2},{4,5},{5,4},{6,7},{7,6},{8,9},{9,8},{10,11... | collective-permute-start | bytes 1572872 | tf_op jit(solution)/shard_map/ppermute | solution.py:617
  62.9 11.4 %collective-permute-start.8 = (bf16[256,1024]{1,0:T(8,128)(2,1)}, bf16[256,1024]{1,0:T(8,128)(2,1)S(1)}, u32[]{:S(2)}, u32[]{:S(2)}) collective-permute-start(bf16[256,1024]{1,0:T(8,128)(2,1)} %later.5), channel_id=1, source_target_pairs={{0,2},{1,3},{2,0},{3,1},{4,6},{5,7},{6,4},{7,5},{8,10},{9,11},{10,... | collective-permute-start | bytes 1572872 | tf_op jit(solution)/shard_map/ppermute | solution.py:617
  74.5 7.3 %collective-permute-start.10 = (bf16[128,1024]{1,0:T(8,128)(2,1)S(1)}, bf16[128,1024]{1,0:T(8,128)(2,1)S(1)}, u32[]{:S(2)}, u32[]{:S(2)}) collective-permute-start(bf16[128,1024]{1,0:T(8,128)(2,1)S(1)} %get-tuple-element.73), channel_id=1, source_target_pairs={{0,1},{1,0},{2,3},{3,2},{4,5},{5,4},{6,7},{7,6},{8,9},{9,8},{10,11... | collective-permute-start | bytes 786440 | tf_op jit(solution)/shard_map/ppermute | solution.py:617
  75.3 7.3 %collective-permute-start.13 = (bf16[128,1024]{1,0:T(8,128)(2,1)S(1)}, bf16[128,1024]{1,0:T(8,128)(2,1)S(1)}, u32[]{:S(2)}, u32[]{:S(2)}) collective-permute-start(bf16[128,1024]{1,0:T(8,128)(2,1)S(1)} %get-tuple-element.75), channel_id=1, source_target_pairs={{0,2},{1,3},{2,0},{3,1},{4,6},{5,7},{6,4},{7,5},{8,10},{9,11},{10,... | collective-permute-start | bytes 786440 | tf_op jit(solution)/shard_map/ppermute | solution.py:617
  82.9 81.6 %copy-start.16 = (f32[128,1024]{1,0:T(8,128)}, f32[128,1024]{1,0:T(8,128)S(1)}, u32[]{:S(2)}) copy-start(f32[128,1024]{1,0:T(8,128)S(1)} %get-tuple-element.145.refs_6_) | copy-start | bytes 1572868
  82.9 81.6 %copy-start.17 = (f32[128,1024]{1,0:T(8,128)}, f32[128,1024]{1,0:T(8,128)S(1)}, u32[]{:S(2)}) copy-start(f32[128,1024]{1,0:T(8,128)S(1)} %get-tuple-element.149.refs_0_) | copy-start | bytes 1572868
  83.1 8.5 %collective-permute-start.11 = (bf16[128,1024]{1,0:T(8,128)(2,1)S(1)}, bf16[128,1024]{1,0:T(8,128)(2,1)S(1)}, u32[]{:S(2)}, u32[]{:S(2)}) collective-permute-start(bf16[128,1024]{1,0:T(8,128)(2,1)S(1)} %get-tuple-element.172), channel_id=1, source_target_pairs={{0,1},{1,0},{2,3},{3,2},{4,5},{5,4},{6,7},{7,6},{8,9},{9,8},{10,11... | collective-permute-start | bytes 786440 | tf_op jit(solution)/shard_map/ppermute | solution.py:617
  84.7 10.1 %collective-permute-start.14 = (bf16[128,1024]{1,0:T(8,128)(2,1)S(1)}, bf16[128,1024]{1,0:T(8,128)(2,1)S(1)}, u32[]{:S(2)}, u32[]{:S(2)}) collective-permute-start(bf16[128,1024]{1,0:T(8,128)(2,1)S(1)} %get-tuple-element.171), channel_id=1, source_target_pairs={{0,2},{1,3},{2,0},{3,1},{4,6},{5,7},{6,4},{7,5},{8,10},{9,11},{10,... | collective-permute-start | bytes 786440 | tf_op jit(solution)/shard_map/ppermute | solution.py:617
  91.6 18.9 %copy-start.31 = (bf16[256,1024]{1,0:T(8,128)(2,1)}, bf16[256,1024]{1,0:T(8,128)(2,1)S(1)}, u32[]{:S(2)}) copy-start(bf16[256,1024]{1,0:T(8,128)(2,1)S(1)} %pad_maximum_fusion.6.rows_a_ref) | copy-start | bytes 1572868
  91.6 10.3 %collective-permute-start.12 = (bf16[256,1024]{1,0:T(8,128)(2,1)S(1)}, bf16[256,1024]{1,0:T(8,128)(2,1)S(1)}, u32[]{:S(2)}, u32[]{:S(2)}) collective-permute-start(bf16[256,1024]{1,0:T(8,128)(2,1)S(1)} %pad_maximum_fusion.6.rows_a_ref), channel_id=1, source_target_pairs={{0,2},{1,3},{2,0},{3,1},{4,6},{5,7},{6,4},{7,5},{8,10},{9,11},{10,... | collective-permute-start | bytes 1572872 | tf_op jit(solution)/shard_map/ppermute | solution.py:617
  94.8 15.8 %copy-start.32 = (bf16[256,1024]{1,0:T(8,128)(2,1)}, bf16[256,1024]{1,0:T(8,128)(2,1)S(1)}, u32[]{:S(2)}) copy-start(bf16[256,1024]{1,0:T(8,128)(2,1)S(1)} %pad_maximum_fusion.7.rows_c_ref) | copy-start | bytes 1572868
  94.8 9.4 %collective-permute-start.15 = (bf16[256,1024]{1,0:T(8,128)(2,1)S(1)}, bf16[256,1024]{1,0:T(8,128)(2,1)}, u32[]{:S(2)}, u32[]{:S(2)}) collective-permute-start(bf16[256,1024]{1,0:T(8,128)(2,1)S(1)} %pad_maximum_fusion.7.rows_c_ref), channel_id=1, source_target_pairs={{0,1},{1,0},{2,3},{3,2},{4,5},{5,4},{6,7},{7,6},{8,9},{9,8},{10,11... | collective-permute-start | bytes 1572872 | tf_op jit(solution)/shard_map/ppermute | solution.py:617
  139.7 15.4 %copy-start.14 = (bf16[256,1024]{1,0:T(8,128)(2,1)S(1)}, bf16[256,1024]{1,0:T(8,128)(2,1)}, u32[]{:S(2)}) copy-start(bf16[256,1024]{1,0:T(8,128)(2,1)} %get-tuple-element.76.stay_a_ref) | copy-start | bytes 1572868
  139.7 15.4 %copy-start.15 = (bf16[256,1024]{1,0:T(8,128)(2,1)S(1)}, bf16[256,1024]{1,0:T(8,128)(2,1)}, u32[]{:S(2)}) copy-start(bf16[256,1024]{1,0:T(8,128)(2,1)} %get-tuple-element.78.stay_b_ref) | copy-start | bytes 1572868
  139.7 110.7 %reduce-scatter.5.cloned.1.call-start = ((), (), s32[]{:S(2)}) async-start(), calls=%async_computation.5 | async-start | bytes 1769472 | tf_op jit(solution)/shard_map/reduce_scatter | solution.py:745
  139.8 14.3 %collective-permute-start.16 = (bf16[256,1024]{1,0:T(8,128)(2,1)}, bf16[256,1024]{1,0:T(8,128)(2,1)S(1)}, u32[]{:S(2)}, u32[]{:S(2)}) collective-permute-start(bf16[256,1024]{1,0:T(8,128)(2,1)} %get-tuple-element.77), channel_id=1, source_target_pairs={{0,2},{1,3},{2,0},{3,1},{4,6},{5,7},{6,4},{7,5},{8,10},{9,11},{10,... | collective-permute-start | bytes 1572872 | tf_op jit(solution)/shard_map/ppermute | solution.py:617
  141.3 13.8 %collective-permute-start.17 = (bf16[256,1024]{1,0:T(8,128)(2,1)S(1)}, bf16[256,1024]{1,0:T(8,128)(2,1)S(1)}, u32[]{:S(2)}, u32[]{:S(2)}) collective-permute-start(bf16[256,1024]{1,0:T(8,128)(2,1)S(1)} %copy-done.39), channel_id=1, source_target_pairs={{0,1},{1,0},{2,3},{3,2},{4,5},{5,4},{6,7},{7,6},{8,9},{9,8},{10,11... | collective-permute-start | bytes 1572872 | tf_op jit(solution)/shard_map/ppermute | solution.py:617
  155.3 7.5 %collective-permute-start.18 = (bf16[128,1024]{1,0:T(8,128)(2,1)S(1)}, bf16[128,1024]{1,0:T(8,128)(2,1)S(1)}, u32[]{:S(2)}, u32[]{:S(2)}) collective-permute-start(bf16[128,1024]{1,0:T(8,128)(2,1)S(1)} %get-tuple-element.81), channel_id=1, source_target_pairs={{0,1},{1,0},{2,3},{3,2},{4,5},{5,4},{6,7},{7,6},{8,9},{9,8},{10,11... | collective-permute-start | bytes 786440 | tf_op jit(solution)/shard_map/ppermute | solution.py:617
  156.9 7.1 %collective-permute-start.19 = (bf16[128,1024]{1,0:T(8,128)(2,1)S(1)}, bf16[128,1024]{1,0:T(8,128)(2,1)S(1)}, u32[]{:S(2)}, u32[]{:S(2)}) collective-permute-start(bf16[128,1024]{1,0:T(8,128)(2,1)S(1)} %get-tuple-element.84), channel_id=1, source_target_pairs={{0,2},{1,3},{2,0},{3,1},{4,6},{5,7},{6,4},{7,5},{8,10},{9,11},{10,... | collective-permute-start | bytes 786440 | tf_op jit(solution)/shard_map/ppermute | solution.py:617
  165.8 9.6 %copy-start.19 = (bf16[128,1024]{1,0:T(8,128)(2,1)}, bf16[128,1024]{1,0:T(8,128)(2,1)S(1)}, u32[]{:S(2)}) copy-start(bf16[128,1024]{1,0:T(8,128)(2,1)S(1)} %get-tuple-element.140.refs_1_) | copy-start | bytes 786436
  165.8 9.6 %copy-start.20 = (bf16[128,1024]{1,0:T(8,128)(2,1)}, bf16[128,1024]{1,0:T(8,128)(2,1)S(1)}, u32[]{:S(2)}) copy-start(bf16[128,1024]{1,0:T(8,128)(2,1)S(1)} %get-tuple-element.159.refs_0_) | copy-start | bytes 786436
  165.8 6.4 %collective-permute-start.20 = (bf16[128,1024]{1,0:T(8,128)(2,1)S(1)}, bf16[128,1024]{1,0:T(8,128)(2,1)S(1)}, u32[]{:S(2)}, u32[]{:S(2)}) collective-permute-start(bf16[128,1024]{1,0:T(8,128)(2,1)S(1)} %get-tuple-element.159.refs_0_), channel_id=1, source_target_pairs={{0,1},{1,0},{2,3},{3,2},{4,5},{5,4},{6,7},{7,6},{8,9},{9,8},{10,11... | collective-permute-start | bytes 786440 | tf_op jit(solution)/shard_map/ppermute | solution.py:617
  166.4 7.7 %collective-permute-start.22 = (bf16[128,1024]{1,0:T(8,128)(2,1)S(1)}, bf16[128,1024]{1,0:T(8,128)(2,1)S(1)}, u32[]{:S(2)}, u32[]{:S(2)}) collective-permute-start(bf16[128,1024]{1,0:T(8,128)(2,1)S(1)} %get-tuple-element.140.refs_1_), channel_id=1, source_target_pairs={{0,2},{1,3},{2,0},{3,1},{4,6},{5,7},{6,4},{7,5},{8,10},{9,11},{10,... | collective-permute-start | bytes 786440 | tf_op jit(solution)/shard_map/ppermute | solution.py:617
  172.2 11.2 %copy-start.29 = (bf16[256,1024]{1,0:T(8,128)(2,1)}, bf16[256,1024]{1,0:T(8,128)(2,1)S(1)}, u32[]{:S(2)}) copy-start(bf16[256,1024]{1,0:T(8,128)(2,1)S(1)} %pad_maximum_fusion.8.grad_a_ref) | copy-start | bytes 1572868
  172.2 11.7 %collective-permute-start.21 = (bf16[256,1024]{1,0:T(8,128)(2,1)S(1)}, bf16[256,1024]{1,0:T(8,128)(2,1)S(1)}, u32[]{:S(2)}, u32[]{:S(2)}) collective-permute-start(bf16[256,1024]{1,0:T(8,128)(2,1)S(1)} %pad_maximum_fusion.8.grad_a_ref), channel_id=1, source_target_pairs={{0,2},{1,3},{2,0},{3,1},{4,6},{5,7},{6,4},{7,5},{8,10},{9,11},{10,... | collective-permute-start | bytes 1572872 | tf_op jit(solution)/shard_map/ppermute | solution.py:617
  174.1 9.3 %copy-start.30 = (bf16[256,1024]{1,0:T(8,128)(2,1)}, bf16[256,1024]{1,0:T(8,128)(2,1)S(1)}, u32[]{:S(2)}) copy-start(bf16[256,1024]{1,0:T(8,128)(2,1)S(1)} %pad_maximum_fusion.9.grad_c_ref) | copy-start | bytes 1572868
  174.1 11.2 %collective-permute-start.23 = (bf16[256,1024]{1,0:T(8,128)(2,1)S(1)}, bf16[256,1024]{1,0:T(8,128)(2,1)S(1)}, u32[]{:S(2)}, u32[]{:S(2)}) collective-permute-start(bf16[256,1024]{1,0:T(8,128)(2,1)S(1)} %pad_maximum_fusion.9.grad_c_ref), channel_id=1, source_target_pairs={{0,1},{1,0},{2,3},{3,2},{4,5},{5,4},{6,7},{7,6},{8,9},{9,8},{10,11... | collective-permute-start | bytes 1572872 | tf_op jit(solution)/shard_map/ppermute | solution.py:617
  186.1 26.0 %collective-permute-start.24 = (bf16[256,1024]{1,0:T(8,128)(2,1)}, bf16[256,1024]{1,0:T(8,128)(2,1)S(1)}, u32[]{:S(2)}, u32[]{:S(2)}) collective-permute-start(bf16[256,1024]{1,0:T(8,128)(2,1)} %later.7), channel_id=1, source_target_pairs={{0,2},{1,3},{2,0},{3,1},{4,6},{5,7},{6,4},{7,5},{8,10},{9,11},{10,... | collective-permute-start | bytes 1572872 | tf_op jit(solution)/shard_map/ppermute | solution.py:617
  186.5 25.7 %collective-permute-start.25 = (bf16[256,1024]{1,0:T(8,128)(2,1)}, bf16[256,1024]{1,0:T(8,128)(2,1)S(1)}, u32[]{:S(2)}, u32[]{:S(2)}) collective-permute-start(bf16[256,1024]{1,0:T(8,128)(2,1)} %later.8), channel_id=1, source_target_pairs={{0,1},{1,0},{2,3},{3,2},{4,5},{5,4},{6,7},{7,6},{8,9},{9,8},{10,11... | collective-permute-start | bytes 1572872 | tf_op jit(solution)/shard_map/ppermute | solution.py:617
  187.9 24.2 %copy-start.3 = (bf16[256,1024]{1,0:T(8,128)(2,1)S(1)}, bf16[256,1024]{1,0:T(8,128)(2,1)}, u32[]{:S(2)}) copy-start(bf16[256,1024]{1,0:T(8,128)(2,1)} %get-tuple-element.85.earlier_ref.stay_a_ref) | copy-start | bytes 1572868
  187.9 24.2 %copy-start.4 = (bf16[256,1024]{1,0:T(8,128)(2,1)S(1)}, bf16[256,1024]{1,0:T(8,128)(2,1)}, u32[]{:S(2)}) copy-start(bf16[256,1024]{1,0:T(8,128)(2,1)} %get-tuple-element.87.stay_b_ref) | copy-start | bytes 1572868
  208.1 11.2 %collective-permute-start.27 = (bf16[256,1024]{1,0:T(8,128)(2,1)}, bf16[256,1024]{1,0:T(8,128)(2,1)S(1)}, u32[]{:S(2)}, u32[]{:S(2)}) collective-permute-start(bf16[256,1024]{1,0:T(8,128)(2,1)} %get-tuple-element.105), channel_id=1, source_target_pairs={{0,2},{1,3},{2,0},{3,1},{4,6},{5,7},{6,4},{7,5},{8,10},{9,11},{10,... | collective-permute-start | bytes 1572872 | tf_op jit(solution)/shard_map/ppermute | solution.py:617
  208.9 11.0 %collective-permute-start.28 = (bf16[256,1024]{1,0:T(8,128)(2,1)}, bf16[256,1024]{1,0:T(8,128)(2,1)S(1)}, u32[]{:S(2)}, u32[]{:S(2)}) collective-permute-start(bf16[256,1024]{1,0:T(8,128)(2,1)} %get-tuple-element.107), channel_id=1, source_target_pairs={{0,1},{1,0},{2,3},{3,2},{4,5},{5,4},{6,7},{7,6},{8,9},{9,8},{10,11... | collective-permute-start | bytes 1572872 | tf_op jit(solution)/shard_map/ppermute | solution.py:617
  215.7 10.5 %copy-start.6 = (bf16[128,1024]{1,0:T(8,128)(2,1)S(1)}, bf16[128,1024]{1,0:T(8,128)(2,1)}, u32[]{:S(2)}) copy-start(bf16[128,1024]{1,0:T(8,128)(2,1)} %copy-done.5) | copy-start | bytes 786436
  223.7 12.9 %copy-start.7 = (f32[128,1024]{1,0:T(8,128)}, f32[128,1024]{1,0:T(8,128)S(1)}, u32[]{:S(2)}) copy-start(f32[128,1024]{1,0:T(8,128)S(1)} %get-tuple-element.110.refs_4_) | copy-start | bytes 1572868
  223.7 12.9 %copy-start.8 = (f32[128,1024]{1,0:T(8,128)}, f32[128,1024]{1,0:T(8,128)S(1)}, u32[]{:S(2)}) copy-start(f32[128,1024]{1,0:T(8,128)S(1)} %get-tuple-element.114.refs_10_) | copy-start | bytes 1572868
  224.9 1.2 collective-permute-start.32
  226.2 4.1 %collective-permute-start.33 = (f32[2176]{0:T(1024)S(1)}, f32[2176]{0:T(1024)S(1)}, u32[]{:S(2)}, u32[]{:S(2)}) collective-permute-start(f32[2176]{0:T(1024)S(1)} %fusion.10), channel_id=1, source_target_pairs={{0,8},{4,12},{8,0},{12,4},{16,24},{20,28},{24,16},{28,20},{1,9},{5... | collective-permute-start | bytes 26120 | tf_op jit(solution)/shard_map/ppermute | solution.py:617
  226.2 19.2 %collective-permute-start.26 = (bf16[128,1024]{1,0:T(8,128)(2,1)S(1)}, bf16[128,1024]{1,0:T(8,128)(2,1)}, u32[]{:S(2)}, u32[]{:S(2)}) collective-permute-start(bf16[128,1024]{1,0:T(8,128)(2,1)S(1)} %copy-done.6), channel_id=1, source_target_pairs={{0,1},{1,0},{2,3},{3,2},{4,5},{5,4},{6,7},{7,6},{8,9},{9,8},{10,11... | collective-permute-start | bytes 786440 | tf_op jit(solution)/shard_map/ppermute | solution.py:617
  226.5 18.9 %collective-permute-start.30 = (bf16[128,1024]{1,0:T(8,128)(2,1)S(1)}, bf16[128,1024]{1,0:T(8,128)(2,1)}, u32[]{:S(2)}, u32[]{:S(2)}) collective-permute-start(bf16[128,1024]{1,0:T(8,128)(2,1)S(1)} %get-tuple-element.113), channel_id=1, source_target_pairs={{0,2},{1,3},{2,0},{3,1},{4,6},{5,7},{6,4},{7,5},{8,10},{9,11},{10,... | collective-permute-start | bytes 786440 | tf_op jit(solution)/shard_map/ppermute | solution.py:617
  227.7 17.7 %collective-permute-start.29 = (bf16[128,1024]{1,0:T(8,128)(2,1)S(1)}, bf16[128,1024]{1,0:T(8,128)(2,1)}, u32[]{:S(2)}, u32[]{:S(2)}) collective-permute-start(bf16[128,1024]{1,0:T(8,128)(2,1)S(1)} %get-tuple-element.111), channel_id=1, source_target_pairs={{0,1},{1,0},{2,3},{3,2},{4,5},{5,4},{6,7},{7,6},{8,9},{9,8},{10,11... | collective-permute-start | bytes 786440 | tf_op jit(solution)/shard_map/ppermute | solution.py:617
  229.4 16.1 %collective-permute-start.31 = (bf16[128,1024]{1,0:T(8,128)(2,1)S(1)}, bf16[128,1024]{1,0:T(8,128)(2,1)}, u32[]{:S(2)}, u32[]{:S(2)}) collective-permute-start(bf16[128,1024]{1,0:T(8,128)(2,1)S(1)} %get-tuple-element.115), channel_id=1, source_target_pairs={{0,2},{1,3},{2,0},{3,1},{4,6},{5,7},{6,4},{7,5},{8,10},{9,11},{10,... | collective-permute-start | bytes 786440 | tf_op jit(solution)/shard_map/ppermute | solution.py:617
  230.3 5.2 %collective-permute-start.34 = (f32[2176]{0:T(1024)S(1)}, f32[2176]{0:T(1024)S(1)}, u32[]{:S(2)}, u32[]{:S(2)}) collective-permute-start(f32[2176]{0:T(1024)S(1)} %add.143), channel_id=1, source_target_pairs={{0,16},{4,20},{8,24},{12,28},{16,0},{20,4},{24,8},{28,12},{1,17},{... | collective-permute-start | bytes 26120 | tf_op jit(solution)/shard_map/ppermute | solution.py:617
  235.5 5.0 %collective-permute-start.35 = (f32[2176]{0:T(1024)S(1)}, f32[2176]{0:T(1024)S(1)}, u32[]{:S(2)}, u32[]{:S(2)}) collective-permute-start(f32[2176]{0:T(1024)S(1)} %add.144), channel_id=1, source_target_pairs={{0,1},{1,0},{2,3},{3,2},{4,5},{5,4},{6,7},{7,6},{8,9},{9,8},{10,11... | collective-permute-start | bytes 26120 | tf_op jit(solution)/shard_map/ppermute | solution.py:617
  240.5 3.7 %collective-permute-start.36 = (f32[2176]{0:T(1024)S(1)}, f32[2176]{0:T(1024)S(1)}, u32[]{:S(2)}, u32[]{:S(2)}) collective-permute-start(f32[2176]{0:T(1024)S(1)} %add.145), channel_id=1, source_target_pairs={{0,2},{1,3},{2,0},{3,1},{4,6},{5,7},{6,4},{7,5},{8,10},{9,11},{10,... | collective-permute-start | bytes 26120 | tf_op jit(solution)/shard_map/ppermute | solution.py:617
  (20 other events, 37.0 us)
Sparse Core Ops, SparseCore 0:
  10.3 27.7 all-gather.2
  39.7 70.7 all-gather.4
  139.8 75.7 reduce-scatter.2
  217.8 32.5 reduce-scatter.4

commit v3 on v2

--- a/solution.py
+++ b/solution.py
@@ -44,6 +44,20 @@
 
 def dot_last(left, right):
     return lax.dot_general(left, right, (((1,), (1,)), ((), ())), preferred_element_type=SINGLE)
+
+
+def dot_first(left_refs, right_ref):
+    total, first = 0.0, 0
+    for left_ref in left_refs:
+        rows = left_ref.shape[0]
+        total = total + lax.dot_general(
+            left_ref[...],
+            right_ref[first : first + rows, :],
+            (((0,), (0,)), ((), ())),
+            preferred_element_type=SINGLE,
+        )
+        first += rows
+    return total
 
 
 def key_span(start):
@@ -265,7 +279,6 @@
     joined,
     natural,
     out_ref,
-    turned,
     bias,
 ):
     query_heads, key_heads, head_dim = sizes
@@ -274,10 +287,10 @@
     columns = natural.shape[1]
     quarter = grad_a_ref.shape[0]
     out_weight = weight_ref[:, columns:]
-    for q, rows_ref in enumerate((grad_a_ref, grad_b_ref, grad_c_ref, grad_d_ref)):
+    grad_refs = (grad_a_ref, grad_b_ref, grad_c_ref, grad_d_ref)
+    for q, rows_ref in enumerate(grad_refs):
         mixed[q * quarter : (q + 1) * quarter, :] = dot(rows_ref[...], out_weight).astype(BFLOAT)
-        turned[:, q * quarter : (q + 1) * quarter] = rows_ref[...].T
-    weight_grad_ref[:, columns:] = dot(turned[...], context_ref[...]).astype(BFLOAT)
+    weight_grad_ref[:, columns:] = dot_first(grad_refs, context_ref).astype(BFLOAT)
     collect(place_ref, mixed, context)
     for head in range(query_heads):
         part = context[:, head * head_dim : (head + 1) * head_dim]
@@ -341,9 +354,7 @@
         part_ref[...] = part.astype(BFLOAT)
         row_gain += jnp.sum(part * rows_refs[q][...].astype(SINGLE), axis=0, keepdims=True)
     row_gain_ref[...] = row_gain
-    for q, rows_ref in enumerate(rows_refs):
-        turned[:, q * quarter : (q + 1) * quarter] = rows_ref[...].T
-    weight_grad_ref[:, :columns] = dot(turned[...], out_ref[...]).astype(BFLOAT)
+    weight_grad_ref[:, :columns] = dot_first(rows_refs, out_ref).astype(BFLOAT)
 
 
 def attend_back(sizes, place, grads, quarters, weight, gains, saved, context, earlier):
@@ -367,7 +378,6 @@
         ((heads * head_dim, LEN), SINGLE),
         ((LEN, columns), BFLOAT),
         ((LEN, columns), BFLOAT),
-        ((width, LEN), BFLOAT),
         ((LEN, TILE), SINGLE),
     ]
     arrays = (*grads, *quarters, weight, gains, *saved, context)
@@ -394,8 +404,6 @@
     part_b_ref,
     part_c_ref,
     part_d_ref,
-    rows_turned,
-    cot_turned,
     gate_up_grad,
     total,
 ):
@@ -408,9 +416,6 @@
 
     @pl.when(step == 0)
     def _():
-        for q in range(4):
-            rows_turned[:, q * quarter : (q + 1) * quarter] = rows_refs[q][...].T
-            cot_turned[:, q * quarter : (q + 1) * quarter] = cot_refs[q][...].T
         total[...] = jnp.zeros(total.shape, SINGLE)
 
     for q in range(4):
@@ -425,8 +430,8 @@
         gate_up_grad[tile, :cols] = (grad_hidden * upward * slope).astype(BFLOAT)
         gate_up_grad[tile, cols:] = (grad_hidden * active).astype(BFLOAT)
         total[tile, :] += dot_last(gate_up_grad[tile, :], weight_ref[:, : 2 * cols])
-    out_ref[:, : 2 * cols] = dot(rows_turned[...], gate_up_grad[...]).astype(BFLOAT)
-    out_ref[:, 2 * cols :] = dot(cot_turned[...], hidden_ref[...]).astype(BFLOAT)
+    out_ref[:, : 2 * cols] = dot_first(rows_refs, gate_up_grad).astype(BFLOAT)
+    out_ref[:, 2 * cols :] = dot_first(cot_refs, hidden_ref).astype(BFLOAT)
 
     @pl.when(step == pl.num_programs(0) - 1)
     def _():
@@ -469,8 +474,6 @@
         in_specs=[whole] * 8 + [block],
         out_specs=[pl.BlockSpec((LEN, cols), lambda j: (0, j)), block] + [whole] * 4,
         scratch_shapes=[
-            pltpu.VMEM((width, LEN), BFLOAT),
-            pltpu.VMEM((width, LEN), BFLOAT),
             pltpu.VMEM((LEN, 2 * cols), BFLOAT),
             pltpu.VMEM((LEN, width), SINGLE),
         ],

time: 259 us -> 258 us (level)
  no operation moved by 1% of the time
where the time goes in v3:
time: 258 us
  waiting for transfers between devices  91.2 us (35%)
  Pallas kernels  81.5 us (32%)
  starting transfers between devices  43.9 us (17%)
  between operations  17.6 us (7%)
  local copies, waits for them, and re-layouts  15.5 us (6%)
  other arithmetic  7.94 us (3%)
    ppermute x37, waiting for transfers between devices, swap(): return lax.ppermute(value, axis, [(i, i ^ bit) for i in range(size)])  83.6 us
    pallas_call x9, Pallas kernels, call_kernel(): pl.pallas_call(kernel, out_shape=[jax.ShapeDtypeStruct(*shape) for shape...  45.3 us
    ppermute x37, starting transfers between devices, swap(): return lax.ppermute(value, axis, [(i, i ^ bit) for i in range(size)])  43.7 us
    pallas_call x1, Pallas kernels, feedfwd(): pl.pallas_call(feedfwd_kernel, grid=(hidden_cols // cols,), out_shape=[ja...  28.1 us
    unnamed x96, local copies, waits for them, and re-layouts  11 us
    pallas_call x1, Pallas kernels, down_parts_of(): pl.pallas_call(down_kernel, grid=(hidden_cols // cols,), out_shape=[jax.S...  8 us
    all_gather x1, waiting for transfers between devices, on_device(): lax.all_gather(interleave(gate_weight, up_weight, down_weight.T), 'dp', a...  6.4 us
  transfers between devices with their start and end apart: 41, of which 25 were waited for; matrix products, arithmetic and copies ran while one was open for 5% of the time, Pallas kernels for 19%

profile of v3, /device:TPU:0, one launch (start us, length us, event | category | flops | bytes accessed | tf_op | source)
XLA Modules:
  0.0 257.6 jit_solution(2994426712121969747)
XLA Ops:
  7.3 1.8 pack_weights.1
  9.6 1.0 copy-done.26
  11.1 3.0 %collective-permute-start = (bf16[128,1024]{1,0:T(8,128)(2,1)S(1)}, bf16[128,1024]{1,0:T(8,128)(2,1)S(1)}, u32[]{:S(2)}, u32[]{:S(2)}) collective-permute-start(bf16[128,1024]{1,0:T(8,128)(2,1)S(1)} %get-tuple-element.164), channel_id=1, source_target_pairs={{0,1},{1,0},{2,3},{3,2},{4,5},{5,4},{6,7},{7,6},{8,9},{9,8},{10,11... | collective-permute-start | bytes 786440 | tf_op jit(solution)/shard_map/ppermute | solution.py:620
  14.1 1.5 collective-permute-start.2
  15.6 4.8 %collective-permute-done = bf16[128,1024]{1,0:T(8,128)(2,1)S(1)} collective-permute-done((bf16[128,1024]{1,0:T(8,128)(2,1)S(1)}, bf16[128,1024]{1,0:T(8,128)(2,1)S(1)}, u32[]{:S(2)}, u32[]{:S(2)}) %collective-permute-start) | collective-permute-done | bytes 262176 | tf_op jit(solution)/shard_map/ppermute | solution.py:620
  20.5 1.8 collective-permute-start.1
  22.4 1.6 collective-permute-start.3
  24.6 1.1 collective-permute-start.6
  30.0 10.5 %collective-permute-done.4 = bf16[128,1024]{1,0:T(8,128)(2,1)S(1)} collective-permute-done((bf16[128,1024]{1,0:T(8,128)(2,1)S(1)}, bf16[128,1024]{1,0:T(8,128)(2,1)S(1)}, u32[]{:S(2)}, u32[]{:S(2)}) %collective-permute-start.4) | collective-permute-done | bytes 262176 | tf_op jit(solution)/shard_map/ppermute | solution.py:620
  41.4 1.1 collective-permute-start.5
  43.3 0.9 collective-permute-start.7
  44.3 16.7 %attend.1 = (f32[512,1024]{1,0:T(8,128)}, bf16[4,64,1024]{2,1,0:T(8,128)(2,1)}, bf16[2,64,1024]{2,1,0:T(8,128)(2,1)}, bf16[4,1024,64]{2,1,0:T(8,128)(2,1)}, bf16...) custom-call(s32[8]{0:T(128)} %stack.2.place_ref, ...), custom_call_target="tpu_custom_call" | custom-call | flops 16000000000 | bytes 1048576 | tf_op jit(solution)/shard_map/attend/pallas_call | solution.py:29
  62.0 0.9 collective-permute-start.9
  62.9 1.0 collective-permute-start.8
  63.8 9.4 %collective-permute-done.9.got_b_ref = bf16[256,1024]{1,0:T(8,128)(2,1)S(1)} collective-permute-done((bf16[256,1024]{1,0:T(8,128)(2,1)}, bf16[256,1024]{1,0:T(8,128)(2,1)S(1)}, u32[]{:S(2)}, u32[]{:S(2)}) %collective-permute-start.9) | collective-permute-done | bytes 524320 | tf_op jit(solution)/shard_map/ppermute | solution.py:620
  73.2 1.0 collective-permute-done.8.got_a_ref
  75.3 2.0 collective-permute-start.13
  77.4 4.4 %collective-permute-done.10 = bf16[128,1024]{1,0:T(8,128)(2,1)S(1)} collective-permute-done((bf16[128,1024]{1,0:T(8,128)(2,1)S(1)}, bf16[128,1024]{1,0:T(8,128)(2,1)S(1)}, u32[]{:S(2)}, u32[]{:S(2)}) %collective-permute-start.10) | collective-permute-done | bytes 262176 | tf_op jit(solution)/shard_map/ppermute | solution.py:620
  83.1 1.6 collective-permute-start.11
  84.7 1.0 collective-permute-start.14
  85.7 5.9 %collective-permute-done.11 = bf16[128,1024]{1,0:T(8,128)(2,1)S(1)} collective-permute-done((bf16[128,1024]{1,0:T(8,128)(2,1)S(1)}, bf16[128,1024]{1,0:T(8,128)(2,1)S(1)}, u32[]{:S(2)}, u32[]{:S(2)}) %collective-permute-start.11) | collective-permute-done | bytes 262176 | tf_op jit(solution)/shard_map/ppermute | solution.py:620
  91.6 3.1 %collective-permute-start.12 = (bf16[256,1024]{1,0:T(8,128)(2,1)S(1)}, bf16[256,1024]{1,0:T(8,128)(2,1)S(1)}, u32[]{:S(2)}, u32[]{:S(2)}) collective-permute-start(bf16[256,1024]{1,0:T(8,128)(2,1)S(1)} %pad_maximum_fusion.6.rows_a_ref), channel_id=1, source_target_pairs={{0,2},{1,3},{2,0},{3,1},{4,6},{5,7},{6,4},{7,5},{8,10},{9,11},{10,... | collective-permute-start | bytes 1572872 | tf_op jit(solution)/shard_map/ppermute | solution.py:620
  95.0 6.9 %collective-permute-done.12.rows_b_ref = bf16[256,1024]{1,0:T(8,128)(2,1)S(1)} collective-permute-done((bf16[256,1024]{1,0:T(8,128)(2,1)S(1)}, bf16[256,1024]{1,0:T(8,128)(2,1)S(1)}, u32[]{:S(2)}, u32[]{:S(2)}) %collective-permute-start.12) | collective-permute-done | bytes 524320 | tf_op jit(solution)/shard_map/ppermute | solution.py:620
  101.9 2.2 collective-permute-done.15.rows_d_ref
  104.1 6.4 %all-gather.5.cloned.1.call-done.weight_ref = bf16[1024,3456]{1,0:T(8,128)(2,1)} async-done(((bf16[128,3456]{1,0:T(8,128)(2,1)}), bf16[1024,3456]{1,0:T(8,128)(2,1)}) %all-gather.5.cloned.1.call-update) | async-done | bytes 7077904 | tf_op jit(solution)/shard_map/all_gather | solution.py:709
  110.5 28.1 %feedfwd.1 = (bf16[1024,1152]{1,0:T(8,128)(2,1)}, bf16[1024,3456]{1,0:T(8,128)(2,1)}, bf16[256,1024]{1,0:T(8,128)(2,1)}, bf16[256,1024]{1,0:T(8,128)(2,1)}, bf16...) custom-call(bf16[256,1024]{1,0:T(8,128)(2,1)} %copy-done.31, bf16[256,1024]{1,0:T(8,128)(2,1)} %copy-done.40, ...), custom_call_target="tpu_custom_call" | custom-call | flops 16000000000 | bytes 1048576 | tf_op jit(solution)/shard_map/feedfwd/pallas_call | solution.py:466
  138.8 1.5 collective-permute-start.16
  140.3 1.5 collective-permute-start.17
  141.8 11.3 %collective-permute-done.16.got_a_ref = bf16[256,1024]{1,0:T(8,128)(2,1)S(1)} collective-permute-done((bf16[256,1024]{1,0:T(8,128)(2,1)}, bf16[256,1024]{1,0:T(8,128)(2,1)S(1)}, u32[]{:S(2)}, u32[]{:S(2)}) %collective-permute-start.16) | collective-permute-done | bytes 524320 | tf_op jit(solution)/shard_map/ppermute | solution.py:620
  153.1 1.0 collective-permute-done.17.got_b_ref
  154.3 1.5 collective-permute-start.18
  155.9 1.1 collective-permute-start.19
  157.0 4.8 %collective-permute-done.18 = bf16[128,1024]{1,0:T(8,128)(2,1)S(1)} collective-permute-done((bf16[128,1024]{1,0:T(8,128)(2,1)S(1)}, bf16[128,1024]{1,0:T(8,128)(2,1)S(1)}, u32[]{:S(2)}, u32[]{:S(2)}) %collective-permute-start.18) | collective-permute-done | bytes 262176 | tf_op jit(solution)/shard_map/ppermute | solution.py:620
  161.8 1.2 collective-permute-done.19
  163.5 1.3 fusion.2
  165.4 1.5 collective-permute-start.22
  166.8 4.3 %collective-permute-done.20 = bf16[128,1024]{1,0:T(8,128)(2,1)S(1)} collective-permute-done((bf16[128,1024]{1,0:T(8,128)(2,1)S(1)}, bf16[128,1024]{1,0:T(8,128)(2,1)S(1)}, u32[]{:S(2)}, u32[]{:S(2)}) %collective-permute-start.20) | collective-permute-done | bytes 262176 | tf_op jit(solution)/shard_map/ppermute | solution.py:620
  171.2 1.8 collective-permute-start.21
  173.1 1.3 collective-permute-start.23
  174.4 8.0 %down_parts.1 = (bf16[256,1024]{1,0:T(8,128)(2,1)}, bf16[256,1024]{1,0:T(8,128)(2,1)}, bf16[256,1024]{1,0:T(8,128)(2,1)}, bf16[256,1024]{1,0:T(8,128)(2,1)}) custom-call(bf16[1024,1152]{1,0:T(8,128)(2,1)} %get-tuple-element.82.hidden_ref, bf16[1024,3456]{1,0:T(8,128)(2,1)} %all-gather.5.cloned.1.call-done.weight_ref, bf16[128,1024]{1,0:T(8,128)(2,1)} %copy-done.20, ...), custom_call_target="tpu_custom_call" | custom-call | flops 1000000000 | bytes 1048576 | tf_op jit(solution)/shard_map/down_parts/pallas_call | solution.py:535
  183.0 1.3 collective-permute-done.23.refs_2_.grad_d_ref
  185.5 1.4 collective-permute-start.25
  186.9 20.2 %attend_back.1 = (bf16[1024,768]{1,0:T(8,128)(2,1)}, f32[2,64,128]{2,1,0:T(8,128)}, f32[1,1024]{1,0:T(1,128)}, bf16[256,1024]{1,0:T(8,128)(2,1)}, bf16[256,1024]...) custom-call(s32[8]{0:T(128)} %stack.2.place_ref, bf16[256,1024]{1,0:T(8,128)(2,1)} %copy-done.29, ...), custom_call_target="tpu_custom_call" | custom-call | flops 16000000000 | bytes 1048576 | tf_op jit(solution)/shard_map/attend_back/pallas_call | solution.py:29
  207.9 1.5 collective-permute-start.28
  210.0 0.9 reduce_sum.87
  214.7 3.5 %collective-permute-done.27.got_a_ref = bf16[256,1024]{1,0:T(8,128)(2,1)S(1)} collective-permute-done((bf16[256,1024]{1,0:T(8,128)(2,1)}, bf16[256,1024]{1,0:T(8,128)(2,1)S(1)}, u32[]{:S(2)}, u32[]{:S(2)}) %collective-permute-start.27) | collective-permute-done | bytes 524320 | tf_op jit(solution)/shard_map/ppermute | solution.py:620
  218.9 1.4 copy-done
  220.3 1.1 copy-done.9
  221.4 1.0 copy-done.10
  224.0 1.2 collective-permute-done.32
  225.4 1.2 collective-permute-start.30
  226.6 1.7 collective-permute-start.29
  228.3 0.9 collective-permute-start.31
  229.3 1.4 collective-permute-start.34
  230.7 1.4 fusion.4
  232.1 2.1 collective-permute-done.34
  234.2 1.1 pad_maximum_fusion
  235.3 4.1 %collective-permute-done.35 = f32[2176]{0:T(1024)S(1)} collective-permute-done((f32[2176]{0:T(1024)S(1)}, f32[2176]{0:T(1024)S(1)}, u32[]{:S(2)}, u32[]{:S(2)}) %collective-permute-start.35) | collective-permute-done | bytes 8736 | tf_op jit(solution)/shard_map/ppermute | solution.py:620
  239.5 1.1 collective-permute-start.36
  240.6 1.1 copy.41
  241.7 1.5 collective-permute-done.36
  244.4 4.1 %finish.1 = (bf16[256,1024]{1,0:T(8,128)(2,1)}, bf16[256,1024]{1,0:T(8,128)(2,1)}) custom-call(bf16[256,1024]{1,0:T(8,128)(2,1)} %tokens_ref.1, f32[1,1024]{1,0:T(1,128)} %bitcast.20, f32[128,1024]{1,0:T(8,128)} %copy-done.17, f32[128,1024]{1,0:T(8,128)} %get-tuple-element.160.refs_1_, f32[128,1024]{1,0:T(8,128)} %copy-done.1, ...), custom_call_target="tpu_custom_call" | custom-call | flops 16000000000 | bytes 1048576 | tf_op jit(solution)/shard_map/finish/pallas_call | solution.py:29
  248.5 1.0 reduce-scatter.5.cloned.1.call-done.value_ref
  249.4 1.7 split_weights.1
  (176 shorter events, 20.1 us)
Async XLA Ops:
  7.2 37.1 %all-gather.3.cloned.1.call-start = ((), (), s32[]{:S(2)}) async-start(), calls=%async_computation.2 | async-start | bytes 1769472 | tf_op jit(solution)/shard_map/all_gather | solution.py:703
  9.0 101.5 %all-gather.5.cloned.1.call-start = ((), (), s32[]{:S(2)}) async-start(), calls=%async_computation.3 | async-start | bytes 7962624 | tf_op jit(solution)/shard_map/all_gather | solution.py:709
  10.6 204.1 %reduce-scatter.3.cloned.1.call-start = ((), (), s32[]{:S(2)}) async-start(), calls=%async_computation.4 | async-start | bytes 7962624 | tf_op jit(solution)/shard_map/reduce_scatter | solution.py:729
  10.8 13.1 %copy-start.21 = (bf16[256,1024]{1,0:T(8,128)(2,1)S(1)}, bf16[256,1024]{1,0:T(8,128)(2,1)}, u32[]{:S(2)}) copy-start(bf16[256,1024]{1,0:T(8,128)(2,1)} %param.24) | copy-start | bytes 1572868
  11.0 14.6 %copy-start.38 = (s32[4]{0:T(128)S(1)}, s32[4]{0:T(128)}, u32[]{:S(2)}) copy-start(s32[4]{0:T(128)} %constant.49.clone) | copy-start | bytes 52
  11.0 18.4 %copy-start.41 = (f32[64]{0:T(128)S(1)}, f32[64]{0:T(128)}, u32[]{:S(2)}) copy-start(f32[64]{0:T(128)} %param.35) | copy-start | bytes 772
  11.1 18.4 %copy-start.42 = (f32[64]{0:T(128)S(1)}, f32[64]{0:T(128)}, u32[]{:S(2)}) copy-start(f32[64]{0:T(128)} %param.34) | copy-start | bytes 772
  11.1 9.3 %collective-permute-start = (bf16[128,1024]{1,0:T(8,128)(2,1)S(1)}, bf16[128,1024]{1,0:T(8,128)(2,1)S(1)}, u32[]{:S(2)}, u32[]{:S(2)}) collective-permute-start(bf16[128,1024]{1,0:T(8,128)(2,1)S(1)} %get-tuple-element.164), channel_id=1, source_target_pairs={{0,1},{1,0},{2,3},{3,2},{4,5},{5,4},{6,7},{7,6},{8,9},{9,8},{10,11... | collective-permute-start | bytes 786440 | tf_op jit(solution)/shard_map/ppermute | solution.py:620
  14.1 8.2 %collective-permute-start.2 = (bf16[128,1024]{1,0:T(8,128)(2,1)S(1)}, bf16[128,1024]{1,0:T(8,128)(2,1)S(1)}, u32[]{:S(2)}, u32[]{:S(2)}) collective-permute-start(bf16[128,1024]{1,0:T(8,128)(2,1)S(1)} %get-tuple-element.163), channel_id=1, source_target_pairs={{0,2},{1,3},{2,0},{3,1},{4,6},{5,7},{6,4},{7,5},{8,10},{9,11},{10,... | collective-permute-start | bytes 786440 | tf_op jit(solution)/shard_map/ppermute | solution.py:620
  20.5 22.9 %copy-start.27 = (bf16[256,1024]{1,0:T(8,128)(2,1)}, bf16[256,1024]{1,0:T(8,128)(2,1)S(1)}, u32[]{:S(2)}) copy-start(bf16[256,1024]{1,0:T(8,128)(2,1)S(1)} %pad_maximum_fusion.2.rows_a_ref) | copy-start | bytes 1572868
  20.5 23.8 %collective-permute-start.1 = (bf16[256,1024]{1,0:T(8,128)(2,1)S(1)}, bf16[256,1024]{1,0:T(8,128)(2,1)}, u32[]{:S(2)}, u32[]{:S(2)}) collective-permute-start(bf16[256,1024]{1,0:T(8,128)(2,1)S(1)} %pad_maximum_fusion.2.rows_a_ref), channel_id=1, source_target_pairs={{0,2},{1,3},{2,0},{3,1},{4,6},{5,7},{6,4},{7,5},{8,10},{9,11},{10,... | collective-permute-start | bytes 1572872 | tf_op jit(solution)/shard_map/ppermute | solution.py:620
  22.3 21.9 %copy-start.28 = (bf16[256,1024]{1,0:T(8,128)(2,1)}, bf16[256,1024]{1,0:T(8,128)(2,1)S(1)}, u32[]{:S(2)}) copy-start(bf16[256,1024]{1,0:T(8,128)(2,1)S(1)} %pad_maximum_fusion.3.rows_c_ref) | copy-start | bytes 1572868
  22.4 21.9 %collective-permute-start.3 = (bf16[256,1024]{1,0:T(8,128)(2,1)S(1)}, bf16[256,1024]{1,0:T(8,128)(2,1)}, u32[]{:S(2)}, u32[]{:S(2)}) collective-permute-start(bf16[256,1024]{1,0:T(8,128)(2,1)S(1)} %pad_maximum_fusion.3.rows_c_ref), channel_id=1, source_target_pairs={{0,1},{1,0},{2,3},{3,2},{4,5},{5,4},{6,7},{7,6},{8,9},{9,8},{10,11... | collective-permute-start | bytes 1572872 | tf_op jit(solution)/shard_map/ppermute | solution.py:620
  24.0 16.6 %collective-permute-start.4 = (bf16[128,1024]{1,0:T(8,128)(2,1)S(1)}, bf16[128,1024]{1,0:T(8,128)(2,1)S(1)}, u32[]{:S(2)}, u32[]{:S(2)}) collective-permute-start(bf16[128,1024]{1,0:T(8,128)(2,1)S(1)} %get-tuple-element.162), channel_id=1, source_target_pairs={{0,1},{1,0},{2,3},{3,2},{4,5},{5,4},{6,7},{7,6},{8,9},{9,8},{10,11... | collective-permute-start | bytes 786440 | tf_op jit(solution)/shard_map/ppermute | solution.py:620
  24.6 17.9 %collective-permute-start.6 = (bf16[128,1024]{1,0:T(8,128)(2,1)S(1)}, bf16[128,1024]{1,0:T(8,128)(2,1)S(1)}, u32[]{:S(2)}, u32[]{:S(2)}) collective-permute-start(bf16[128,1024]{1,0:T(8,128)(2,1)S(1)} %get-tuple-element.161), channel_id=1, source_target_pairs={{0,2},{1,3},{2,0},{3,1},{4,6},{5,7},{6,4},{7,5},{8,10},{9,11},{10,... | collective-permute-start | bytes 786440 | tf_op jit(solution)/shard_map/ppermute | solution.py:620
  41.4 19.6 %collective-permute-start.5 = (bf16[256,1024]{1,0:T(8,128)(2,1)}, bf16[256,1024]{1,0:T(8,128)(2,1)S(1)}, u32[]{:S(2)}, u32[]{:S(2)}) collective-permute-start(bf16[256,1024]{1,0:T(8,128)(2,1)} %pad_maximum_fusion.4.cot_a_ref), channel_id=1, source_target_pairs={{0,2},{1,3},{2,0},{3,1},{4,6},{5,7},{6,4},{7,5},{8,10},{9,11},{10,... | collective-permute-start | bytes 1572872 | tf_op jit(solution)/shard_map/ppermute | solution.py:620
  43.3 17.7 %collective-permute-start.7 = (bf16[256,1024]{1,0:T(8,128)(2,1)}, bf16[256,1024]{1,0:T(8,128)(2,1)S(1)}, u32[]{:S(2)}, u32[]{:S(2)}) collective-permute-start(bf16[256,1024]{1,0:T(8,128)(2,1)} %pad_maximum_fusion.5.cot_c_ref), channel_id=1, source_target_pairs={{0,1},{1,0},{2,3},{3,2},{4,5},{5,4},{6,7},{7,6},{8,9},{9,8},{10,11... | collective-permute-start | bytes 1572872 | tf_op jit(solution)/shard_map/ppermute | solution.py:620
  62.0 12.2 %copy-start.12 = (bf16[256,1024]{1,0:T(8,128)(2,1)S(1)}, bf16[256,1024]{1,0:T(8,128)(2,1)}, u32[]{:S(2)}) copy-start(bf16[256,1024]{1,0:T(8,128)(2,1)} %get-tuple-element.68.stay_a_ref) | copy-start | bytes 1572868
  62.0 12.2 %copy-start.13 = (bf16[256,1024]{1,0:T(8,128)(2,1)S(1)}, bf16[256,1024]{1,0:T(8,128)(2,1)}, u32[]{:S(2)}) copy-start(bf16[256,1024]{1,0:T(8,128)(2,1)} %get-tuple-element.70.stay_b_ref) | copy-start | bytes 1572868
  62.0 11.2 %collective-permute-start.9 = (bf16[256,1024]{1,0:T(8,128)(2,1)}, bf16[256,1024]{1,0:T(8,128)(2,1)S(1)}, u32[]{:S(2)}, u32[]{:S(2)}) collective-permute-start(bf16[256,1024]{1,0:T(8,128)(2,1)} %later.6), channel_id=1, source_target_pairs={{0,1},{1,0},{2,3},{3,2},{4,5},{5,4},{6,7},{7,6},{8,9},{9,8},{10,11... | collective-permute-start | bytes 1572872 | tf_op jit(solution)/shard_map/ppermute | solution.py:620
  62.9 11.4 %collective-permute-start.8 = (bf16[256,1024]{1,0:T(8,128)(2,1)}, bf16[256,1024]{1,0:T(8,128)(2,1)S(1)}, u32[]{:S(2)}, u32[]{:S(2)}) collective-permute-start(bf16[256,1024]{1,0:T(8,128)(2,1)} %later.5), channel_id=1, source_target_pairs={{0,2},{1,3},{2,0},{3,1},{4,6},{5,7},{6,4},{7,5},{8,10},{9,11},{10,... | collective-permute-start | bytes 1572872 | tf_op jit(solution)/shard_map/ppermute | solution.py:620
  74.5 7.3 %collective-permute-start.10 = (bf16[128,1024]{1,0:T(8,128)(2,1)S(1)}, bf16[128,1024]{1,0:T(8,128)(2,1)S(1)}, u32[]{:S(2)}, u32[]{:S(2)}) collective-permute-start(bf16[128,1024]{1,0:T(8,128)(2,1)S(1)} %get-tuple-element.73), channel_id=1, source_target_pairs={{0,1},{1,0},{2,3},{3,2},{4,5},{5,4},{6,7},{7,6},{8,9},{9,8},{10,11... | collective-permute-start | bytes 786440 | tf_op jit(solution)/shard_map/ppermute | solution.py:620
  75.3 7.3 %collective-permute-start.13 = (bf16[128,1024]{1,0:T(8,128)(2,1)S(1)}, bf16[128,1024]{1,0:T(8,128)(2,1)S(1)}, u32[]{:S(2)}, u32[]{:S(2)}) collective-permute-start(bf16[128,1024]{1,0:T(8,128)(2,1)S(1)} %get-tuple-element.75), channel_id=1, source_target_pairs={{0,2},{1,3},{2,0},{3,1},{4,6},{5,7},{6,4},{7,5},{8,10},{9,11},{10,... | collective-permute-start | bytes 786440 | tf_op jit(solution)/shard_map/ppermute | solution.py:620
  82.9 80.6 %copy-start.16 = (f32[128,1024]{1,0:T(8,128)}, f32[128,1024]{1,0:T(8,128)S(1)}, u32[]{:S(2)}) copy-start(f32[128,1024]{1,0:T(8,128)S(1)} %get-tuple-element.145.refs_6_) | copy-start | bytes 1572868
  82.9 80.6 %copy-start.17 = (f32[128,1024]{1,0:T(8,128)}, f32[128,1024]{1,0:T(8,128)S(1)}, u32[]{:S(2)}) copy-start(f32[128,1024]{1,0:T(8,128)S(1)} %get-tuple-element.149.refs_0_) | copy-start | bytes 1572868
  83.1 8.5 %collective-permute-start.11 = (bf16[128,1024]{1,0:T(8,128)(2,1)S(1)}, bf16[128,1024]{1,0:T(8,128)(2,1)S(1)}, u32[]{:S(2)}, u32[]{:S(2)}) collective-permute-start(bf16[128,1024]{1,0:T(8,128)(2,1)S(1)} %get-tuple-element.172), channel_id=1, source_target_pairs={{0,1},{1,0},{2,3},{3,2},{4,5},{5,4},{6,7},{7,6},{8,9},{9,8},{10,11... | collective-permute-start | bytes 786440 | tf_op jit(solution)/shard_map/ppermute | solution.py:620
  84.7 10.1 %collective-permute-start.14 = (bf16[128,1024]{1,0:T(8,128)(2,1)S(1)}, bf16[128,1024]{1,0:T(8,128)(2,1)S(1)}, u32[]{:S(2)}, u32[]{:S(2)}) collective-permute-start(bf16[128,1024]{1,0:T(8,128)(2,1)S(1)} %get-tuple-element.171), channel_id=1, source_target_pairs={{0,2},{1,3},{2,0},{3,1},{4,6},{5,7},{6,4},{7,5},{8,10},{9,11},{10,... | collective-permute-start | bytes 786440 | tf_op jit(solution)/shard_map/ppermute | solution.py:620
  91.6 18.9 %copy-start.31 = (bf16[256,1024]{1,0:T(8,128)(2,1)}, bf16[256,1024]{1,0:T(8,128)(2,1)S(1)}, u32[]{:S(2)}) copy-start(bf16[256,1024]{1,0:T(8,128)(2,1)S(1)} %pad_maximum_fusion.6.rows_a_ref) | copy-start | bytes 1572868
  91.6 10.3 %collective-permute-start.12 = (bf16[256,1024]{1,0:T(8,128)(2,1)S(1)}, bf16[256,1024]{1,0:T(8,128)(2,1)S(1)}, u32[]{:S(2)}, u32[]{:S(2)}) collective-permute-start(bf16[256,1024]{1,0:T(8,128)(2,1)S(1)} %pad_maximum_fusion.6.rows_a_ref), channel_id=1, source_target_pairs={{0,2},{1,3},{2,0},{3,1},{4,6},{5,7},{6,4},{7,5},{8,10},{9,11},{10,... | collective-permute-start | bytes 1572872 | tf_op jit(solution)/shard_map/ppermute | solution.py:620
  94.8 15.8 %copy-start.32 = (bf16[256,1024]{1,0:T(8,128)(2,1)}, bf16[256,1024]{1,0:T(8,128)(2,1)S(1)}, u32[]{:S(2)}) copy-start(bf16[256,1024]{1,0:T(8,128)(2,1)S(1)} %pad_maximum_fusion.7.rows_c_ref) | copy-start | bytes 1572868
  94.8 9.4 %collective-permute-start.15 = (bf16[256,1024]{1,0:T(8,128)(2,1)S(1)}, bf16[256,1024]{1,0:T(8,128)(2,1)}, u32[]{:S(2)}, u32[]{:S(2)}) collective-permute-start(bf16[256,1024]{1,0:T(8,128)(2,1)S(1)} %pad_maximum_fusion.7.rows_c_ref), channel_id=1, source_target_pairs={{0,1},{1,0},{2,3},{3,2},{4,5},{5,4},{6,7},{7,6},{8,9},{9,8},{10,11... | collective-permute-start | bytes 1572872 | tf_op jit(solution)/shard_map/ppermute | solution.py:620
  138.7 15.4 %copy-start.14 = (bf16[256,1024]{1,0:T(8,128)(2,1)S(1)}, bf16[256,1024]{1,0:T(8,128)(2,1)}, u32[]{:S(2)}) copy-start(bf16[256,1024]{1,0:T(8,128)(2,1)} %get-tuple-element.76.stay_a_ref) | copy-start | bytes 1572868
  138.7 15.4 %copy-start.15 = (bf16[256,1024]{1,0:T(8,128)(2,1)S(1)}, bf16[256,1024]{1,0:T(8,128)(2,1)}, u32[]{:S(2)}) copy-start(bf16[256,1024]{1,0:T(8,128)(2,1)} %get-tuple-element.78.stay_b_ref) | copy-start | bytes 1572868
  138.7 110.7 %reduce-scatter.5.cloned.1.call-start = ((), (), s32[]{:S(2)}) async-start(), calls=%async_computation.5 | async-start | bytes 1769472 | tf_op jit(solution)/shard_map/reduce_scatter | solution.py:748
  138.8 14.3 %collective-permute-start.16 = (bf16[256,1024]{1,0:T(8,128)(2,1)}, bf16[256,1024]{1,0:T(8,128)(2,1)S(1)}, u32[]{:S(2)}, u32[]{:S(2)}) collective-permute-start(bf16[256,1024]{1,0:T(8,128)(2,1)} %get-tuple-element.77), channel_id=1, source_target_pairs={{0,2},{1,3},{2,0},{3,1},{4,6},{5,7},{6,4},{7,5},{8,10},{9,11},{10,... | collective-permute-start | bytes 1572872 | tf_op jit(solution)/shard_map/ppermute | solution.py:620
  140.3 13.8 %collective-permute-start.17 = (bf16[256,1024]{1,0:T(8,128)(2,1)S(1)}, bf16[256,1024]{1,0:T(8,128)(2,1)S(1)}, u32[]{:S(2)}, u32[]{:S(2)}) collective-permute-start(bf16[256,1024]{1,0:T(8,128)(2,1)S(1)} %copy-done.39), channel_id=1, source_target_pairs={{0,1},{1,0},{2,3},{3,2},{4,5},{5,4},{6,7},{7,6},{8,9},{9,8},{10,11... | collective-permute-start | bytes 1572872 | tf_op jit(solution)/shard_map/ppermute | solution.py:620
  154.3 7.5 %collective-permute-start.18 = (bf16[128,1024]{1,0:T(8,128)(2,1)S(1)}, bf16[128,1024]{1,0:T(8,128)(2,1)S(1)}, u32[]{:S(2)}, u32[]{:S(2)}) collective-permute-start(bf16[128,1024]{1,0:T(8,128)(2,1)S(1)} %get-tuple-element.81), channel_id=1, source_target_pairs={{0,1},{1,0},{2,3},{3,2},{4,5},{5,4},{6,7},{7,6},{8,9},{9,8},{10,11... | collective-permute-start | bytes 786440 | tf_op jit(solution)/shard_map/ppermute | solution.py:620
  155.9 7.1 %collective-permute-start.19 = (bf16[128,1024]{1,0:T(8,128)(2,1)S(1)}, bf16[128,1024]{1,0:T(8,128)(2,1)S(1)}, u32[]{:S(2)}, u32[]{:S(2)}) collective-permute-start(bf16[128,1024]{1,0:T(8,128)(2,1)S(1)} %get-tuple-element.84), channel_id=1, source_target_pairs={{0,2},{1,3},{2,0},{3,1},{4,6},{5,7},{6,4},{7,5},{8,10},{9,11},{10,... | collective-permute-start | bytes 786440 | tf_op jit(solution)/shard_map/ppermute | solution.py:620
  164.8 9.6 %copy-start.19 = (bf16[128,1024]{1,0:T(8,128)(2,1)}, bf16[128,1024]{1,0:T(8,128)(2,1)S(1)}, u32[]{:S(2)}) copy-start(bf16[128,1024]{1,0:T(8,128)(2,1)S(1)} %get-tuple-element.140.refs_1_) | copy-start | bytes 786436
  164.8 9.6 %copy-start.20 = (bf16[128,1024]{1,0:T(8,128)(2,1)}, bf16[128,1024]{1,0:T(8,128)(2,1)S(1)}, u32[]{:S(2)}) copy-start(bf16[128,1024]{1,0:T(8,128)(2,1)S(1)} %get-tuple-element.159.refs_0_) | copy-start | bytes 786436
  164.8 6.4 %collective-permute-start.20 = (bf16[128,1024]{1,0:T(8,128)(2,1)S(1)}, bf16[128,1024]{1,0:T(8,128)(2,1)S(1)}, u32[]{:S(2)}, u32[]{:S(2)}) collective-permute-start(bf16[128,1024]{1,0:T(8,128)(2,1)S(1)} %get-tuple-element.159.refs_0_), channel_id=1, source_target_pairs={{0,1},{1,0},{2,3},{3,2},{4,5},{5,4},{6,7},{7,6},{8,9},{9,8},{10,11... | collective-permute-start | bytes 786440 | tf_op jit(solution)/shard_map/ppermute | solution.py:620
  165.4 7.7 %collective-permute-start.22 = (bf16[128,1024]{1,0:T(8,128)(2,1)S(1)}, bf16[128,1024]{1,0:T(8,128)(2,1)S(1)}, u32[]{:S(2)}, u32[]{:S(2)}) collective-permute-start(bf16[128,1024]{1,0:T(8,128)(2,1)S(1)} %get-tuple-element.140.refs_1_), channel_id=1, source_target_pairs={{0,2},{1,3},{2,0},{3,1},{4,6},{5,7},{6,4},{7,5},{8,10},{9,11},{10,... | collective-permute-start | bytes 786440 | tf_op jit(solution)/shard_map/ppermute | solution.py:620
  171.2 11.2 %copy-start.29 = (bf16[256,1024]{1,0:T(8,128)(2,1)}, bf16[256,1024]{1,0:T(8,128)(2,1)S(1)}, u32[]{:S(2)}) copy-start(bf16[256,1024]{1,0:T(8,128)(2,1)S(1)} %pad_maximum_fusion.8.grad_a_ref) | copy-start | bytes 1572868
  171.2 11.7 %collective-permute-start.21 = (bf16[256,1024]{1,0:T(8,128)(2,1)S(1)}, bf16[256,1024]{1,0:T(8,128)(2,1)S(1)}, u32[]{:S(2)}, u32[]{:S(2)}) collective-permute-start(bf16[256,1024]{1,0:T(8,128)(2,1)S(1)} %pad_maximum_fusion.8.grad_a_ref), channel_id=1, source_target_pairs={{0,2},{1,3},{2,0},{3,1},{4,6},{5,7},{6,4},{7,5},{8,10},{9,11},{10,... | collective-permute-start | bytes 1572872 | tf_op jit(solution)/shard_map/ppermute | solution.py:620
  173.1 9.3 %copy-start.30 = (bf16[256,1024]{1,0:T(8,128)(2,1)}, bf16[256,1024]{1,0:T(8,128)(2,1)S(1)}, u32[]{:S(2)}) copy-start(bf16[256,1024]{1,0:T(8,128)(2,1)S(1)} %pad_maximum_fusion.9.grad_c_ref) | copy-start | bytes 1572868
  173.1 11.2 %collective-permute-start.23 = (bf16[256,1024]{1,0:T(8,128)(2,1)S(1)}, bf16[256,1024]{1,0:T(8,128)(2,1)S(1)}, u32[]{:S(2)}, u32[]{:S(2)}) collective-permute-start(bf16[256,1024]{1,0:T(8,128)(2,1)S(1)} %pad_maximum_fusion.9.grad_c_ref), channel_id=1, source_target_pairs={{0,1},{1,0},{2,3},{3,2},{4,5},{5,4},{6,7},{7,6},{8,9},{9,8},{10,11... | collective-permute-start | bytes 1572872 | tf_op jit(solution)/shard_map/ppermute | solution.py:620
  185.1 25.9 %collective-permute-start.24 = (bf16[256,1024]{1,0:T(8,128)(2,1)}, bf16[256,1024]{1,0:T(8,128)(2,1)S(1)}, u32[]{:S(2)}, u32[]{:S(2)}) collective-permute-start(bf16[256,1024]{1,0:T(8,128)(2,1)} %later.7), channel_id=1, source_target_pairs={{0,2},{1,3},{2,0},{3,1},{4,6},{5,7},{6,4},{7,5},{8,10},{9,11},{10,... | collective-permute-start | bytes 1572872 | tf_op jit(solution)/shard_map/ppermute | solution.py:620
  185.5 25.6 %collective-permute-start.25 = (bf16[256,1024]{1,0:T(8,128)(2,1)}, bf16[256,1024]{1,0:T(8,128)(2,1)S(1)}, u32[]{:S(2)}, u32[]{:S(2)}) collective-permute-start(bf16[256,1024]{1,0:T(8,128)(2,1)} %later.8), channel_id=1, source_target_pairs={{0,1},{1,0},{2,3},{3,2},{4,5},{5,4},{6,7},{7,6},{8,9},{9,8},{10,11... | collective-permute-start | bytes 1572872 | tf_op jit(solution)/shard_map/ppermute | solution.py:620
  186.9 24.2 %copy-start.3 = (bf16[256,1024]{1,0:T(8,128)(2,1)S(1)}, bf16[256,1024]{1,0:T(8,128)(2,1)}, u32[]{:S(2)}) copy-start(bf16[256,1024]{1,0:T(8,128)(2,1)} %get-tuple-element.85.earlier_ref.stay_a_ref) | copy-start | bytes 1572868
  186.9 24.2 %copy-start.4 = (bf16[256,1024]{1,0:T(8,128)(2,1)S(1)}, bf16[256,1024]{1,0:T(8,128)(2,1)}, u32[]{:S(2)}) copy-start(bf16[256,1024]{1,0:T(8,128)(2,1)} %get-tuple-element.87.stay_b_ref) | copy-start | bytes 1572868
  207.1 11.2 %collective-permute-start.27 = (bf16[256,1024]{1,0:T(8,128)(2,1)}, bf16[256,1024]{1,0:T(8,128)(2,1)S(1)}, u32[]{:S(2)}, u32[]{:S(2)}) collective-permute-start(bf16[256,1024]{1,0:T(8,128)(2,1)} %get-tuple-element.105), channel_id=1, source_target_pairs={{0,2},{1,3},{2,0},{3,1},{4,6},{5,7},{6,4},{7,5},{8,10},{9,11},{10,... | collective-permute-start | bytes 1572872 | tf_op jit(solution)/shard_map/ppermute | solution.py:620
  207.9 11.0 %collective-permute-start.28 = (bf16[256,1024]{1,0:T(8,128)(2,1)}, bf16[256,1024]{1,0:T(8,128)(2,1)S(1)}, u32[]{:S(2)}, u32[]{:S(2)}) collective-permute-start(bf16[256,1024]{1,0:T(8,128)(2,1)} %get-tuple-element.107), channel_id=1, source_target_pairs={{0,1},{1,0},{2,3},{3,2},{4,5},{5,4},{6,7},{7,6},{8,9},{9,8},{10,11... | collective-permute-start | bytes 1572872 | tf_op jit(solution)/shard_map/ppermute | solution.py:620
  214.7 10.4 %copy-start.6 = (bf16[128,1024]{1,0:T(8,128)(2,1)S(1)}, bf16[128,1024]{1,0:T(8,128)(2,1)}, u32[]{:S(2)}) copy-start(bf16[128,1024]{1,0:T(8,128)(2,1)} %copy-done.5) | copy-start | bytes 786436
  222.6 12.7 %copy-start.7 = (f32[128,1024]{1,0:T(8,128)}, f32[128,1024]{1,0:T(8,128)S(1)}, u32[]{:S(2)}) copy-start(f32[128,1024]{1,0:T(8,128)S(1)} %get-tuple-element.110.refs_4_) | copy-start | bytes 1572868
  222.6 12.7 %copy-start.8 = (f32[128,1024]{1,0:T(8,128)}, f32[128,1024]{1,0:T(8,128)S(1)}, u32[]{:S(2)}) copy-start(f32[128,1024]{1,0:T(8,128)S(1)} %get-tuple-element.114.refs_10_) | copy-start | bytes 1572868
  223.9 1.2 collective-permute-start.32
  225.1 4.1 %collective-permute-start.33 = (f32[2176]{0:T(1024)S(1)}, f32[2176]{0:T(1024)S(1)}, u32[]{:S(2)}, u32[]{:S(2)}) collective-permute-start(f32[2176]{0:T(1024)S(1)} %fusion.10), channel_id=1, source_target_pairs={{0,8},{4,12},{8,0},{12,4},{16,24},{20,28},{24,16},{28,20},{1,9},{5... | collective-permute-start | bytes 26120 | tf_op jit(solution)/shard_map/ppermute | solution.py:620
  225.1 19.2 %collective-permute-start.26 = (bf16[128,1024]{1,0:T(8,128)(2,1)S(1)}, bf16[128,1024]{1,0:T(8,128)(2,1)}, u32[]{:S(2)}, u32[]{:S(2)}) collective-permute-start(bf16[128,1024]{1,0:T(8,128)(2,1)S(1)} %copy-done.6), channel_id=1, source_target_pairs={{0,1},{1,0},{2,3},{3,2},{4,5},{5,4},{6,7},{7,6},{8,9},{9,8},{10,11... | collective-permute-start | bytes 786440 | tf_op jit(solution)/shard_map/ppermute | solution.py:620
  225.4 18.9 %collective-permute-start.30 = (bf16[128,1024]{1,0:T(8,128)(2,1)S(1)}, bf16[128,1024]{1,0:T(8,128)(2,1)}, u32[]{:S(2)}, u32[]{:S(2)}) collective-permute-start(bf16[128,1024]{1,0:T(8,128)(2,1)S(1)} %get-tuple-element.113), channel_id=1, source_target_pairs={{0,2},{1,3},{2,0},{3,1},{4,6},{5,7},{6,4},{7,5},{8,10},{9,11},{10,... | collective-permute-start | bytes 786440 | tf_op jit(solution)/shard_map/ppermute | solution.py:620
  226.6 17.7 %collective-permute-start.29 = (bf16[128,1024]{1,0:T(8,128)(2,1)S(1)}, bf16[128,1024]{1,0:T(8,128)(2,1)}, u32[]{:S(2)}, u32[]{:S(2)}) collective-permute-start(bf16[128,1024]{1,0:T(8,128)(2,1)S(1)} %get-tuple-element.111), channel_id=1, source_target_pairs={{0,1},{1,0},{2,3},{3,2},{4,5},{5,4},{6,7},{7,6},{8,9},{9,8},{10,11... | collective-permute-start | bytes 786440 | tf_op jit(solution)/shard_map/ppermute | solution.py:620
  228.3 16.0 %collective-permute-start.31 = (bf16[128,1024]{1,0:T(8,128)(2,1)S(1)}, bf16[128,1024]{1,0:T(8,128)(2,1)}, u32[]{:S(2)}, u32[]{:S(2)}) collective-permute-start(bf16[128,1024]{1,0:T(8,128)(2,1)S(1)} %get-tuple-element.115), channel_id=1, source_target_pairs={{0,2},{1,3},{2,0},{3,1},{4,6},{5,7},{6,4},{7,5},{8,10},{9,11},{10,... | collective-permute-start | bytes 786440 | tf_op jit(solution)/shard_map/ppermute | solution.py:620
  229.3 5.0 %collective-permute-start.34 = (f32[2176]{0:T(1024)S(1)}, f32[2176]{0:T(1024)S(1)}, u32[]{:S(2)}, u32[]{:S(2)}) collective-permute-start(f32[2176]{0:T(1024)S(1)} %add.143), channel_id=1, source_target_pairs={{0,16},{4,20},{8,24},{12,28},{16,0},{20,4},{24,8},{28,12},{1,17},{... | collective-permute-start | bytes 26120 | tf_op jit(solution)/shard_map/ppermute | solution.py:620
  234.2 5.2 %collective-permute-start.35 = (f32[2176]{0:T(1024)S(1)}, f32[2176]{0:T(1024)S(1)}, u32[]{:S(2)}, u32[]{:S(2)}) collective-permute-start(f32[2176]{0:T(1024)S(1)} %add.144), channel_id=1, source_target_pairs={{0,1},{1,0},{2,3},{3,2},{4,5},{5,4},{6,7},{7,6},{8,9},{9,8},{10,11... | collective-permute-start | bytes 26120 | tf_op jit(solution)/shard_map/ppermute | solution.py:620
  239.5 3.7 %collective-permute-start.36 = (f32[2176]{0:T(1024)S(1)}, f32[2176]{0:T(1024)S(1)}, u32[]{:S(2)}, u32[]{:S(2)}) collective-permute-start(f32[2176]{0:T(1024)S(1)} %add.145), channel_id=1, source_target_pairs={{0,2},{1,3},{2,0},{3,1},{4,6},{5,7},{6,4},{7,5},{8,10},{9,11},{10,... | collective-permute-start | bytes 26120 | tf_op jit(solution)/shard_map/ppermute | solution.py:620
  (20 other events, 37.0 us)
Sparse Core Ops, SparseCore 0:
  10.3 27.7 all-gather.2
  39.7 70.7 all-gather.4
  138.8 75.7 reduce-scatter.2
  216.8 32.5 reduce-scatter.4

commit v4 on v3

--- a/solution.py
+++ b/solution.py
@@ -144,7 +144,13 @@
         mixed[q * quarter : (q + 1) * quarter, :] = dot(rows_ref[...], weight)
     collect(place_ref, mixed, natural)
     for start in range(0, LEN, 128):
-        raw_ref[:, start : start + 128] = natural[start : start + 128, :].T
+        turned = natural[start : start + 128, :].T
+        raw_ref[:, start : start + 128] = turned[: heads * head_dim]
+        for head in range(key_heads):
+            first = (heads + head) * head_dim
+            extended[head, :head_dim, start : start + 128] = turned[
+                first : first + head_dim
+            ].astype(BFLOAT)
 
     segment = segment_ref[...]
     first_count = jnp.sum((segment == 0).astype(SINGLE), axis=1, keepdims=True)
@@ -175,7 +181,6 @@
             key_row_ref[head - query_heads] = turned.T.astype(BFLOAT)
     for head in range(key_heads):
         first = (heads + head) * head_dim
-        extended[head, :head_dim, :] = raw_ref[first : first + head_dim, :].astype(BFLOAT)
         extended[head, head_dim:, :] = jnp.ones((extended.shape[1] - head_dim, LEN), BFLOAT)
         value_row_ref[head] = natural[:, first : first + head_dim].astype(BFLOAT)
     factor = LOG2E * head_dim ** (-0.5)
@@ -209,7 +214,7 @@
     columns = (query_heads + 2 * key_heads) * head_dim
     quarter, width = quarters[0].shape
     shapes = [
-        ((columns, LEN), SINGLE),
+        (((query_heads + key_heads) * head_dim, LEN), SINGLE),
         ((query_heads, head_dim, LEN), BFLOAT),
         ((key_heads, head_dim, LEN), BFLOAT),
         ((query_heads, LEN, head_dim), BFLOAT),

time: 258 us -> 258 us (level)
    unnamed x96 -> x106, local copies, waits for them, and re-layouts: 11 us -> 11.7 us
where the time goes in v4:
time: 258 us
  waiting for transfers between devices  90.9 us (35%)
  Pallas kernels  81.7 us (32%)
  starting transfers between devices  44.4 us (17%)
  between operations  17.6 us (7%)
  local copies, waits for them, and re-layouts  15 us (6%)
  other arithmetic  7.93 us (3%)
    ppermute x37, waiting for transfers between devices, swap(): return lax.ppermute(value, axis, [(i, i ^ bit) for i in range(size)])  83.8 us
    pallas_call x9, Pallas kernels, call_kernel(): pl.pallas_call(kernel, out_shape=[jax.ShapeDtypeStruct(*shape) for shape...  45.6 us
    ppermute x37, starting transfers between devices, swap(): return lax.ppermute(value, axis, [(i, i ^ bit) for i in range(size)])  44.3 us
    pallas_call x1, Pallas kernels, feedfwd(): pl.pallas_call(feedfwd_kernel, grid=(hidden_cols // cols,), out_shape=[ja...  28.1 us
    unnamed x106, local copies, waits for them, and re-layouts  11.7 us
    pallas_call x1, Pallas kernels, down_parts_of(): pl.pallas_call(down_kernel, grid=(hidden_cols // cols,), out_shape=[jax.S...  8.02 us
    all_gather x1, waiting for transfers between devices, on_device(): lax.all_gather(interleave(gate_weight, up_weight, down_weight.T), 'dp', a...  6.67 us
  transfers between devices with their start and end apart: 41, of which 25 were waited for; matrix products, arithmetic and copies ran while one was open for 5% of the time, Pallas kernels for 19%

profile of v4, /device:TPU:0, one launch (start us, length us, event | category | flops | bytes accessed | tf_op | source)
XLA Modules:
  0.0 257.6 jit_solution(6698569205950155500)
XLA Ops:
  7.3 1.8 pack_weights.1
  9.6 1.0 copy-done.27
  11.1 3.0 %collective-permute-start = (bf16[128,1024]{1,0:T(8,128)(2,1)S(1)}, bf16[128,1024]{1,0:T(8,128)(2,1)S(1)}, u32[]{:S(2)}, u32[]{:S(2)}) collective-permute-start(bf16[128,1024]{1,0:T(8,128)(2,1)S(1)} %get-tuple-element.164), channel_id=1, source_target_pairs={{0,1},{1,0},{2,3},{3,2},{4,5},{5,4},{6,7},{7,6},{8,9},{9,8},{10,11... | collective-permute-start | bytes 786440 | tf_op jit(solution)/shard_map/ppermute | solution.py:625
  14.1 1.5 collective-permute-start.2
  15.6 4.8 %collective-permute-done = bf16[128,1024]{1,0:T(8,128)(2,1)S(1)} collective-permute-done((bf16[128,1024]{1,0:T(8,128)(2,1)S(1)}, bf16[128,1024]{1,0:T(8,128)(2,1)S(1)}, u32[]{:S(2)}, u32[]{:S(2)}) %collective-permute-start) | collective-permute-done | bytes 262176 | tf_op jit(solution)/shard_map/ppermute | solution.py:625
  20.5 1.8 collective-permute-start.1
  22.3 1.6 collective-permute-start.3
  24.5 1.1 collective-permute-start.6
  30.0 10.5 %collective-permute-done.4 = bf16[128,1024]{1,0:T(8,128)(2,1)S(1)} collective-permute-done((bf16[128,1024]{1,0:T(8,128)(2,1)S(1)}, bf16[128,1024]{1,0:T(8,128)(2,1)S(1)}, u32[]{:S(2)}, u32[]{:S(2)}) %collective-permute-start.4) | collective-permute-done | bytes 262176 | tf_op jit(solution)/shard_map/ppermute | solution.py:625
  40.5 0.8 pad_maximum_fusion.4.cot_a_ref
  41.4 1.1 collective-permute-start.5
  43.3 0.9 collective-permute-start.7
  44.2 16.6 %attend.1 = (f32[384,1024]{1,0:T(8,128)}, bf16[4,64,1024]{2,1,0:T(8,128)(2,1)}, bf16[2,64,1024]{2,1,0:T(8,128)(2,1)}, bf16[4,1024,64]{2,1,0:T(8,128)(2,1)}, bf16...) custom-call(s32[8]{0:T(128)} %stack.2.place_ref, ...), custom_call_target="tpu_custom_call" | custom-call | flops 16000000000 | bytes 1048576 | tf_op jit(solution)/shard_map/attend/pallas_call | solution.py:29
  61.8 0.9 collective-permute-start.9
  62.7 1.0 collective-permute-start.8
  63.6 9.4 %collective-permute-done.9.got_b_ref = bf16[256,1024]{1,0:T(8,128)(2,1)S(1)} collective-permute-done((bf16[256,1024]{1,0:T(8,128)(2,1)}, bf16[256,1024]{1,0:T(8,128)(2,1)S(1)}, u32[]{:S(2)}, u32[]{:S(2)}) %collective-permute-start.9) | collective-permute-done | bytes 524320 | tf_op jit(solution)/shard_map/ppermute | solution.py:625
  73.0 1.0 collective-permute-done.8.got_a_ref
  75.1 2.0 collective-permute-start.13
  77.2 4.0 %collective-permute-done.10 = bf16[128,1024]{1,0:T(8,128)(2,1)S(1)} collective-permute-done((bf16[128,1024]{1,0:T(8,128)(2,1)S(1)}, bf16[128,1024]{1,0:T(8,128)(2,1)S(1)}, u32[]{:S(2)}, u32[]{:S(2)}) %collective-permute-start.10) | collective-permute-done | bytes 262176 | tf_op jit(solution)/shard_map/ppermute | solution.py:625
  82.9 1.5 collective-permute-start.11
  84.4 1.1 collective-permute-start.14
  85.5 5.9 %collective-permute-done.11 = bf16[128,1024]{1,0:T(8,128)(2,1)S(1)} collective-permute-done((bf16[128,1024]{1,0:T(8,128)(2,1)S(1)}, bf16[128,1024]{1,0:T(8,128)(2,1)S(1)}, u32[]{:S(2)}, u32[]{:S(2)}) %collective-permute-start.11) | collective-permute-done | bytes 262176 | tf_op jit(solution)/shard_map/ppermute | solution.py:625
  91.4 3.1 %collective-permute-start.12 = (bf16[256,1024]{1,0:T(8,128)(2,1)S(1)}, bf16[256,1024]{1,0:T(8,128)(2,1)S(1)}, u32[]{:S(2)}, u32[]{:S(2)}) collective-permute-start(bf16[256,1024]{1,0:T(8,128)(2,1)S(1)} %pad_maximum_fusion.6.rows_a_ref), channel_id=1, source_target_pairs={{0,2},{1,3},{2,0},{3,1},{4,6},{5,7},{6,4},{7,5},{8,10},{9,11},{10,... | collective-permute-start | bytes 1572872 | tf_op jit(solution)/shard_map/ppermute | solution.py:625
  94.8 6.9 %collective-permute-done.12.rows_b_ref = bf16[256,1024]{1,0:T(8,128)(2,1)S(1)} collective-permute-done((bf16[256,1024]{1,0:T(8,128)(2,1)S(1)}, bf16[256,1024]{1,0:T(8,128)(2,1)S(1)}, u32[]{:S(2)}, u32[]{:S(2)}) %collective-permute-start.12) | collective-permute-done | bytes 524320 | tf_op jit(solution)/shard_map/ppermute | solution.py:625
  101.6 2.2 collective-permute-done.15.rows_d_ref
  103.9 6.7 %all-gather.5.cloned.1.call-done.weight_ref = bf16[1024,3456]{1,0:T(8,128)(2,1)} async-done(((bf16[128,3456]{1,0:T(8,128)(2,1)}), bf16[1024,3456]{1,0:T(8,128)(2,1)}) %all-gather.5.cloned.1.call-update) | async-done | bytes 7077904 | tf_op jit(solution)/shard_map/all_gather | solution.py:714
  110.5 28.1 %feedfwd.1 = (bf16[1024,1152]{1,0:T(8,128)(2,1)}, bf16[1024,3456]{1,0:T(8,128)(2,1)}, bf16[256,1024]{1,0:T(8,128)(2,1)}, bf16[256,1024]{1,0:T(8,128)(2,1)}, bf16...) custom-call(bf16[256,1024]{1,0:T(8,128)(2,1)} %copy-done.32, bf16[256,1024]{1,0:T(8,128)(2,1)} %copy-done.41, ...), custom_call_target="tpu_custom_call" | custom-call | flops 16000000000 | bytes 1048576 | tf_op jit(solution)/shard_map/feedfwd/pallas_call | solution.py:471
  138.7 1.5 collective-permute-start.16
  140.3 1.5 collective-permute-start.17
  141.7 11.3 %collective-permute-done.16.got_a_ref = bf16[256,1024]{1,0:T(8,128)(2,1)S(1)} collective-permute-done((bf16[256,1024]{1,0:T(8,128)(2,1)}, bf16[256,1024]{1,0:T(8,128)(2,1)S(1)}, u32[]{:S(2)}, u32[]{:S(2)}) %collective-permute-start.16) | collective-permute-done | bytes 524320 | tf_op jit(solution)/shard_map/ppermute | solution.py:625
  153.1 1.0 collective-permute-done.17.got_b_ref
  154.3 1.5 collective-permute-start.18
  155.8 1.1 collective-permute-start.19
  157.0 4.8 %collective-permute-done.18 = bf16[128,1024]{1,0:T(8,128)(2,1)S(1)} collective-permute-done((bf16[128,1024]{1,0:T(8,128)(2,1)S(1)}, bf16[128,1024]{1,0:T(8,128)(2,1)S(1)}, u32[]{:S(2)}, u32[]{:S(2)}) %collective-permute-start.18) | collective-permute-done | bytes 262176 | tf_op jit(solution)/shard_map/ppermute | solution.py:625
  161.8 1.2 collective-permute-done.19
  163.5 1.3 fusion.2
  165.4 1.5 collective-permute-start.22
  166.8 4.3 %collective-permute-done.20 = bf16[128,1024]{1,0:T(8,128)(2,1)S(1)} collective-permute-done((bf16[128,1024]{1,0:T(8,128)(2,1)S(1)}, bf16[128,1024]{1,0:T(8,128)(2,1)S(1)}, u32[]{:S(2)}, u32[]{:S(2)}) %collective-permute-start.20) | collective-permute-done | bytes 262176 | tf_op jit(solution)/shard_map/ppermute | solution.py:625
  171.2 1.8 collective-permute-start.21
  173.1 1.3 collective-permute-start.23
  174.4 8.0 %down_parts.1 = (bf16[256,1024]{1,0:T(8,128)(2,1)}, bf16[256,1024]{1,0:T(8,128)(2,1)}, bf16[256,1024]{1,0:T(8,128)(2,1)}, bf16[256,1024]{1,0:T(8,128)(2,1)}) custom-call(bf16[1024,1152]{1,0:T(8,128)(2,1)} %get-tuple-element.82.hidden_ref, bf16[1024,3456]{1,0:T(8,128)(2,1)} %all-gather.5.cloned.1.call-done.weight_ref, bf16[128,1024]{1,0:T(8,128)(2,1)} %copy-done.21, ...), custom_call_target="tpu_custom_call" | custom-call | flops 1000000000 | bytes 1048576 | tf_op jit(solution)/shard_map/down_parts/pallas_call | solution.py:540
  183.0 1.3 collective-permute-done.23.refs_2_.grad_d_ref
  185.5 1.4 collective-permute-start.25
  186.9 20.0 %attend_back.1 = (bf16[1024,768]{1,0:T(8,128)(2,1)}, f32[2,64,128]{2,1,0:T(8,128)}, f32[1,1024]{1,0:T(1,128)}, bf16[256,1024]{1,0:T(8,128)(2,1)}, bf16[256,1024]...) custom-call(s32[8]{0:T(128)} %stack.2.place_ref, bf16[256,1024]{1,0:T(8,128)(2,1)} %copy-done.30, ...), custom_call_target="tpu_custom_call" | custom-call | flops 16000000000 | bytes 1048576 | tf_op jit(solution)/shard_map/attend_back/pallas_call | solution.py:29
  207.7 1.4 collective-permute-start.28
  209.9 0.9 reduce_sum.87
  213.5 0.9 copy-done.11
  214.7 3.4 %collective-permute-done.27.got_a_ref = bf16[256,1024]{1,0:T(8,128)(2,1)S(1)} collective-permute-done((bf16[256,1024]{1,0:T(8,128)(2,1)}, bf16[256,1024]{1,0:T(8,128)(2,1)S(1)}, u32[]{:S(2)}, u32[]{:S(2)}) %collective-permute-start.27) | collective-permute-done | bytes 524320 | tf_op jit(solution)/shard_map/ppermute | solution.py:625
  218.7 1.0 copy-done.9
  219.7 1.0 copy-done.10
  220.8 0.9 pair_sum.7
  223.7 1.2 collective-permute-done.32
  225.2 1.2 collective-permute-start.30
  226.4 1.7 collective-permute-start.29
  228.1 0.9 collective-permute-start.31
  229.0 1.5 collective-permute-start.34
  230.7 3.0 %collective-permute-done.34 = f32[2176]{0:T(1024)S(1)} collective-permute-done((f32[2176]{0:T(1024)S(1)}, f32[2176]{0:T(1024)S(1)}, u32[]{:S(2)}, u32[]{:S(2)}) %collective-permute-start.34) | collective-permute-done | bytes 8736 | tf_op jit(solution)/shard_map/ppermute | solution.py:625
  234.1 1.1 pad_maximum_fusion
  235.2 4.0 %collective-permute-done.35 = f32[2176]{0:T(1024)S(1)} collective-permute-done((f32[2176]{0:T(1024)S(1)}, f32[2176]{0:T(1024)S(1)}, u32[]{:S(2)}, u32[]{:S(2)}) %collective-permute-start.35) | collective-permute-done | bytes 8736 | tf_op jit(solution)/shard_map/ppermute | solution.py:625
  239.2 1.1 collective-permute-start.36
  240.4 1.1 copy.41
  241.5 1.5 collective-permute-done.36
  245.1 4.1 %finish.1 = (bf16[256,1024]{1,0:T(8,128)(2,1)}, bf16[256,1024]{1,0:T(8,128)(2,1)}) custom-call(bf16[256,1024]{1,0:T(8,128)(2,1)} %tokens_ref.1, f32[1,1024]{1,0:T(1,128)} %bitcast.20, f32[128,1024]{1,0:T(8,128)} %copy-done.17, f32[128,1024]{1,0:T(8,128)} %get-tuple-element.160.refs_1_, f32[128,1024]{1,0:T(8,128)} %copy-done.1, bf16[128,1024]{1,0:T(8,128)(2,1)} %copy-done.42, ...), custom_call_target="tpu_custom_call" | custom-call | flops 16000000000 | bytes 1048576 | tf_op jit(solution)/shard_map/finish/pallas_call | solution.py:29
  249.3 1.7 split_weights.1
  (186 shorter events, 21.2 us)
Async XLA Ops:
  7.2 37.0 %all-gather.3.cloned.1.call-start = ((), (), s32[]{:S(2)}) async-start(), calls=%async_computation.2 | async-start | bytes 1769472 | tf_op jit(solution)/shard_map/all_gather | solution.py:708
  9.0 101.5 %all-gather.5.cloned.1.call-start = ((), (), s32[]{:S(2)}) async-start(), calls=%async_computation.3 | async-start | bytes 7962624 | tf_op jit(solution)/shard_map/all_gather | solution.py:714
  10.6 204.1 %reduce-scatter.3.cloned.1.call-start = ((), (), s32[]{:S(2)}) async-start(), calls=%async_computation.4 | async-start | bytes 7962624 | tf_op jit(solution)/shard_map/reduce_scatter | solution.py:734
  11.0 12.9 %copy-start.22 = (bf16[256,1024]{1,0:T(8,128)(2,1)S(1)}, bf16[256,1024]{1,0:T(8,128)(2,1)}, u32[]{:S(2)}) copy-start(bf16[256,1024]{1,0:T(8,128)(2,1)} %param.24) | copy-start | bytes 1572868
  11.1 9.3 %collective-permute-start = (bf16[128,1024]{1,0:T(8,128)(2,1)S(1)}, bf16[128,1024]{1,0:T(8,128)(2,1)S(1)}, u32[]{:S(2)}, u32[]{:S(2)}) collective-permute-start(bf16[128,1024]{1,0:T(8,128)(2,1)S(1)} %get-tuple-element.164), channel_id=1, source_target_pairs={{0,1},{1,0},{2,3},{3,2},{4,5},{5,4},{6,7},{7,6},{8,9},{9,8},{10,11... | collective-permute-start | bytes 786440 | tf_op jit(solution)/shard_map/ppermute | solution.py:625
  14.1 11.5 %copy-start.39 = (s32[4]{0:T(128)S(1)}, s32[4]{0:T(128)}, u32[]{:S(2)}) copy-start(s32[4]{0:T(128)} %constant.49.clone) | copy-start | bytes 52
  14.1 15.3 %copy-start.46 = (f32[64]{0:T(128)S(1)}, f32[64]{0:T(128)}, u32[]{:S(2)}) copy-start(f32[64]{0:T(128)} %param.35) | copy-start | bytes 772
  14.1 15.3 %copy-start.47 = (f32[64]{0:T(128)S(1)}, f32[64]{0:T(128)}, u32[]{:S(2)}) copy-start(f32[64]{0:T(128)} %param.34) | copy-start | bytes 772
  14.1 8.2 %collective-permute-start.2 = (bf16[128,1024]{1,0:T(8,128)(2,1)S(1)}, bf16[128,1024]{1,0:T(8,128)(2,1)S(1)}, u32[]{:S(2)}, u32[]{:S(2)}) collective-permute-start(bf16[128,1024]{1,0:T(8,128)(2,1)S(1)} %get-tuple-element.163), channel_id=1, source_target_pairs={{0,2},{1,3},{2,0},{3,1},{4,6},{5,7},{6,4},{7,5},{8,10},{9,11},{10,... | collective-permute-start | bytes 786440 | tf_op jit(solution)/shard_map/ppermute | solution.py:625
  20.4 20.9 %copy-start.28 = (bf16[256,1024]{1,0:T(8,128)(2,1)}, bf16[256,1024]{1,0:T(8,128)(2,1)S(1)}, u32[]{:S(2)}) copy-start(bf16[256,1024]{1,0:T(8,128)(2,1)S(1)} %pad_maximum_fusion.2.rows_a_ref) | copy-start | bytes 1572868
  20.5 23.8 %collective-permute-start.1 = (bf16[256,1024]{1,0:T(8,128)(2,1)S(1)}, bf16[256,1024]{1,0:T(8,128)(2,1)}, u32[]{:S(2)}, u32[]{:S(2)}) collective-permute-start(bf16[256,1024]{1,0:T(8,128)(2,1)S(1)} %pad_maximum_fusion.2.rows_a_ref), channel_id=1, source_target_pairs={{0,2},{1,3},{2,0},{3,1},{4,6},{5,7},{6,4},{7,5},{8,10},{9,11},{10,... | collective-permute-start | bytes 1572872 | tf_op jit(solution)/shard_map/ppermute | solution.py:625
  22.3 20.9 %copy-start.29 = (bf16[256,1024]{1,0:T(8,128)(2,1)}, bf16[256,1024]{1,0:T(8,128)(2,1)S(1)}, u32[]{:S(2)}) copy-start(bf16[256,1024]{1,0:T(8,128)(2,1)S(1)} %pad_maximum_fusion.3.rows_c_ref) | copy-start | bytes 1572868
  22.3 21.9 %collective-permute-start.3 = (bf16[256,1024]{1,0:T(8,128)(2,1)S(1)}, bf16[256,1024]{1,0:T(8,128)(2,1)}, u32[]{:S(2)}, u32[]{:S(2)}) collective-permute-start(bf16[256,1024]{1,0:T(8,128)(2,1)S(1)} %pad_maximum_fusion.3.rows_c_ref), channel_id=1, source_target_pairs={{0,1},{1,0},{2,3},{3,2},{4,5},{5,4},{6,7},{7,6},{8,9},{9,8},{10,11... | collective-permute-start | bytes 1572872 | tf_op jit(solution)/shard_map/ppermute | solution.py:625
  23.9 16.6 %collective-permute-start.4 = (bf16[128,1024]{1,0:T(8,128)(2,1)S(1)}, bf16[128,1024]{1,0:T(8,128)(2,1)S(1)}, u32[]{:S(2)}, u32[]{:S(2)}) collective-permute-start(bf16[128,1024]{1,0:T(8,128)(2,1)S(1)} %get-tuple-element.162), channel_id=1, source_target_pairs={{0,1},{1,0},{2,3},{3,2},{4,5},{5,4},{6,7},{7,6},{8,9},{9,8},{10,11... | collective-permute-start | bytes 786440 | tf_op jit(solution)/shard_map/ppermute | solution.py:625
  24.5 17.9 %collective-permute-start.6 = (bf16[128,1024]{1,0:T(8,128)(2,1)S(1)}, bf16[128,1024]{1,0:T(8,128)(2,1)S(1)}, u32[]{:S(2)}, u32[]{:S(2)}) collective-permute-start(bf16[128,1024]{1,0:T(8,128)(2,1)S(1)} %get-tuple-element.161), channel_id=1, source_target_pairs={{0,2},{1,3},{2,0},{3,1},{4,6},{5,7},{6,4},{7,5},{8,10},{9,11},{10,... | collective-permute-start | bytes 786440 | tf_op jit(solution)/shard_map/ppermute | solution.py:625
  41.4 19.4 %collective-permute-start.5 = (bf16[256,1024]{1,0:T(8,128)(2,1)}, bf16[256,1024]{1,0:T(8,128)(2,1)S(1)}, u32[]{:S(2)}, u32[]{:S(2)}) collective-permute-start(bf16[256,1024]{1,0:T(8,128)(2,1)} %pad_maximum_fusion.4.cot_a_ref), channel_id=1, source_target_pairs={{0,2},{1,3},{2,0},{3,1},{4,6},{5,7},{6,4},{7,5},{8,10},{9,11},{10,... | collective-permute-start | bytes 1572872 | tf_op jit(solution)/shard_map/ppermute | solution.py:625
  43.3 17.5 %collective-permute-start.7 = (bf16[256,1024]{1,0:T(8,128)(2,1)}, bf16[256,1024]{1,0:T(8,128)(2,1)S(1)}, u32[]{:S(2)}, u32[]{:S(2)}) collective-permute-start(bf16[256,1024]{1,0:T(8,128)(2,1)} %pad_maximum_fusion.5.cot_c_ref), channel_id=1, source_target_pairs={{0,1},{1,0},{2,3},{3,2},{4,5},{5,4},{6,7},{7,6},{8,9},{9,8},{10,11... | collective-permute-start | bytes 1572872 | tf_op jit(solution)/shard_map/ppermute | solution.py:625
  61.8 12.2 %copy-start.12 = (bf16[256,1024]{1,0:T(8,128)(2,1)S(1)}, bf16[256,1024]{1,0:T(8,128)(2,1)}, u32[]{:S(2)}) copy-start(bf16[256,1024]{1,0:T(8,128)(2,1)} %get-tuple-element.68.stay_a_ref) | copy-start | bytes 1572868
  61.8 12.2 %copy-start.13 = (bf16[256,1024]{1,0:T(8,128)(2,1)S(1)}, bf16[256,1024]{1,0:T(8,128)(2,1)}, u32[]{:S(2)}) copy-start(bf16[256,1024]{1,0:T(8,128)(2,1)} %get-tuple-element.70.stay_b_ref) | copy-start | bytes 1572868
  61.8 11.3 %collective-permute-start.9 = (bf16[256,1024]{1,0:T(8,128)(2,1)}, bf16[256,1024]{1,0:T(8,128)(2,1)S(1)}, u32[]{:S(2)}, u32[]{:S(2)}) collective-permute-start(bf16[256,1024]{1,0:T(8,128)(2,1)} %later.6), channel_id=1, source_target_pairs={{0,1},{1,0},{2,3},{3,2},{4,5},{5,4},{6,7},{7,6},{8,9},{9,8},{10,11... | collective-permute-start | bytes 1572872 | tf_op jit(solution)/shard_map/ppermute | solution.py:625
  62.7 11.3 %collective-permute-start.8 = (bf16[256,1024]{1,0:T(8,128)(2,1)}, bf16[256,1024]{1,0:T(8,128)(2,1)S(1)}, u32[]{:S(2)}, u32[]{:S(2)}) collective-permute-start(bf16[256,1024]{1,0:T(8,128)(2,1)} %later.5), channel_id=1, source_target_pairs={{0,2},{1,3},{2,0},{3,1},{4,6},{5,7},{6,4},{7,5},{8,10},{9,11},{10,... | collective-permute-start | bytes 1572872 | tf_op jit(solution)/shard_map/ppermute | solution.py:625
  74.2 6.9 %collective-permute-start.10 = (bf16[128,1024]{1,0:T(8,128)(2,1)S(1)}, bf16[128,1024]{1,0:T(8,128)(2,1)S(1)}, u32[]{:S(2)}, u32[]{:S(2)}) collective-permute-start(bf16[128,1024]{1,0:T(8,128)(2,1)S(1)} %get-tuple-element.73), channel_id=1, source_target_pairs={{0,1},{1,0},{2,3},{3,2},{4,5},{5,4},{6,7},{7,6},{8,9},{9,8},{10,11... | collective-permute-start | bytes 786440 | tf_op jit(solution)/shard_map/ppermute | solution.py:625
  75.1 6.9 %collective-permute-start.13 = (bf16[128,1024]{1,0:T(8,128)(2,1)S(1)}, bf16[128,1024]{1,0:T(8,128)(2,1)S(1)}, u32[]{:S(2)}, u32[]{:S(2)}) collective-permute-start(bf16[128,1024]{1,0:T(8,128)(2,1)S(1)} %get-tuple-element.75), channel_id=1, source_target_pairs={{0,2},{1,3},{2,0},{3,1},{4,6},{5,7},{6,4},{7,5},{8,10},{9,11},{10,... | collective-permute-start | bytes 786440 | tf_op jit(solution)/shard_map/ppermute | solution.py:625
  82.3 81.2 %copy-start.16 = (f32[128,1024]{1,0:T(8,128)}, f32[128,1024]{1,0:T(8,128)S(1)}, u32[]{:S(2)}) copy-start(f32[128,1024]{1,0:T(8,128)S(1)} %get-tuple-element.145.refs_6_) | copy-start | bytes 1572868
  82.3 81.2 %copy-start.17 = (f32[128,1024]{1,0:T(8,128)}, f32[128,1024]{1,0:T(8,128)S(1)}, u32[]{:S(2)}) copy-start(f32[128,1024]{1,0:T(8,128)S(1)} %get-tuple-element.149.refs_0_) | copy-start | bytes 1572868
  82.9 8.5 %collective-permute-start.11 = (bf16[128,1024]{1,0:T(8,128)(2,1)S(1)}, bf16[128,1024]{1,0:T(8,128)(2,1)S(1)}, u32[]{:S(2)}, u32[]{:S(2)}) collective-permute-start(bf16[128,1024]{1,0:T(8,128)(2,1)S(1)} %get-tuple-element.172), channel_id=1, source_target_pairs={{0,1},{1,0},{2,3},{3,2},{4,5},{5,4},{6,7},{7,6},{8,9},{9,8},{10,11... | collective-permute-start | bytes 786440 | tf_op jit(solution)/shard_map/ppermute | solution.py:625
  84.4 10.0 %collective-permute-start.14 = (bf16[128,1024]{1,0:T(8,128)(2,1)S(1)}, bf16[128,1024]{1,0:T(8,128)(2,1)S(1)}, u32[]{:S(2)}, u32[]{:S(2)}) collective-permute-start(bf16[128,1024]{1,0:T(8,128)(2,1)S(1)} %get-tuple-element.171), channel_id=1, source_target_pairs={{0,2},{1,3},{2,0},{3,1},{4,6},{5,7},{6,4},{7,5},{8,10},{9,11},{10,... | collective-permute-start | bytes 786440 | tf_op jit(solution)/shard_map/ppermute | solution.py:625
  91.4 19.1 %copy-start.32 = (bf16[256,1024]{1,0:T(8,128)(2,1)}, bf16[256,1024]{1,0:T(8,128)(2,1)S(1)}, u32[]{:S(2)}) copy-start(bf16[256,1024]{1,0:T(8,128)(2,1)S(1)} %pad_maximum_fusion.6.rows_a_ref) | copy-start | bytes 1572868
  91.4 10.2 %collective-permute-start.12 = (bf16[256,1024]{1,0:T(8,128)(2,1)S(1)}, bf16[256,1024]{1,0:T(8,128)(2,1)S(1)}, u32[]{:S(2)}, u32[]{:S(2)}) collective-permute-start(bf16[256,1024]{1,0:T(8,128)(2,1)S(1)} %pad_maximum_fusion.6.rows_a_ref), channel_id=1, source_target_pairs={{0,2},{1,3},{2,0},{3,1},{4,6},{5,7},{6,4},{7,5},{8,10},{9,11},{10,... | collective-permute-start | bytes 1572872 | tf_op jit(solution)/shard_map/ppermute | solution.py:625
  94.5 16.0 %copy-start.33 = (bf16[256,1024]{1,0:T(8,128)(2,1)}, bf16[256,1024]{1,0:T(8,128)(2,1)S(1)}, u32[]{:S(2)}) copy-start(bf16[256,1024]{1,0:T(8,128)(2,1)S(1)} %pad_maximum_fusion.7.rows_c_ref) | copy-start | bytes 1572868
  94.5 9.4 %collective-permute-start.15 = (bf16[256,1024]{1,0:T(8,128)(2,1)S(1)}, bf16[256,1024]{1,0:T(8,128)(2,1)}, u32[]{:S(2)}, u32[]{:S(2)}) collective-permute-start(bf16[256,1024]{1,0:T(8,128)(2,1)S(1)} %pad_maximum_fusion.7.rows_c_ref), channel_id=1, source_target_pairs={{0,1},{1,0},{2,3},{3,2},{4,5},{5,4},{6,7},{7,6},{8,9},{9,8},{10,11... | collective-permute-start | bytes 1572872 | tf_op jit(solution)/shard_map/ppermute | solution.py:625
  101.6 8.9 %copy-start.41 = (bf16[256,1024]{1,0:T(8,128)(2,1)}, bf16[256,1024]{1,0:T(8,128)(2,1)S(1)}, u32[]{:S(2)}) copy-start(bf16[256,1024]{1,0:T(8,128)(2,1)S(1)} %collective-permute-done.12.rows_b_ref) | copy-start | bytes 1572868
  138.6 15.4 %copy-start.14 = (bf16[256,1024]{1,0:T(8,128)(2,1)S(1)}, bf16[256,1024]{1,0:T(8,128)(2,1)}, u32[]{:S(2)}) copy-start(bf16[256,1024]{1,0:T(8,128)(2,1)} %get-tuple-element.76.stay_a_ref) | copy-start | bytes 1572868
  138.6 15.4 %copy-start.15 = (bf16[256,1024]{1,0:T(8,128)(2,1)S(1)}, bf16[256,1024]{1,0:T(8,128)(2,1)}, u32[]{:S(2)}) copy-start(bf16[256,1024]{1,0:T(8,128)(2,1)} %get-tuple-element.78.stay_b_ref) | copy-start | bytes 1572868
  138.7 110.7 %reduce-scatter.5.cloned.1.call-start = ((), (), s32[]{:S(2)}) async-start(), calls=%async_computation.5 | async-start | bytes 1769472 | tf_op jit(solution)/shard_map/reduce_scatter | solution.py:753
  138.7 14.3 %collective-permute-start.16 = (bf16[256,1024]{1,0:T(8,128)(2,1)}, bf16[256,1024]{1,0:T(8,128)(2,1)S(1)}, u32[]{:S(2)}, u32[]{:S(2)}) collective-permute-start(bf16[256,1024]{1,0:T(8,128)(2,1)} %get-tuple-element.77), channel_id=1, source_target_pairs={{0,2},{1,3},{2,0},{3,1},{4,6},{5,7},{6,4},{7,5},{8,10},{9,11},{10,... | collective-permute-start | bytes 1572872 | tf_op jit(solution)/shard_map/ppermute | solution.py:625
  140.3 13.8 %collective-permute-start.17 = (bf16[256,1024]{1,0:T(8,128)(2,1)S(1)}, bf16[256,1024]{1,0:T(8,128)(2,1)S(1)}, u32[]{:S(2)}, u32[]{:S(2)}) collective-permute-start(bf16[256,1024]{1,0:T(8,128)(2,1)S(1)} %copy-done.40), channel_id=1, source_target_pairs={{0,1},{1,0},{2,3},{3,2},{4,5},{5,4},{6,7},{7,6},{8,9},{9,8},{10,11... | collective-permute-start | bytes 1572872 | tf_op jit(solution)/shard_map/ppermute | solution.py:625
  154.3 7.5 %collective-permute-start.18 = (bf16[128,1024]{1,0:T(8,128)(2,1)S(1)}, bf16[128,1024]{1,0:T(8,128)(2,1)S(1)}, u32[]{:S(2)}, u32[]{:S(2)}) collective-permute-start(bf16[128,1024]{1,0:T(8,128)(2,1)S(1)} %get-tuple-element.81), channel_id=1, source_target_pairs={{0,1},{1,0},{2,3},{3,2},{4,5},{5,4},{6,7},{7,6},{8,9},{9,8},{10,11... | collective-permute-start | bytes 786440 | tf_op jit(solution)/shard_map/ppermute | solution.py:625
  155.8 7.1 %collective-permute-start.19 = (bf16[128,1024]{1,0:T(8,128)(2,1)S(1)}, bf16[128,1024]{1,0:T(8,128)(2,1)S(1)}, u32[]{:S(2)}, u32[]{:S(2)}) collective-permute-start(bf16[128,1024]{1,0:T(8,128)(2,1)S(1)} %get-tuple-element.84), channel_id=1, source_target_pairs={{0,2},{1,3},{2,0},{3,1},{4,6},{5,7},{6,4},{7,5},{8,10},{9,11},{10,... | collective-permute-start | bytes 786440 | tf_op jit(solution)/shard_map/ppermute | solution.py:625
  164.8 9.6 %copy-start.20 = (bf16[128,1024]{1,0:T(8,128)(2,1)}, bf16[128,1024]{1,0:T(8,128)(2,1)S(1)}, u32[]{:S(2)}) copy-start(bf16[128,1024]{1,0:T(8,128)(2,1)S(1)} %get-tuple-element.140.refs_1_) | copy-start | bytes 786436
  164.8 9.6 %copy-start.21 = (bf16[128,1024]{1,0:T(8,128)(2,1)}, bf16[128,1024]{1,0:T(8,128)(2,1)S(1)}, u32[]{:S(2)}) copy-start(bf16[128,1024]{1,0:T(8,128)(2,1)S(1)} %get-tuple-element.159.refs_0_) | copy-start | bytes 786436
  164.8 6.4 %collective-permute-start.20 = (bf16[128,1024]{1,0:T(8,128)(2,1)S(1)}, bf16[128,1024]{1,0:T(8,128)(2,1)S(1)}, u32[]{:S(2)}, u32[]{:S(2)}) collective-permute-start(bf16[128,1024]{1,0:T(8,128)(2,1)S(1)} %get-tuple-element.159.refs_0_), channel_id=1, source_target_pairs={{0,1},{1,0},{2,3},{3,2},{4,5},{5,4},{6,7},{7,6},{8,9},{9,8},{10,11... | collective-permute-start | bytes 786440 | tf_op jit(solution)/shard_map/ppermute | solution.py:625
  165.4 7.7 %collective-permute-start.22 = (bf16[128,1024]{1,0:T(8,128)(2,1)S(1)}, bf16[128,1024]{1,0:T(8,128)(2,1)S(1)}, u32[]{:S(2)}, u32[]{:S(2)}) collective-permute-start(bf16[128,1024]{1,0:T(8,128)(2,1)S(1)} %get-tuple-element.140.refs_1_), channel_id=1, source_target_pairs={{0,2},{1,3},{2,0},{3,1},{4,6},{5,7},{6,4},{7,5},{8,10},{9,11},{10,... | collective-permute-start | bytes 786440 | tf_op jit(solution)/shard_map/ppermute | solution.py:625
  171.2 11.2 %copy-start.30 = (bf16[256,1024]{1,0:T(8,128)(2,1)}, bf16[256,1024]{1,0:T(8,128)(2,1)S(1)}, u32[]{:S(2)}) copy-start(bf16[256,1024]{1,0:T(8,128)(2,1)S(1)} %pad_maximum_fusion.8.grad_a_ref) | copy-start | bytes 1572868
  171.2 11.7 %collective-permute-start.21 = (bf16[256,1024]{1,0:T(8,128)(2,1)S(1)}, bf16[256,1024]{1,0:T(8,128)(2,1)S(1)}, u32[]{:S(2)}, u32[]{:S(2)}) collective-permute-start(bf16[256,1024]{1,0:T(8,128)(2,1)S(1)} %pad_maximum_fusion.8.grad_a_ref), channel_id=1, source_target_pairs={{0,2},{1,3},{2,0},{3,1},{4,6},{5,7},{6,4},{7,5},{8,10},{9,11},{10,... | collective-permute-start | bytes 1572872 | tf_op jit(solution)/shard_map/ppermute | solution.py:625
  173.1 9.3 %copy-start.31 = (bf16[256,1024]{1,0:T(8,128)(2,1)}, bf16[256,1024]{1,0:T(8,128)(2,1)S(1)}, u32[]{:S(2)}) copy-start(bf16[256,1024]{1,0:T(8,128)(2,1)S(1)} %pad_maximum_fusion.9.grad_c_ref) | copy-start | bytes 1572868
  173.1 11.2 %collective-permute-start.23 = (bf16[256,1024]{1,0:T(8,128)(2,1)S(1)}, bf16[256,1024]{1,0:T(8,128)(2,1)S(1)}, u32[]{:S(2)}, u32[]{:S(2)}) collective-permute-start(bf16[256,1024]{1,0:T(8,128)(2,1)S(1)} %pad_maximum_fusion.9.grad_c_ref), channel_id=1, source_target_pairs={{0,1},{1,0},{2,3},{3,2},{4,5},{5,4},{6,7},{7,6},{8,9},{9,8},{10,11... | collective-permute-start | bytes 1572872 | tf_op jit(solution)/shard_map/ppermute | solution.py:625
  185.1 25.8 %collective-permute-start.24 = (bf16[256,1024]{1,0:T(8,128)(2,1)}, bf16[256,1024]{1,0:T(8,128)(2,1)S(1)}, u32[]{:S(2)}, u32[]{:S(2)}) collective-permute-start(bf16[256,1024]{1,0:T(8,128)(2,1)} %later.7), channel_id=1, source_target_pairs={{0,2},{1,3},{2,0},{3,1},{4,6},{5,7},{6,4},{7,5},{8,10},{9,11},{10,... | collective-permute-start | bytes 1572872 | tf_op jit(solution)/shard_map/ppermute | solution.py:625
  185.5 25.4 %collective-permute-start.25 = (bf16[256,1024]{1,0:T(8,128)(2,1)}, bf16[256,1024]{1,0:T(8,128)(2,1)S(1)}, u32[]{:S(2)}, u32[]{:S(2)}) collective-permute-start(bf16[256,1024]{1,0:T(8,128)(2,1)} %later.8), channel_id=1, source_target_pairs={{0,1},{1,0},{2,3},{3,2},{4,5},{5,4},{6,7},{7,6},{8,9},{9,8},{10,11... | collective-permute-start | bytes 1572872 | tf_op jit(solution)/shard_map/ppermute | solution.py:625
  186.9 24.0 %copy-start.3 = (bf16[256,1024]{1,0:T(8,128)(2,1)S(1)}, bf16[256,1024]{1,0:T(8,128)(2,1)}, u32[]{:S(2)}) copy-start(bf16[256,1024]{1,0:T(8,128)(2,1)} %get-tuple-element.85.earlier_ref.stay_a_ref) | copy-start | bytes 1572868
  186.9 24.0 %copy-start.4 = (bf16[256,1024]{1,0:T(8,128)(2,1)S(1)}, bf16[256,1024]{1,0:T(8,128)(2,1)}, u32[]{:S(2)}) copy-start(bf16[256,1024]{1,0:T(8,128)(2,1)} %get-tuple-element.87.stay_b_ref) | copy-start | bytes 1572868
  206.9 11.2 %collective-permute-start.27 = (bf16[256,1024]{1,0:T(8,128)(2,1)}, bf16[256,1024]{1,0:T(8,128)(2,1)S(1)}, u32[]{:S(2)}, u32[]{:S(2)}) collective-permute-start(bf16[256,1024]{1,0:T(8,128)(2,1)} %get-tuple-element.105), channel_id=1, source_target_pairs={{0,2},{1,3},{2,0},{3,1},{4,6},{5,7},{6,4},{7,5},{8,10},{9,11},{10,... | collective-permute-start | bytes 1572872 | tf_op jit(solution)/shard_map/ppermute | solution.py:625
  207.7 11.0 %collective-permute-start.28 = (bf16[256,1024]{1,0:T(8,128)(2,1)}, bf16[256,1024]{1,0:T(8,128)(2,1)S(1)}, u32[]{:S(2)}, u32[]{:S(2)}) collective-permute-start(bf16[256,1024]{1,0:T(8,128)(2,1)} %get-tuple-element.107), channel_id=1, source_target_pairs={{0,1},{1,0},{2,3},{3,2},{4,5},{5,4},{6,7},{7,6},{8,9},{9,8},{10,11... | collective-permute-start | bytes 1572872 | tf_op jit(solution)/shard_map/ppermute | solution.py:625
  220.8 9.8 %copy-start.18 = (bf16[128,3456]{1,0:T(8,128)(2,1)S(1)}, bf16[128,3456]{1,0:T(8,128)(2,1)}, u32[]{:S(2)}) copy-start(bf16[128,3456]{1,0:T(8,128)(2,1)} %reduce-scatter.3.cloned.1.call-done.refs_1_) | copy-start | bytes 2654212
  222.4 6.6 %copy-start.7 = (f32[128,1024]{1,0:T(8,128)}, f32[128,1024]{1,0:T(8,128)S(1)}, u32[]{:S(2)}) copy-start(f32[128,1024]{1,0:T(8,128)S(1)} %get-tuple-element.110.refs_4_) | copy-start | bytes 1572868
  223.6 1.2 collective-permute-start.32
  224.9 4.1 %collective-permute-start.33 = (f32[2176]{0:T(1024)S(1)}, f32[2176]{0:T(1024)S(1)}, u32[]{:S(2)}, u32[]{:S(2)}) collective-permute-start(f32[2176]{0:T(1024)S(1)} %fusion.10), channel_id=1, source_target_pairs={{0,8},{4,12},{8,0},{12,4},{16,24},{20,28},{24,16},{28,20},{1,9},{5... | collective-permute-start | bytes 26120 | tf_op jit(solution)/shard_map/ppermute | solution.py:625
  224.9 19.2 %collective-permute-start.26 = (bf16[128,1024]{1,0:T(8,128)(2,1)S(1)}, bf16[128,1024]{1,0:T(8,128)(2,1)S(1)}, u32[]{:S(2)}, u32[]{:S(2)}) collective-permute-start(bf16[128,1024]{1,0:T(8,128)(2,1)S(1)} %copy-done.6), channel_id=1, source_target_pairs={{0,1},{1,0},{2,3},{3,2},{4,5},{5,4},{6,7},{7,6},{8,9},{9,8},{10,11... | collective-permute-start | bytes 786440 | tf_op jit(solution)/shard_map/ppermute | solution.py:625
  225.2 18.9 %collective-permute-start.30 = (bf16[128,1024]{1,0:T(8,128)(2,1)S(1)}, bf16[128,1024]{1,0:T(8,128)(2,1)S(1)}, u32[]{:S(2)}, u32[]{:S(2)}) collective-permute-start(bf16[128,1024]{1,0:T(8,128)(2,1)S(1)} %get-tuple-element.113), channel_id=1, source_target_pairs={{0,2},{1,3},{2,0},{3,1},{4,6},{5,7},{6,4},{7,5},{8,10},{9,11},{10,... | collective-permute-start | bytes 786440 | tf_op jit(solution)/shard_map/ppermute | solution.py:625
  226.4 17.7 %collective-permute-start.29 = (bf16[128,1024]{1,0:T(8,128)(2,1)}, bf16[128,1024]{1,0:T(8,128)(2,1)S(1)}, u32[]{:S(2)}, u32[]{:S(2)}) collective-permute-start(bf16[128,1024]{1,0:T(8,128)(2,1)} %get-tuple-element.111), channel_id=1, source_target_pairs={{0,1},{1,0},{2,3},{3,2},{4,5},{5,4},{6,7},{7,6},{8,9},{9,8},{10,11... | collective-permute-start | bytes 786440 | tf_op jit(solution)/shard_map/ppermute | solution.py:625
  228.1 16.0 %collective-permute-start.31 = (bf16[128,1024]{1,0:T(8,128)(2,1)S(1)}, bf16[128,1024]{1,0:T(8,128)(2,1)S(1)}, u32[]{:S(2)}, u32[]{:S(2)}) collective-permute-start(bf16[128,1024]{1,0:T(8,128)(2,1)S(1)} %get-tuple-element.115), channel_id=1, source_target_pairs={{0,2},{1,3},{2,0},{3,1},{4,6},{5,7},{6,4},{7,5},{8,10},{9,11},{10,... | collective-permute-start | bytes 786440 | tf_op jit(solution)/shard_map/ppermute | solution.py:625
  229.0 4.7 %collective-permute-start.34 = (f32[2176]{0:T(1024)S(1)}, f32[2176]{0:T(1024)S(1)}, u32[]{:S(2)}, u32[]{:S(2)}) collective-permute-start(f32[2176]{0:T(1024)S(1)} %add.143), channel_id=1, source_target_pairs={{0,16},{4,20},{8,24},{12,28},{16,0},{20,4},{24,8},{28,12},{1,17},{... | collective-permute-start | bytes 26120 | tf_op jit(solution)/shard_map/ppermute | solution.py:625
  233.8 5.5 %collective-permute-start.35 = (f32[2176]{0:T(1024)S(1)}, f32[2176]{0:T(1024)S(1)}, u32[]{:S(2)}, u32[]{:S(2)}) collective-permute-start(f32[2176]{0:T(1024)S(1)} %add.144), channel_id=1, source_target_pairs={{0,1},{1,0},{2,3},{3,2},{4,5},{5,4},{6,7},{7,6},{8,9},{9,8},{10,11... | collective-permute-start | bytes 26120 | tf_op jit(solution)/shard_map/ppermute | solution.py:625
  239.2 3.7 %collective-permute-start.36 = (f32[2176]{0:T(1024)S(1)}, f32[2176]{0:T(1024)S(1)}, u32[]{:S(2)}, u32[]{:S(2)}) collective-permute-start(f32[2176]{0:T(1024)S(1)} %add.145), channel_id=1, source_target_pairs={{0,2},{1,3},{2,0},{3,1},{4,6},{5,7},{6,4},{7,5},{8,10},{9,11},{10,... | collective-permute-start | bytes 26120 | tf_op jit(solution)/shard_map/ppermute | solution.py:625
  (25 other events, 34.2 us)
Sparse Core Ops, SparseCore 0:
  10.3 27.7 all-gather.2
  39.7 70.7 all-gather.4
  138.8 75.8 reduce-scatter.2
  216.8 32.4 reduce-scatter.4
